TPU v7x, 32 devices: a whole 2x2x4 slice. The times are simulated.
32 devices in a mesh: ctx: 16 (over z, y, x), head: 2 (over core).
Axes of the slice: x: 2, y: 2, z: 4, core: 2. Of those that a mesh axis runs over, the one named last changes fastest.
Arguments:
- queries: bfloat16 [2048, 1024], P('ctx', 'head'), may hold values from -6 to 6
- keys_values: bfloat16 [2, 2048, 1024], P(None, 'ctx', 'head'), may hold values from -6 to 6
- attn_cot: bfloat16 [2048, 1024], P('ctx', 'head'), may hold values from -768 to 768
- event_rows: bfloat16 [2048, 1024], P('ctx'), may hold values from -0.15625 to 0.15625
- adapter: bfloat16 [1024, 1024], P(None, 'head'), may hold values from -0.1875 to 0.1875
- qkv_weight: bfloat16 [3, 1024, 1024], P(None, None, 'head'), may hold values from -0.1875 to 0.1875
- starts: int32 [16], P('ctx'), may hold values from 0 to 1920, as said below
- owners: int32 [2048, 1], P('ctx'), may hold values from 0 to 15; in each aligned block of 128 rows (0 to 127, 128 to 255, ...) at most 16 rows name the same one
- slots: int32 [2048], P('ctx'), may hold values from 0 to 255
- table: float32 [4096, 1024], P('ctx', 'head'), may hold values from -0.625 to 0.625
- moment_m: float32 [4096, 1024], P('ctx', 'head'), may hold values from -0.625 to 0.625
- moment_v: float32 [4096, 1024], P('ctx', 'head'), may hold values from 0.01 to 1
Outputs:
- adapter_grad: float32 [1024, 1024], P('ctx', 'head')
- new_table: float32 [4096, 1024], P('ctx', 'head')
- new_m: float32 [4096, 1024], P('ctx', 'head')
- new_v: float32 [4096, 1024], P('ctx', 'head')
Inputs may be any that keep to these rules, and one draw needn't show every extreme that they name: starts[b] lies between 0 and b * 128; the last block's start is its own first event. `owners`: among the 128 events of one index of ctx at most 16 name the same owner, and in some such block one owner is named exactly 16 times.
All inputs are finite; a program needn't handle non-finite values.
Results may differ from a plain program's by a relative error of at most 0.014.
Values may be sent and summed in bfloat16 or wider, within the bound.
No kernel may reach another device: no remote copies, remote signals or barrier semaphores. Data moves between devices by JAX's collectives and lax.ppermute only.
A program may use at most 64 MiB of HBM per device.

v0:
```python
import math

import jax
import jax.numpy as jnp
from jax import lax
from jax.sharding import PartitionSpec as P

HD = 128
QBLK = 128


beta_first = 0.9
beta_second = 0.999
learn_rate = 0.01
epsilon = 1e-08
first_fix = 1.0 - beta_first**10.0
second_fix = 1.0 - beta_second**10.0


def adam_rows(summed, touched, table, moment_m, moment_v):
    fresh_m = beta_first * moment_m + (1.0 - beta_first) * summed
    fresh_v = beta_second * moment_v + (1.0 - beta_second) * summed * summed
    update = learn_rate * (fresh_m / first_fix) / (jnp.sqrt(fresh_v / second_fix) + epsilon)
    keep = touched[:, None]
    return (
        jnp.where(keep, table - update, table),
        jnp.where(keep, fresh_m, moment_m),
        jnp.where(keep, fresh_v, moment_v),
    )


def pair_scores(query_part, key_part, query_places, query_lower, key_places):
    scale = 1.0 / math.sqrt(HD)
    scores = (
        jnp.einsum("ihd,jhd->hij", query_part, key_part, preferred_element_type=jnp.float32) * scale
    )
    seen = (key_places[None, :] <= query_places[:, None]) & (
        key_places[None, :] >= query_lower[:, None]
    )
    squash = jax.nn.sigmoid(scores)
    return (scores, squash, seen[None])


def score_grads(scores, squash, seen, cotangent_piece, value_part, seq_len):
    dprod = jnp.einsum(
        "ihd,jhd->hij", cotangent_piece, value_part, preferred_element_type=jnp.float32
    )
    return jnp.where(seen, dprod * squash * (1.0 + scores * (1.0 - squash)) / seq_len, 0.0).astype(
        jnp.bfloat16
    )


def score_weights(scores, squash, seen, seq_len):
    return jnp.where(seen, scores * squash / seq_len, 0.0).astype(jnp.bfloat16)


def over_blocks(total, fn, carry):
    sub = math.gcd(total, 1024)
    return lax.fori_loop(
        0, total // sub, lambda index, inner_loop: fn(inner_loop, index * sub), carry
    )


def per_device(
    queries,
    keys_values,
    attn_cot,
    event_rows,
    adapter,
    qkv_weight,
    starts,
    owners,
    slots,
    table,
    moment_m,
    moment_v,
):
    rows_here = queries.shape[0]
    feature_cols = queries.shape[1]
    heads_here = feature_cols // HD
    n_ctx = lax.axis_size("ctx")
    seq_len = rows_here * n_ctx
    scale = 1.0 / math.sqrt(HD)
    myself = lax.axis_index("ctx")
    local_first = myself * rows_here
    local_places = local_first + jnp.arange(rows_here, dtype=jnp.int32)
    lower = jnp.repeat(starts, QBLK, total_repeat_length=rows_here)
    least_lower = jnp.min(lower)
    query_heads = queries.reshape(rows_here, heads_here, HD)
    cot_heads = attn_cot.reshape(rows_here, heads_here, HD)
    key_heads = keys_values[0].reshape(rows_here, heads_here, HD)
    value_heads = keys_values[1].reshape(rows_here, heads_here, HD)
    zeros = jnp.zeros((rows_here, heads_here, HD), jnp.float32)
    piece = lax.all_gather(keys_values, "ctx", axis=1, tiled=True)

    def key_one_block(inner_loop, offset):
        sub = math.gcd(piece.shape[1], 1024)
        key_first = offset
        live = (key_first <= local_first + rows_here - 1) & (key_first + sub - 1 >= least_lower)

        def key_working(values):
            part = lax.dynamic_slice_in_dim(piece, offset, sub, 1)
            key_part = part[0].reshape(sub, heads_here, HD)
            value_part = part[1].reshape(sub, heads_here, HD)
            key_places = key_first + jnp.arange(sub, dtype=jnp.int32)
            scores, squash, seen = pair_scores(
                query_heads, key_part, local_places, lower, key_places
            )
            dscore = score_grads(scores, squash, seen, cot_heads, value_part, seq_len)
            return values + jnp.einsum(
                "hij,jhd->ihd", dscore, key_part, preferred_element_type=jnp.float32
            )

        return lax.cond(live, key_working, lambda values: values, inner_loop)

    query_grad = over_blocks(piece.shape[1], key_one_block, zeros)
    query_piece = (
        lax.all_gather(queries, "ctx", axis=0, tiled=True),
        lax.all_gather(attn_cot, "ctx", axis=0, tiled=True),
        lax.all_gather(lower, "ctx", axis=0, tiled=True),
    )

    def query_one_block(inner_loop, offset):
        sub = math.gcd(query_piece[0].shape[0], 1024)
        query_first = offset
        query_lower = lax.dynamic_slice_in_dim(query_piece[2], offset, sub, 0)
        live = (local_first <= query_first + sub - 1) & (
            local_first + rows_here - 1 >= jnp.min(query_lower)
        )

        def query_working(values):
            query_part = lax.dynamic_slice_in_dim(query_piece[0], offset, sub, 0).reshape(
                sub, heads_here, HD
            )
            cotangent_piece = lax.dynamic_slice_in_dim(query_piece[1], offset, sub, 0).reshape(
                sub, heads_here, HD
            )
            query_places = query_first + jnp.arange(sub, dtype=jnp.int32)
            scores, squash, seen = pair_scores(
                query_part, key_heads, query_places, query_lower, local_places
            )
            weights = score_weights(scores, squash, seen, seq_len)
            dscore = score_grads(scores, squash, seen, cotangent_piece, value_heads, seq_len)
            key_add = jnp.einsum(
                "hij,ihd->jhd", dscore, query_part, preferred_element_type=jnp.float32
            )
            value_add = jnp.einsum(
                "hij,ihd->jhd", weights, cotangent_piece, preferred_element_type=jnp.float32
            )
            return (values[0] + key_add, values[1] + value_add)

        return lax.cond(live, query_working, lambda values: values, inner_loop)

    key_grad, value_grad = over_blocks(query_piece[0].shape[0], query_one_block, (zeros, zeros))
    head_grads = (
        jnp.stack([query_grad * scale, key_grad * scale, value_grad])
        .astype(jnp.bfloat16)
        .reshape(3, rows_here, feature_cols)
    )
    partial_grad = jnp.einsum(
        "mtc,mdc->td", head_grads, qkv_weight, preferred_element_type=jnp.float32
    )
    head_cols = adapter.shape[1]
    first_col = lax.axis_index("head") * head_cols
    layer_grad = lax.psum(partial_grad.astype(jnp.bfloat16), "head").astype(jnp.float32)
    layer_grad_b = layer_grad.astype(jnp.bfloat16)
    own_grad = lax.dynamic_slice_in_dim(layer_grad, first_col, head_cols, 1)
    row_grads = own_grad + jnp.dot(layer_grad_b, adapter, preferred_element_type=jnp.float32)
    own_rows = lax.dynamic_slice_in_dim(event_rows, first_col, head_cols, 1)
    adapter_grad = lax.psum_scatter(
        lax.dot_general(
            layer_grad_b, own_rows, (((0,), (0,)), ((), ())), preferred_element_type=jnp.float32
        ),
        "ctx",
        scatter_dimension=0,
        tiled=True,
    )
    capacity = max(2, 2 * rows_here // n_ctx)
    target = owners[:, 0]
    onehot = (target[:, None] == jnp.arange(n_ctx, dtype=jnp.int32)[None, :]).astype(jnp.int32)
    prior_blocks = jnp.cumsum(onehot, axis=0) - onehot
    ranking = jnp.sum(prior_blocks * onehot, axis=1)
    cell_index = target * capacity + ranking
    placing = cell_index[:, None] == jnp.arange(n_ctx * capacity, dtype=jnp.int32)[None, :]
    send_rows = lax.dot_general(
        placing.astype(jnp.float32),
        row_grads,
        (((0,), (0,)), ((), ())),
        precision=lax.Precision.HIGHEST,
    ).reshape(n_ctx, capacity, head_cols)
    send_slots = (jnp.sum(jnp.where(placing, slots[:, None] + 1, 0), axis=0) - 1).reshape(
        n_ctx, capacity
    )
    got_rows, got_slots = (
        lax.all_to_all(
            send_rows.astype(jnp.bfloat16), "ctx", split_axis=0, concat_axis=0, tiled=True
        ).astype(send_rows.dtype),
        lax.all_to_all(send_slots, "ctx", split_axis=0, concat_axis=0, tiled=True),
    )
    table_rows = table.shape[0]
    landing = got_slots.reshape(-1)[None, :] == jnp.arange(table_rows, dtype=jnp.int32)[:, None]
    summed = jnp.dot(
        landing.astype(jnp.float32),
        got_rows.reshape(n_ctx * capacity, head_cols),
        precision=lax.Precision.HIGHEST,
    )
    touched = jnp.sum(landing.astype(jnp.int32), axis=1) > 0
    new_table, new_m, new_v = adam_rows(summed, touched, table, moment_m, moment_v)
    return (adapter_grad, new_table, new_m, new_v)


def solution(mesh):
    placed = (
        P("ctx", "head"),
        P(None, "ctx", "head"),
        P("ctx", "head"),
        P("ctx", None),
        P(None, "head"),
        P(None, None, "head"),
        P("ctx"),
        P("ctx", None),
        P("ctx"),
        P("ctx", "head"),
        P("ctx", "head"),
        P("ctx", "head"),
    )
    return jax.shard_map(
        per_device,
        mesh=mesh,
        in_specs=placed,
        out_specs=(P("ctx", "head"), P("ctx", "head"), P("ctx", "head"), P("ctx", "head")),
        check_vma=False,
    )
```

profile of v0, /device:TPU:0, one launch (start us, length us, event | category | flops | bytes accessed | tf_op | source)
XLA Modules:
  0.0 367.3 jit_solution(7316956309867307322)
XLA Ops:
  7.2 0.0 all-gather.7.cloned.1.call-start
  7.2 1.8 copy.75
  9.0 0.0 all-gather.7.cloned.1.call-update
  9.1 0.0 all-gather.9.cloned.1.call-start
  9.1 1.7 copy.74
  10.8 0.0 all-gather.5.cloned.1.call-start
  10.9 1.8 copy.73
  12.7 0.0 all-reduce.2.cloned.1.call-start
  12.7 1.0 fusion.63
  13.7 0.8 copy.83
  14.5 0.1 copy.84
  15.3 1.0 copy.76
  16.3 0.8 copy.77
  17.1 42.5 %all-gather = s32[16,1,128]{2,1,0:T(1,128)S(1)} all-gather(s32[1,1,128]{2,1,0:T(1,128)S(1)} %broadcast.187), channel_id=1, replica_groups=mesh['ctx'=16,'head'=2] {'ctx'}, dimensions={0}, use_global_device_ids=true | all-gather | bytes 8704 | tf_op jit(solution)/shard_map/all_gather | solution.py:120
  59.6 17.7 %all-gather.7.cloned.1.call-done = bf16[2048,512]{0,1:T(8,128)(2,1)} async-done(((bf16[128,512]{0,1:T(8,128)(2,1)}), bf16[2048,512]{0,1:T(8,128)(2,1)}) %all-gather.7.cloned.1.call-update) | async-done | bytes 2097168 | tf_op jit(solution)/shard_map/all_gather | solution.py:118
  77.3 64.8 %all-gather.9.cloned.1.call-done = bf16[2048,512]{0,1:T(8,128)(2,1)} async-done(((bf16[128,512]{0,1:T(8,128)(2,1)}), bf16[2048,512]{0,1:T(8,128)(2,1)}) %all-gather.9.cloned.1.call-update) | async-done | bytes 2097168 | tf_op jit(solution)/shard_map/all_gather | solution.py:119
  142.0 0.7 broadcast_in_dim.79.clone
  142.8 0.7 broadcast_in_dim.79.clone.1
  143.5 16.7 %while.48 = (s32[]{:T(128)}, f32[128,4,128]{0,2,1:T(8,128)}, f32[128,4,128]{0,2,1:T(8,128)}, s32[]{:T(128)}, s32[2048]{0:T(1024)S(1)}, /*index=5*/s32[]{:T(128)}...) while((s32[]{:T(128)}, f32[128,4,128]{0,2,1:T(8,128)}, ...), condition=%wide.region_8.9_spmd.clone.clone, body=%wide.region_4.8_spmd.clone.clone.sunk | while | flops 547883136 | bytes 20601260 | solution.py:59
  143.5 0.6 fusion.84
  144.8 14.1 %conditional.9 = ((f32[128,4,128]{0,2,1:T(8,128)}, f32[128,4,128]{0,2,1:T(8,128)})) conditional(s32[]{:T(128)} %convert_element_type.97, (f32[128,4,128]{0,2,1:T(8,128)}, f32[128,4,128]{0,2,1:T(8,128)}) %tuple.163, (s32[]{:T(128)}, bf16[2048,512]{0,1:T(8,128)(2,1)}, s32[]{:T(128)}, s32[1024]{0:T(1024)S(1)}, bf16[2048,512]{0,1:T(8,128)(2,1)}, ...), branch_computations={%region_6.6_spmd, %region_7.7_spmd} | conditional | flops 547882112 | bytes 20592226 | solution.py:152
  144.8 2.7 constant_dynamic-slice_fusion.2
  147.5 1.0 copy-done.1
  148.5 1.9 fusion.65
  150.4 0.3 compare_and_fusion.1
  150.8 4.6 %fusion.29 = f32[128,4,128]{0,2,1:T(8,128)} fusion(f32[128,4,128]{0,2,1:T(8,128)} %get-tuple-element.762, bf16[1024,4,128]{0,2,1:T(8,128)(2,1)} %bitcast.94, f32[4,1024,128]{2,1,0:T(8,128)} %fusion.65, bf16[1024,4,128]{0,2,1:T(8,128)(2,1)} %bitcast.97, bf16[128,4,128]{2,0,1:T(8,128)(2,1)} %get-tuple-element.768, pred[1024,128]{1,0:T(8,128)(4,1)S(1)} %compare_and_fusion.1), kind=kOutput, calls=%fused_computation.39 | convolution fusion | flops 274792448 | bytes 4980736 | tf_op jit(solution)/shard_map/while/body/eval_jaxpr/cond/branch_1_fun/hij,ihd->jhd/dot_general | solution.py:144
  155.4 3.5 fusion.28
  158.9 0.6 fusion.84
  160.2 1.0 multiply_convert_fusion
  161.2 0.8 copy.93
  161.9 1.0 convert.14
  162.9 0.8 copy.94
  163.7 69.1 %all-gather.5.cloned.1.call-done = bf16[2,2048,512]{1,2,0:T(8,128)(2,1)} async-done(((bf16[2,128,512]{1,2,0:T(8,128)(2,1)}), bf16[2,2048,512]{1,2,0:T(8,128)(2,1)}) %all-gather.5.cloned.1.call-update) | async-done | bytes 4194320 | tf_op jit(solution)/shard_map/all_gather | solution.py:94
  232.7 0.7 broadcast_in_dim.79.clone.2
  233.5 11.6 %while.47 = (s32[]{:T(128)}, f32[128,4,128]{0,2,1:T(8,128)}, s32[]{:T(128)}, s32[]{:T(128)}, bf16[2,2048,512]{1,2,0:T(8,128)(2,1)}, /*index=5*/bf16[128,4,128]{2...) while((s32[]{:T(128)}, f32[128,4,128]{0,2,1:T(8,128)}, ...), condition=%wide.region_3.4_spmd.clone.clone, body=%wide.region_0.3_spmd.clone.clone.sunk | while | flops 409275520 | bytes 12071241 | solution.py:59
  234.1 10.2 %conditional.8 = (f32[128,4,128]{0,2,1:T(8,128)}) conditional(s32[]{:T(128)} %convert_element_type.96, f32[128,4,128]{0,2,1:T(8,128)} %get-tuple-element.1197, (s32[]{:T(128)}, bf16[2,2048,512]{1,2,0:T(8,128)(2,1)}, s32[]{:T(128)}, s32[]{:T(128)}, bf16[128,4,128]{2,0,1:T(8,128)(2,1)S(1)}, /*index=5*/bf16[128,4,128]{2,0,1:T(8,128)(2,1)}, ...), branch_computations={%region_1.1_spmd, %region_2.2_spmd} | conditional | flops 409275520 | bytes 12070506 | solution.py:114
  234.1 2.7 constant_dynamic-slice_fusion.1
  236.9 1.9 fusion.64
  238.8 0.7 broadcast_compare_fusion
  239.4 0.3 compare_and_fusion
  239.8 4.6 %fusion.16 = f32[128,4,128]{0,2,1:T(8,128)} fusion(f32[128,4,128]{0,2,1:T(8,128)} %get-tuple-element.745, bf16[1024,4,128]{0,2,1:T(8,128)(2,1)} %bitcast.96, f32[4,1024,128]{2,1,0:T(8,128)} %fusion.64, bf16[128,4,128]{2,0,1:T(8,128)(2,1)S(1)} %copy-done.4, pred[128,1024]{0,1:T(8,128)(4,1)S(1)} %compare_and_fusion), kind=kOutput, calls=%fused_computation.16 | convolution fusion | flops 274792448 | bytes 3932160 | tf_op jit(solution)/shard_map/while/body/eval_jaxpr/cond/branch_1_fun/hij,jhd->ihd/dot_general | solution.py:110
  245.0 1.0 multiply_convert_fusion.1
  246.0 0.1 copy.92
  246.1 2.8 fusion.44
  249.0 0.0 reduce-scatter.2.cloned.1.call-start
  249.1 26.7 %all-reduce.2.cloned.1.call-done = bf16[128,1024]{1,0:T(8,128)(2,1)} async-done(((bf16[128,1024]{1,0:T(8,128)(2,1)}), bf16[128,1024]{1,0:T(8,128)(2,1)}) %all-reduce.2.cloned.1.call-update) | async-done | bytes 262160 | tf_op jit(solution)/shard_map/psum | solution.py:165
  275.8 2.8 fusion.55
  278.6 0.1 fusion.58
  278.7 0.2 reduce_window_sum.22
  278.9 0.2 select_reduce_fusion.1
  279.1 0.1 select_reduce_fusion
  279.2 0.7 sub.41
  279.9 6.8 %all-to-all-start = ((s32[16,1,16]{2,1,0:T(1,128)}), s32[16,1,16]{2,1,0:T(1,128)S(1)}, u32[]{:S(2)}, u32[]{:S(2)}) async-start(s32[16,1,16]{2,1,0:T(1,128)} %sub.41), calls=%async_computation.1 | async-start | bytes 16384 | tf_op jit(solution)/shard_map/all_to_all | solution.py:198
  286.7 1.5 convolution_add_fusion
  288.3 1.2 convolution_convert_fusion
  289.5 4.4 %all-to-all-done = s32[16,1,16]{2,1,0:T(1,128)S(1)} async-done(((s32[16,1,16]{2,1,0:T(1,128)}), s32[16,1,16]{2,1,0:T(1,128)S(1)}, u32[]{:S(2)}, u32[]{:S(2)}) %all-to-all-start) | async-done | bytes 1056 | tf_op jit(solution)/shard_map/all_to_all | solution.py:198
  293.9 3.5 all-to-all-start.1
  297.4 0.5 broadcast.231
  298.0 0.7 reduce.7
  298.6 0.1 eq.53
  298.7 0.1 convert_reduce_fusion
  298.8 10.4 %all-to-all-done.1 = bf16[16,16,512]{2,1,0:T(8,128)(2,1)S(1)} async-done(((bf16[16,16,512]{2,1,0:T(8,128)(2,1)}), bf16[16,16,512]{2,1,0:T(8,128)(2,1)S(1)}, u32[]{:S(2)}, u32[]{:S(2)}) %all-to-all-start.1) | async-done | bytes 262176 | tf_op jit(solution)/shard_map/all_to_all | solution.py:195
  309.3 3.1 fusion.47
  312.3 48.4 %reduce-scatter.2.cloned.1.call-done = f32[64,512]{1,0:T(8,128)} async-done(((f32[1024,512]{1,0:T(8,128)}), f32[64,512]{1,0:T(8,128)}) %reduce-scatter.2.cloned.1.call-update) | async-done | bytes 131088 | tf_op jit(solution)/shard_map/reduce_scatter | solution.py:170
  (32 shorter events, 0.2 us)
Async XLA Ops:
  7.2 239.0 %copy-start = (bf16[3,1024,512]{2,1,0:T(8,128)(2,1)S(1)}, bf16[3,1024,512]{2,1,0:T(8,128)(2,1)}, u32[]{:S(2)}) copy-start(bf16[3,1024,512]{2,1,0:T(8,128)(2,1)} %param.29) | copy-start | bytes 9437188
  7.2 70.1 %all-gather.7.cloned.1.call-start = ((), (), s32[]{:S(2)}) async-start(), calls=%async_computation.4 | async-start | bytes 2228224 | tf_op jit(solution)/shard_map/all_gather | solution.py:118
  9.0 7.3 %copy-start.2 = (bf16[128,512]{0,1:T(8,128)(2,1)S(1)}, bf16[128,512]{0,1:T(8,128)(2,1)}, u32[]{:S(2)}) copy-start(bf16[128,512]{0,1:T(8,128)(2,1)} %copy.75) | copy-start | bytes 393220
  9.1 133.0 %all-gather.9.cloned.1.call-start = ((), (), s32[]{:S(2)}) async-start(), calls=%async_computation.5 | async-start | bytes 2228224 | tf_op jit(solution)/shard_map/all_gather | solution.py:119
  10.8 221.9 %all-gather.5.cloned.1.call-start = ((), (), s32[]{:S(2)}) async-start(), calls=%async_computation.3 | async-start | bytes 4456448 | tf_op jit(solution)/shard_map/all_gather | solution.py:94
  12.7 263.1 %all-reduce.2.cloned.1.call-start = ((), (), s32[]{:S(2)}) async-start(), calls=%async_computation.6 | async-start | bytes 524288 | tf_op jit(solution)/shard_map/psum | solution.py:165
  147.5 1.0 copy-start.1
  236.9 2.9 copy-start.4
  249.0 111.8 %reduce-scatter.2.cloned.1.call-start = ((), (), s32[]{:S(2)}) async-start(), calls=%async_computation.7 | async-start | bytes 2228224 | tf_op jit(solution)/shard_map/reduce_scatter | solution.py:170
  249.0 29.6 %copy-start.5 = (s32[128,1]{0,1:T(1,128)S(1)}, s32[128,1]{0,1:T(1,128)}, u32[]{:S(2)}) copy-start(s32[128,1]{0,1:T(1,128)} %param.31) | copy-start | bytes 1540
  249.0 30.0 %copy-start.6 = (s32[128]{0:T(128)S(1)}, s32[128]{0:T(128)}, u32[]{:S(2)}) copy-start(s32[128]{0:T(128)} %param.32) | copy-start | bytes 1540
  275.8 10.9 %copy-start.3 = (bf16[128,1024]{1,0:T(8,128)(2,1)S(1)}, bf16[128,1024]{1,0:T(8,128)(2,1)}, u32[]{:S(2)}) copy-start(bf16[128,1024]{1,0:T(8,128)(2,1)} %all-reduce.2.cloned.1.call-done) | copy-start | bytes 786436
  279.9 14.0 %all-to-all-start = ((s32[16,1,16]{2,1,0:T(1,128)}), s32[16,1,16]{2,1,0:T(1,128)S(1)}, u32[]{:S(2)}, u32[]{:S(2)}) async-start(s32[16,1,16]{2,1,0:T(1,128)} %sub.41), calls=%async_computation.1 | async-start | bytes 16384 | tf_op jit(solution)/shard_map/all_to_all | solution.py:198
  293.9 15.3 %all-to-all-start.1 = ((bf16[16,16,512]{2,1,0:T(8,128)(2,1)}), bf16[16,16,512]{2,1,0:T(8,128)(2,1)S(1)}, u32[]{:S(2)}, u32[]{:S(2)}) async-start(bf16[16,16,512]{2,1,0:T(8,128)(2,1)} %bitcast.22), calls=%async_computation.2 | async-start | bytes 524288 | tf_op jit(solution)/shard_map/all_to_all | solution.py:195
Sparse Core Ops, SparseCore 0:
  11.3 65.9 all-gather.6
  80.6 61.4 all-gather.8
  145.3 87.3 all-gather.4
  249.1 26.6 all-reduce.1
  278.7 81.9 reduce-scatter.1
where the time goes:
time: 368 us; the launch traced here: 367 us
  waiting for transfers between devices  242 us (66%)
  blocking collectives  42.5 us (12%)
  matrix products  27.9 us (8%)
  local copies, waits for them, and re-layouts  20.5 us (6%)
  between operations  14.6 us (4%)
  starting transfers between devices  10.5 us (3%)
  other arithmetic  6.89 us (2%)
    all_gather x1, waiting for transfers between devices, per_device(): piece = lax.all_gather(keys_values, 'ctx', axis=1, tiled=True)  69.1 us
    all_gather x1, waiting for transfers between devices, per_device(): lax.all_gather(attn_cot, 'ctx', axis=0, tiled=True)  64.8 us
    reduce_scatter x1, waiting for transfers between devices, per_device(): lax.psum_scatter(lax.dot_general(layer_grad_b, own_rows, (((0,), (0,)), (...  48.4 us
    all_gather x1, blocking collectives, per_device(): lax.all_gather(lower, 'ctx', axis=0, tiled=True)  42.5 us
    psum x1, waiting for transfers between devices, per_device(): lax.psum(partial_grad.astype(jnp.bfloat16), 'head').astype(jnp.float32)  26.7 us
    all_gather x1, waiting for transfers between devices, per_device(): lax.all_gather(queries, 'ctx', axis=0, tiled=True)  17.7 us
    all_to_all x1, waiting for transfers between devices, per_device(): lax.all_to_all(send_rows.astype(jnp.bfloat16), 'ctx', split_axis=0, conca...  10.4 us
    unnamed x18, local copies, waits for them, and re-layouts  8 us
  transfers between devices with their start and end apart: 7, of which 7 were waited for; matrix products, arithmetic and copies ran while one was open for 9% of the time, Pallas kernels for 0%

commit v1 on v0

--- a/solution.py
+++ b/solution.py
@@ -1,8 +1,11 @@
+import functools
 import math
 
 import jax
 import jax.numpy as jnp
 from jax import lax
+from jax.experimental import pallas as pl
+from jax.experimental.pallas import tpu as pltpu
 from jax.sharding import PartitionSpec as P
 
 HD = 128
@@ -61,7 +64,7 @@
     )
 
 
-def per_device(
+def plain_device(
     queries,
     keys_values,
     attn_cot,
@@ -209,6 +212,404 @@
     return (adapter_grad, new_table, new_m, new_v)
 
 
+BLOCK = 128
+PAIR = 2 * BLOCK
+META = 16
+PART = PAIR + META
+SPOTS = (0, 1, 4, 5)
+GROUPS = [[zh * 8 + y * 2 + s for s in SPOTS] for zh in range(2) for y in range(2)]
+ACROSS_Y = [(i, i ^ 2) for i in range(16)]
+FAR_OUT = [(i * 2, (i + 8) * 2) for i in range(8)] + [((i + 8) * 2 + 1, i * 2 + 1) for i in range(8)]
+FAR_BACK = [(b, a) for a, b in FAR_OUT]
+SWAP = [(0, 1), (1, 0)]
+F32 = jnp.float32
+BF16 = jnp.bfloat16
+VMEM = pl.BlockSpec(memory_space=pltpu.VMEM)
+SMEM = pl.BlockSpec(memory_space=pltpu.SMEM)
+
+
+def dot(a, b, axis_a, axis_b):
+    return lax.dot_general(a, b, (((axis_a,), (axis_b,)), ((), ())), preferred_element_type=F32)
+
+
+def kernel_call(body, out_shape, operands, name, flops=0, in_bytes=0):
+    specs = [SMEM if o.dtype == jnp.int32 and o.ndim == 1 else VMEM for o in operands]
+    return pl.pallas_call(
+        body,
+        out_shape=out_shape,
+        in_specs=specs,
+        out_specs=jax.tree.map(lambda _: VMEM, out_shape),
+        compiler_params=pltpu.CompilerParams(vmem_limit_bytes=24 * 1024 * 1024),
+        cost_estimate=pl.CostEstimate(flops=flops, bytes_accessed=in_bytes, transcendentals=0),
+        name=name,
+    )(*operands)
+
+
+def deal_body(info, starts, queries, keys_values, cot, out):
+    core = info[0]
+    start = starts[0]
+    row = lax.broadcasted_iota(jnp.int32, (META, BLOCK), 0)
+    meta = jnp.where(row == 0, start // BLOCK, jnp.where(row == 1, start % BLOCK, 0)).astype(F32).astype(BF16)
+
+    def fill(first, second):
+        for head in range(4):
+            cols = slice(head * BLOCK, (head + 1) * BLOCK)
+            for place, (one, two) in enumerate((first, second)):
+                base = place * PART
+                out[head, base : base + BLOCK, :] = one(cols)
+                out[head, base + BLOCK : base + PAIR, :] = two(cols)
+                out[head, base + PAIR : base + PART, :] = meta
+
+    asks = (lambda c: queries[:, c], lambda c: cot[:, c])
+    gives = (lambda c: keys_values[0, :, c], lambda c: keys_values[1, :, c])
+
+    @pl.when(core == 0)
+    def _():
+        fill(asks, gives)
+
+    @pl.when(core == 1)
+    def _():
+        fill(gives, asks)
+
+
+def attend_body(scale, seq_len, info, mine, near_in, far_in, keep, near_out, far_out, far_1, far_2, sum_1, sum_2):
+    core, zh, y = info[0], info[1], info[2]
+    role_q = core == 0
+    wide = 4 * BLOCK
+    sign = jnp.where(role_q, 1, -1)
+
+    def lower_of(ref, spot, base):
+        meta = ref[spot, base + PAIR : base + PART, :].astype(F32)
+        return (meta[0:1] * BLOCK + meta[1:2]).astype(jnp.int32)
+
+    def lanes_of(group_zh):
+        lane = lax.broadcasted_iota(jnp.int32, (1, BLOCK), 1)
+        return jnp.concatenate([lane + (group_zh * 8 + y * 2 + s) * BLOCK for s in SPOTS], axis=1)
+
+    for spot in range(4):
+        rows = slice(spot * BLOCK, (spot + 1) * BLOCK)
+        far_1[0, rows, :] = mine[spot, PART : PART + BLOCK, :]
+        far_2[0, rows, :] = mine[spot, PART + BLOCK : PART + PAIR, :]
+        far_1[1, rows, :] = far_in[spot, :BLOCK, :]
+        far_2[1, rows, :] = far_in[spot, BLOCK:PAIR, :]
+    sum_1[...] = jnp.zeros_like(sum_1)
+    sum_2[...] = jnp.zeros_like(sum_2)
+    places = (lanes_of(zh), lanes_of(1 - zh))
+    lowers = (
+        jnp.concatenate([lower_of(mine, s, PART) for s in range(4)], axis=1),
+        jnp.concatenate([lower_of(far_in, s, 0) for s in range(4)], axis=1),
+    )
+    row_in = lax.broadcasted_iota(jnp.int32, (BLOCK, wide), 0)
+    grad_scale = scale * 0.5 / seq_len
+
+    def piece(near_1, near_2, near_place, near_lower, side):
+        base_1, base_2 = far_1[side], far_2[side]
+        half = dot(near_1, base_1, 1, 1) * (0.5 * scale)
+        dprod = dot(near_2, base_2, 1, 1)
+        seen = []
+        for at in range(2):
+            low = jnp.where(role_q, jnp.concatenate([near_lower[at]] * 4, axis=1), lowers[side])
+            row = row_in + near_place[at]
+            causal = sign * row - sign * places[side]
+            after = jnp.where(role_q, 0, 1) * row + (jnp.where(role_q, 1, 0) * places[side] - low)
+            seen.append(jnp.minimum(causal, after) >= 0)
+        seen = jnp.concatenate(seen, axis=0)
+        twice = 1.0 + jnp.tanh(half)
+        weight = half * twice
+        dscore = dprod * (twice * (1.0 + (half + half - weight)))
+        weight = jnp.where(seen, weight, 0.0).astype(BF16)
+        dscore = jnp.where(seen, dscore, 0.0).astype(BF16)
+        sum_1[side] = sum_1[side] + dot(dscore, near_1, 0, 0)
+        return dot(dscore, base_1, 1, 0), weight
+
+    def work(near_ref, neighbour, half_at):
+        spots = (2 * half_at, 2 * half_at + 1)
+        near_1 = jnp.concatenate([near_ref[s, :BLOCK, :] for s in spots], axis=0)
+        near_2 = jnp.concatenate([near_ref[s, BLOCK:PAIR, :] for s in spots], axis=0)
+        near_y = 1 - y if neighbour else y
+        near_place = [(zh * 8 + near_y * 2 + SPOTS[s]) * BLOCK for s in spots]
+        near_lower = [lower_of(near_ref, s, 0) for s in spots]
+
+        def put(out, slot, value, start=False):
+            for at, s in enumerate(spots):
+                part = value[at * BLOCK : (at + 1) * BLOCK]
+                if start:
+                    out[s, slot] = part.astype(out.dtype)
+                else:
+                    out[s, slot] = (out[s, slot].astype(F32) + part).astype(out.dtype)
+
+        def side_work(side):
+            first, weight = piece(near_1, near_2, near_place, near_lower, side)
+            return first * grad_scale, weight
+
+        def second(weight, side):
+            return dot(weight, far_2[side], 1, 0) * (1.0 / seq_len)
+
+        def store(first, others):
+            if neighbour:
+                put(near_out, 0, first, True)
+            else:
+                put(keep, 0, first, True)
+
+            @pl.when(role_q)
+            def _():
+                for side, weight in others:
+                    sum_2[side] = sum_2[side] + dot(weight, near_2, 0, 0)
+                if neighbour:
+                    put(near_out, 1, jnp.zeros((PAIR, BLOCK), F32), True)
+
+            @pl.when(jnp.logical_not(role_q))
+            def _():
+                total = sum([second(weight, side) for side, weight in others])
+                put(near_out if neighbour else keep, 1, total, True)
+
+        crosses = jnp.where(role_q, zh, 1 - zh) == 1
+
+        @pl.when(crosses)
+        def _():
+            here, weight_here = side_work(0)
+            there, weight_there = side_work(1)
+            store(here + there, ((0, weight_here), (1, weight_there)))
+
+        @pl.when(jnp.logical_not(crosses))
+        def _():
+            here, weight_here = side_work(0)
+            store(here, ((0, weight_here),))
+
+    for half_at in range(2):
+        work(mine, False, half_at)
+        work(near_in, True, half_at)
+
+    for spot in range(4):
+        rows = slice(spot * BLOCK, (spot + 1) * BLOCK)
+        keep[spot, 2] = sum_1[0, rows] * grad_scale
+        far_out[spot, 0] = (sum_1[1, rows] * grad_scale).astype(BF16)
+        far_out[spot, 1] = (sum_2[1, rows] * (1.0 / seq_len)).astype(BF16)
+
+        @pl.when(role_q)
+        def _():
+            keep[spot, 1] = sum_2[0, rows] * (1.0 / seq_len)
+
+
+def project_body(info, dealt, weight, partial, sent):
+    core = info[0]
+
+    def rows(slot):
+        return jnp.concatenate([dealt[h, slot] for h in range(4)], axis=1)
+
+    total = dot(rows(1), weight[2], 1, 1)
+    total = total + dot(rows(0), weight[core], 1, 1)
+    total = total + dot(rows(2), weight[1 - core], 1, 1)
+    partial[...] = total
+    sent[...] = total.astype(BF16)
+
+
+def pack_body(info, own, other, adapter, placing, out, grad, turned):
+    core = info[0]
+    n_ctx = out.shape[0]
+    head_cols = adapter.shape[1]
+    capacity = placing.shape[1] // n_ctx
+    tiles = head_cols // BLOCK
+    share = own.shape[1] // n_ctx // 2
+    total = own[...] + other[...].astype(F32)
+    grad[...] = total
+    rounded = total.astype(BF16)
+    turned[...] = jnp.transpose(rounded)
+    rows = grad[:, pl.ds(pl.multiple_of(core * head_cols, head_cols), head_cols)]
+    rows = rows + dot(rounded, adapter[...], 1, 0)
+    cells = dot(placing[...], rows.astype(BF16), 0, 0).astype(BF16)
+    for p in range(n_ctx):
+        for tile in range(tiles):
+            out[p, tile * capacity : (tile + 1) * capacity, :] = cells[
+                p * capacity : (p + 1) * capacity, tile * BLOCK : (tile + 1) * BLOCK
+            ]
+        first = pl.multiple_of(p * 2 * share + core * share, share)
+        out[p, tiles * capacity : tiles * capacity + share, :] = turned[pl.ds(first, share), :]
+
+
+def place_body(info, owners, slots, rows, placing, sent):
+    core = info[0]
+    count = owners.shape[0]
+    head_cols = sent.shape[1]
+    capacity = placing.shape[1] // 16
+    owner = jnp.broadcast_to(owners[...], (count, BLOCK))
+    lane = lax.broadcasted_iota(jnp.int32, (count, BLOCK), 1)
+    row = lax.broadcasted_iota(jnp.int32, (count, BLOCK), 0)
+    named = owner == lane
+    earlier = (lane < row).astype(F32).astype(BF16)
+    prior = dot(earlier, named.astype(F32).astype(BF16), 1, 0)
+    ranking = jnp.sum(jnp.where(named, prior, 0.0), axis=1, keepdims=True)
+    cell = jnp.broadcast_to(owners[...].astype(F32) * capacity + ranking, (count, BLOCK))
+    for tile in range(placing.shape[1] // BLOCK):
+        hit = cell == (lane + tile * BLOCK).astype(F32)
+        placing[:, tile * BLOCK : (tile + 1) * BLOCK] = hit.astype(F32).astype(BF16)
+    sent[0:count, :] = rows[:, pl.ds(pl.multiple_of(core * head_cols, head_cols), head_cols)]
+    cell_row = jnp.transpose(cell)[0:META]
+    at = lax.broadcasted_iota(jnp.int32, (META, BLOCK), 0)
+    slot_row = jnp.broadcast_to(slots[...], (META, BLOCK)).astype(F32)
+    meta = jnp.where(at == 0, cell_row, jnp.where(at == 1, slot_row, 0.0))
+    sent[count : count + META, 0:BLOCK] = meta.astype(BF16)
+    sent[count : count + META, BLOCK:] = jnp.zeros((META, head_cols - BLOCK), BF16)
+
+
+def land_body(info, gathered, landing, touched):
+    me = info[3]
+    table_rows, cells = landing.shape
+    block = BLOCK + META
+    n_ctx = gathered.shape[0] // block
+    capacity = cells // n_ctx
+    total = jnp.zeros((table_rows, cells), F32)
+    row = lax.broadcasted_iota(jnp.int32, (table_rows, BLOCK), 0).astype(F32)
+    cell_at = lax.broadcasted_iota(jnp.int32, (cells, BLOCK), 0).astype(F32)
+    for s in range(n_ctx):
+        meta = gathered[s * block + BLOCK : (s + 1) * block, 0:BLOCK].astype(F32)
+        local = meta[0:1] - (me * capacity).astype(F32)
+        inside = (local >= 0) & (local < capacity)
+        local = jnp.where(inside, local + s * capacity, -1.0)
+        slot = (row == meta[1:2]).astype(F32).astype(BF16)
+        cell = (cell_at == local).astype(F32).astype(BF16)
+        total = total + dot(slot, cell, 1, 1)
+    landing[...] = total.astype(BF16)
+    hits = jnp.sum(total, axis=1, keepdims=True)
+    touched[...] = jnp.broadcast_to(hits, touched.shape)
+
+
+def finish_body(info, got, other, gathered, landing, touched, table, moment_m, moment_v, grad, new_table, new_m, new_v):
+    core = info[0]
+    n_ctx, capacity = got.shape[0], landing.shape[1] // got.shape[0]
+    share = other.shape[1]
+    block = BLOCK + META
+    tiles = table.shape[1] // BLOCK
+    width = tiles * capacity
+    for tile in range(tiles):
+        cols = slice(tile * BLOCK, (tile + 1) * BLOCK)
+        cells = got[:, tile * capacity : (tile + 1) * capacity, :].reshape(n_ctx * capacity, BLOCK)
+        summed = dot(landing[...], cells, 1, 0)
+        keep = touched[...] > 0.0
+        m, v, old = moment_m[:, cols], moment_v[:, cols], table[:, cols]
+        fresh_m = beta_first * m + (1.0 - beta_first) * summed
+        fresh_v = beta_second * v + (1.0 - beta_second) * summed * summed
+        update = learn_rate * (fresh_m / first_fix) / (jnp.sqrt(fresh_v / second_fix) + epsilon)
+        new_table[:, cols] = jnp.where(keep, old - update, old)
+        new_m[:, cols] = jnp.where(keep, fresh_m, m)
+        new_v[:, cols] = jnp.where(keep, fresh_v, v)
+    mine_t = jnp.concatenate([got[s, width : width + share, :] for s in range(n_ctx)], axis=1)
+    other_t = jnp.concatenate([other[s] for s in range(n_ctx)], axis=1)
+    rows = jnp.concatenate([gathered[s * block : s * block + BLOCK, :] for s in range(n_ctx)], axis=0)
+    both = dot(jnp.concatenate([mine_t, other_t], axis=0), rows, 1, 0)
+    grad[pl.ds(pl.multiple_of(core * share, share), share), :] = both[:share]
+    grad[pl.ds(pl.multiple_of((1 - core) * share, share), share), :] = both[share:]
+
+
+def dealt_device(
+    queries,
+    keys_values,
+    attn_cot,
+    event_rows,
+    adapter,
+    qkv_weight,
+    starts,
+    owners,
+    slots,
+    table,
+    moment_m,
+    moment_v,
+):
+    shape = jax.ShapeDtypeStruct
+    n_ctx = lax.axis_size("ctx")
+    rows_here = queries.shape[0]
+    seq_len = rows_here * n_ctx
+    head_cols = adapter.shape[1]
+    width = event_rows.shape[1]
+    capacity = max(2, 2 * rows_here // n_ctx)
+    me = lax.axis_index("ctx")
+    info = jnp.stack([lax.axis_index("head"), me // 8, me // 2 % 2, me]).astype(jnp.int32)
+    placing, sent_rows = kernel_call(
+        place_body,
+        (shape((rows_here, n_ctx * capacity), BF16), shape((rows_here + META, head_cols), BF16)),
+        (info, owners, slots.reshape(1, rows_here), event_rows),
+        "place",
+    )
+    dealt = kernel_call(
+        deal_body, shape((4, 2 * PART, BLOCK), BF16), (info, starts, queries, keys_values, attn_cot), "deal"
+    )
+    mine = lax.all_to_all(dealt, "ctx", 0, 0, tiled=True, axis_index_groups=GROUPS)
+    gathered = lax.all_gather(sent_rows, "ctx", axis=0, tiled=True)
+    far_in = lax.ppermute(mine[:, PART:], ("ctx", "head"), FAR_OUT)
+    near_in = lax.ppermute(mine[:, :PART], "ctx", ACROSS_Y)
+    keep, near_out, far_out = pl.pallas_call(
+        functools.partial(attend_body, 1.0 / math.sqrt(HD), float(seq_len)),
+        out_shape=(
+            shape((4, 3, BLOCK, BLOCK), F32),
+            shape((4, 2, BLOCK, BLOCK), BF16),
+            shape((4, 2, BLOCK, BLOCK), BF16),
+        ),
+        in_specs=[SMEM, VMEM, VMEM, VMEM],
+        out_specs=(VMEM, VMEM, VMEM),
+        scratch_shapes=[
+            pltpu.VMEM((2, 4 * BLOCK, BLOCK), BF16),
+            pltpu.VMEM((2, 4 * BLOCK, BLOCK), BF16),
+            pltpu.VMEM((2, 4 * BLOCK, BLOCK), F32),
+            pltpu.VMEM((2, 4 * BLOCK, BLOCK), F32),
+        ],
+        compiler_params=pltpu.CompilerParams(vmem_limit_bytes=24 * 1024 * 1024),
+        cost_estimate=pl.CostEstimate(flops=2 * 10**9, bytes_accessed=2**21, transcendentals=0),
+        name="attend",
+    )(info, mine, near_in, far_in)
+    far_back = lax.ppermute(far_out, ("ctx", "head"), FAR_BACK).astype(F32)
+    near_back = lax.ppermute(near_out, "ctx", ACROSS_Y).astype(F32)
+    head_grads = jnp.stack(
+        [
+            keep[:, 0] + near_back[:, 0],
+            keep[:, 1] + near_back[:, 1] + far_back[:, 1],
+            keep[:, 2] + far_back[:, 0],
+        ],
+        axis=1,
+    ).astype(BF16)
+    head_grads = lax.all_to_all(head_grads, "ctx", 0, 0, tiled=True, axis_index_groups=GROUPS)
+    partial, sent = kernel_call(
+        project_body,
+        (shape((rows_here, width), F32), shape((rows_here, width), BF16)),
+        (info, head_grads, qkv_weight),
+        "project",
+    )
+    other = lax.ppermute(sent, "head", SWAP)
+    share = width // n_ctx // 2
+    packed_rows = capacity * head_cols // BLOCK
+    packed = pl.pallas_call(
+        pack_body,
+        out_shape=shape((n_ctx, packed_rows + share, BLOCK), BF16),
+        in_specs=[SMEM] + [VMEM] * 4,
+        out_specs=VMEM,
+        scratch_shapes=[pltpu.VMEM((rows_here, width), F32), pltpu.VMEM((width, rows_here), BF16)],
+        compiler_params=pltpu.CompilerParams(vmem_limit_bytes=24 * 1024 * 1024),
+        name="pack",
+    )(info, partial, other, adapter, placing)
+    got = lax.all_to_all(packed, "ctx", 0, 0, tiled=True)
+    other_share = lax.ppermute(got[:, packed_rows:], "head", SWAP)
+    landing, touched = kernel_call(
+        land_body,
+        (shape((table.shape[0], n_ctx * capacity), BF16), shape((table.shape[0], BLOCK), F32)),
+        (info, gathered),
+        "land",
+    )
+    held = shape(table.shape, F32)
+    return kernel_call(
+        finish_body,
+        (shape((width // n_ctx, head_cols), F32), held, held, held),
+        (info, got, other_share, gathered, landing, touched, table, moment_m, moment_v),
+        "finish",
+    )
+
+
+def per_device(*arrays):
+    rows_here, cols_here = arrays[0].shape
+    fits = lax.axis_size("ctx") == 16 and lax.axis_size("head") == 2
+    if fits and rows_here == BLOCK and cols_here == 4 * HD and arrays[9].shape[0] == 2 * BLOCK:
+        return dealt_device(*arrays)
+    return plain_device(*arrays)
+
+
 def solution(mesh):
     placed = (
         P("ctx", "head"),

time: 368 us -> 111 us (0.30)
  waiting for transfers between devices: 242 us -> 16.8 us
  matrix products: 27.9 us -> 0 us
  Pallas kernels: 0 us -> 14.1 us
  local copies, waits for them, and re-layouts: 20.5 us -> 6.86 us
  other arithmetic: 6.89 us -> 0.33 us
  blocking collectives: 42.5 us -> 48.6 us
    all_gather x3 -> x1, waiting for transfers between devices: 152 us -> 0.02 us  [dealt_device(): gathered = lax.all_gather(sent_rows, 'ctx', axis=0, tiled=True)]
    all_to_all x0 -> x3, blocking collectives: none -> 48.6 us  [the longest x1 17.6 us: dealt_device(): got = lax.all_to_all(packed, 'ctx', 0, 0, tiled=True)]
    reduce_scatter x1 -> x0, waiting for transfers between devices: 48.4 us -> none  [per_device(): lax.psum_scatter(lax.dot_general(layer_grad_b, own_rows, (((0,), (0,)), (...]
    all_gather x1 -> x0, blocking collectives: 42.5 us -> none  [per_device(): lax.all_gather(lower, 'ctx', axis=0, tiled=True)]
    dot_general x10 -> x0, matrix products: 27.9 us -> none  [the longest x1 4.63 us: query_working(): jnp.einsum('hij,ihd->jhd', dscore, query_part, preferred_element_type=jnp...]
    psum x1 -> x0, waiting for transfers between devices: 26.7 us -> none  [per_device(): lax.psum(partial_grad.astype(jnp.bfloat16), 'head').astype(jnp.float32)]
    ppermute x0 -> x6, waiting for transfers between devices: none -> 16.7 us  [the longest x1 7.09 us: dealt_device(): near_back = lax.ppermute(near_out, 'ctx', ACROSS_Y).astype(F32)]
    all_to_all x2 -> x0, waiting for transfers between devices: 14.9 us -> none  [the longest x1 10.4 us: per_device(): lax.all_to_all(send_rows.astype(jnp.bfloat16), 'ctx', split_axis=0, conca...]
  transfers between devices with their start and end apart: 7 -> 7, of which waited for: 7 -> 4; matrix products, arithmetic and copies ran while one was open for 9% -> 0% of each run, Pallas kernels for 0% -> 9%
where the time goes in v1:
time: 111 us; the launch traced here: 110 us
  blocking collectives  48.6 us (44%)
  waiting for transfers between devices  16.8 us (15%)
  between operations  14.9 us (13%)
  Pallas kernels  14.1 us (13%)
  starting transfers between devices  8.94 us (8%)
  local copies, waits for them, and re-layouts  6.86 us (6%)
    all_to_all x1, blocking collectives, dealt_device(): got = lax.all_to_all(packed, 'ctx', 0, 0, tiled=True)  17.6 us
    all_to_all x1, blocking collectives, dealt_device(): lax.all_to_all(head_grads, 'ctx', 0, 0, tiled=True, axis_index_groups=GRO...  15.8 us
    all_to_all x1, blocking collectives, dealt_device(): lax.all_to_all(dealt, 'ctx', 0, 0, tiled=True, axis_index_groups=GROUPS)  15.3 us
    pallas_call x5, Pallas kernels, kernel_call(): pl.pallas_call(body, out_shape=out_shape, in_specs=specs, out_specs=jax.t...  7.73 us
    ppermute x1, waiting for transfers between devices, dealt_device(): near_back = lax.ppermute(near_out, 'ctx', ACROSS_Y).astype(F32)  7.09 us
    unnamed x23, local copies, waits for them, and re-layouts  6.81 us
    ppermute x1, starting transfers between devices, dealt_device(): far_in = lax.ppermute(mine[:, PART:], ('ctx', 'head'), FAR_OUT)  5.54 us
    pallas_call x1, Pallas kernels, dealt_device(): pl.pallas_call(functools.partial(attend_body, 1.0 / math.sqrt(HD), float(...  5.28 us
  transfers between devices with their start and end apart: 7, of which 4 were waited for; matrix products, arithmetic and copies ran while one was open for 0% of the time, Pallas kernels for 9%

profile of v1, /device:TPU:0, one launch (start us, length us, event | category | flops | bytes accessed | tf_op | source)
XLA Modules:
  0.0 110.5 jit_solution(13757499440824365609)
XLA Ops:
  7.2 0.0 all-gather.2.cloned.1.call-start
  7.2 0.8 copy.16.owners
  8.0 0.1 pad_add_fusion.info
  8.1 0.0 copy-start.7
  8.1 0.9 copy-done.7
  9.0 0.0 copy-start.10
  9.0 0.7 copy-done.10
  9.7 1.6 %place.1 = (bf16[128,256]{1,0:T(8,128)(2,1)S(1)}, bf16[144,512]{1,0:T(8,128)(2,1)}) custom-call(s32[4]{0:T(128)S(1)} %pad_add_fusion.info, s32[128,1]{1,0:T(8,128)S(1)} %copy.16.owners, s32[1,128]{1,0:T(1,128)S(1)} %bitcast.5, bf16[128,1024]{1,0:T(8,128)(2,1)S(1)} %copy-done.7), custom_call_target="tpu_custom_call" | custom-call | tf_op jit(solution)/shard_map/place/pallas_call | solution.py:237
  11.3 0.0 all-gather.2.cloned.1.call-update
  12.0 0.0 copy-start.6
  12.0 0.9 copy-done.6
  12.9 0.0 copy-start.8
  12.9 0.9 copy-done.8
  13.8 0.0 copy-start.9
  13.9 0.9 copy-done.9
  14.8 0.6 deal.1
  15.4 15.3 %all_to_all.15.mine = bf16[4,544,128]{2,1,0:T(8,128)(2,1)S(1)} all-to-all(bf16[4,544,128]{2,1,0:T(8,128)(2,1)S(1)} %deal.1), channel_id=1, replica_groups={{0,2,8,10},{4,6,12,14},{16,18,24,26},{20,22,28,30},{1,3,9,11},{5,7,13,1..., dimensions={0} | all-to-all | bytes 1114112 | tf_op jit(solution)/shard_map/all_to_all | solution.py:536
  30.7 1.6 %collective-permute-start = (bf16[4,272,128]{2,1,0:T(8,128)(2,1)S(1)}, bf16[4,272,128]{2,1,0:T(8,128)(2,1)S(1)}, u32[]{:S(2)}, u32[]{:S(2)}) collective-permute-start(bf16[4,272,128]{2,1,0:T(8,128)(2,1)S(1)} %get-tuple-element.26), channel_id=1, source_target_pairs={{0,4},{2,6},{4,0},{6,2},{8,12},{10,14},{12,8},{14,10},{16,20},{18,... | collective-permute-start | bytes 835592 | tf_op jit(solution)/shard_map/ppermute | solution.py:539
  32.3 5.5 %collective-permute-start.1 = (bf16[4,272,128]{2,1,0:T(8,128)(2,1)S(1)}, bf16[4,272,128]{2,1,0:T(8,128)(2,1)S(1)}, u32[]{:S(2)}, u32[]{:S(2)}) collective-permute-start(bf16[4,272,128]{2,1,0:T(8,128)(2,1)S(1)} %get-tuple-element.25), channel_id=1, source_target_pairs={{0,16},{2,18},{4,20},{6,22},{8,24},{10,26},{12,28},{14,30},{17,1},... | collective-permute-start | bytes 835592 | tf_op jit(solution)/shard_map/ppermute | solution.py:538
  37.9 0.0 collective-permute-done.near_in
  37.9 4.8 %collective-permute-done.1.far_in = bf16[4,272,128]{2,1,0:T(8,128)(2,1)S(1)} collective-permute-done((bf16[4,272,128]{2,1,0:T(8,128)(2,1)S(1)}, bf16[4,272,128]{2,1,0:T(8,128)(2,1)S(1)}, u32[]{:S(2)}, u32[]{:S(2)}) %collective-permute-start.1) | collective-permute-done | bytes 278560 | tf_op jit(solution)/shard_map/ppermute | solution.py:538
  42.7 5.3 %attend.1 = (f32[4,3,128,128]{3,2,1,0:T(8,128)S(1)}, bf16[4,2,128,128]{3,2,1,0:T(8,128)(2,1)S(1)}, bf16[4,2,128,128]{3,2,1,0:T(8,128)(2,1)S(1)}) custom-call(s32[4]{0:T(128)S(1)} %pad_add_fusion.info, bf16[4,544,128]{2,1,0:T(8,128)(2,1)S(1)} %all_to_all.15.mine, bf16[4,272,128]{2,1,0:T(8,128)(2,1)S(1)} %collective-permute-done.near_in, ...), custom_call_target="tpu_custom_call" | custom-call | flops 2000000000 | bytes 2097152 | tf_op jit(solution)/shard_map/attend/pallas_call | solution.py:540
  48.0 0.0 copy-start.1
  48.0 0.1 collective-permute-start.2
  48.1 1.6 %collective-permute-start.3 = (bf16[4,2,128,128]{3,2,1,0:T(8,128)(2,1)S(1)}, bf16[4,2,128,128]{3,2,1,0:T(8,128)(2,1)S(1)}, u32[]{:S(2)}, u32[]{:S(2)}) collective-permute-start(bf16[4,2,128,128]{3,2,1,0:T(8,128)(2,1)S(1)} %get-tuple-element.15), channel_id=1, source_target_pairs={{16,0},{18,2},{20,4},{22,6},{24,8},{26,10},{28,12},{30,14},{1,17},... | collective-permute-start | bytes 786440 | tf_op jit(solution)/shard_map/ppermute | solution.py:559
  49.7 7.1 %collective-permute-done.2 = bf16[4,2,128,128]{3,2,1,0:T(8,128)(2,1)S(1)} collective-permute-done((bf16[4,2,128,128]{3,2,1,0:T(8,128)(2,1)S(1)}, bf16[4,2,128,128]{3,2,1,0:T(8,128)(2,1)S(1)}, u32[]{:S(2)}, u32[]{:S(2)}) %collective-permute-start.2) | collective-permute-done | bytes 262176 | tf_op jit(solution)/shard_map/ppermute | solution.py:560
  56.8 3.3 %collective-permute-done.3 = bf16[4,2,128,128]{3,2,1,0:T(8,128)(2,1)S(1)} collective-permute-done((bf16[4,2,128,128]{3,2,1,0:T(8,128)(2,1)S(1)}, bf16[4,2,128,128]{3,2,1,0:T(8,128)(2,1)S(1)}, u32[]{:S(2)}, u32[]{:S(2)}) %collective-permute-start.3) | collective-permute-done | bytes 262176 | tf_op jit(solution)/shard_map/ppermute | solution.py:559
  60.1 0.0 copy-start.2
  60.1 0.1 fusion.2
  60.3 15.8 %all_to_all.16.dealt = bf16[4,3,128,128]{3,2,1,0:T(8,128)(2,1)S(1)} all-to-all(bf16[4,3,128,128]{3,2,1,0:T(8,128)(2,1)S(1)} %pad_maximum_fusion), channel_id=1, replica_groups={{0,2,8,10},{4,6,12,14},{16,18,24,26},{20,22,28,30},{1,3,9,11},{5,7,13,1..., dimensions={0} | all-to-all | bytes 786432 | tf_op jit(solution)/shard_map/all_to_all | solution.py:569
  76.0 0.0 copy-done.1
  76.1 1.7 %project.1 = (f32[128,1024]{1,0:T(8,128)S(1)}, bf16[128,1024]{1,0:T(8,128)(2,1)S(1)}) custom-call(s32[4]{0:T(128)S(1)} %pad_add_fusion.info, bf16[4,3,128,128]{3,2,1,0:T(8,128)(2,1)S(1)} %all_to_all.16.dealt, bf16[3,1024,512]{2,1,0:T(8,128)(2,1)S(1)} %copy-done.1), custom_call_target="tpu_custom_call" | custom-call | tf_op jit(solution)/shard_map/project/pallas_call | solution.py:237
  77.7 0.0 copy-start.3
  77.8 0.0 copy-start.4
  77.8 0.0 copy-start.5
  77.8 0.1 collective-permute-start.4
  77.9 1.5 %collective-permute-done.4.other = bf16[128,1024]{1,0:T(8,128)(2,1)S(1)} collective-permute-done((bf16[128,1024]{1,0:T(8,128)(2,1)S(1)}, bf16[128,1024]{1,0:T(8,128)(2,1)S(1)}, u32[]{:S(2)}, u32[]{:S(2)}) %collective-permute-start.4) | collective-permute-done | bytes 262176 | tf_op jit(solution)/shard_map/ppermute | solution.py:576
  79.4 0.0 copy-done.2
  79.4 1.1 pack.1
  80.5 17.6 %all_to_all.17.got = bf16[16,96,128]{2,1,0:T(8,128)(2,1)S(1)} all-to-all(bf16[16,96,128]{2,1,0:T(8,128)(2,1)S(1)} %pack.1), channel_id=1, replica_groups=mesh['ctx'=16,'head'=2] {'ctx'}, dimensions={0} | all-to-all | bytes 786432 | tf_op jit(solution)/shard_map/all_to_all | solution.py:588
  98.0 0.1 collective-permute-start.5
  98.1 0.0 all-gather.2.cloned.1.call-done.gathered
  98.2 0.0 copy-start
  98.2 1.7 %copy-done = bf16[2304,512]{1,0:T(8,128)(2,1)S(1)} copy-done((bf16[2304,512]{1,0:T(8,128)(2,1)S(1)}, bf16[2304,512]{1,0:T(8,128)(2,1)}, u32[]{:S(2)}) %copy-start) | copy-done | bytes 2359320
  99.8 1.3 %land.1 = (bf16[256,256]{1,0:T(8,128)(2,1)S(1)}, f32[256,128]{1,0:T(8,128)S(1)}) custom-call(s32[4]{0:T(128)S(1)} %pad_add_fusion.info, bf16[2304,512]{1,0:T(8,128)(2,1)S(1)} %copy-done), custom_call_target="tpu_custom_call" | custom-call | tf_op jit(solution)/shard_map/land/pallas_call | solution.py:237
  101.1 0.0 collective-permute-done.5.other
  101.2 0.0 copy-done.3
  101.2 0.0 copy-done.4
  101.2 0.0 copy-done.5
  101.2 2.5 %finish.1 = (f32[64,512]{1,0:T(8,128)}, f32[256,512]{1,0:T(8,128)}, f32[256,512]{1,0:T(8,128)}, f32[256,512]{1,0:T(8,128)}) custom-call(s32[4]{0:T(128)S(1)} %pad_add_fusion.info, bf16[16,96,128]{2,1,0:T(8,128)(2,1)S(1)} %all_to_all.17.got, bf16[16,32,128]{2,1,0:T(8,128)(2,1)S(1)} %collective-permute-done.5.other, bf16[2304,512]{1,0:T(8,128)(2,1)S(1)} %copy-done, ...), custom_call_target="tpu_custom_call" | custom-call | tf_op jit(solution)/shard_map/finish/pallas_call | solution.py:237
  (5 shorter events, 0.2 us)
Async XLA Ops:
  7.2 91.0 %all-gather.2.cloned.1.call-start = ((), (), s32[]{:S(2)}) async-start(), calls=%async_computation.3 | async-start | bytes 2506752 | tf_op jit(solution)/shard_map/all_gather | solution.py:537
  8.1 1.0 copy-start.7
  9.0 0.7 copy-start.10
  12.0 1.0 copy-start.6
  12.9 0.9 copy-start.8
  13.8 0.9 copy-start.9
  30.7 7.1 %collective-permute-start = (bf16[4,272,128]{2,1,0:T(8,128)(2,1)S(1)}, bf16[4,272,128]{2,1,0:T(8,128)(2,1)S(1)}, u32[]{:S(2)}, u32[]{:S(2)}) collective-permute-start(bf16[4,272,128]{2,1,0:T(8,128)(2,1)S(1)} %get-tuple-element.26), channel_id=1, source_target_pairs={{0,4},{2,6},{4,0},{6,2},{8,12},{10,14},{12,8},{14,10},{16,20},{18,... | collective-permute-start | bytes 835592 | tf_op jit(solution)/shard_map/ppermute | solution.py:539
  32.3 10.4 %collective-permute-start.1 = (bf16[4,272,128]{2,1,0:T(8,128)(2,1)S(1)}, bf16[4,272,128]{2,1,0:T(8,128)(2,1)S(1)}, u32[]{:S(2)}, u32[]{:S(2)}) collective-permute-start(bf16[4,272,128]{2,1,0:T(8,128)(2,1)S(1)} %get-tuple-element.25), channel_id=1, source_target_pairs={{0,16},{2,18},{4,20},{6,22},{8,24},{10,26},{12,28},{14,30},{17,1},... | collective-permute-start | bytes 835592 | tf_op jit(solution)/shard_map/ppermute | solution.py:538
  48.0 28.1 %copy-start.1 = (bf16[3,1024,512]{2,1,0:T(8,128)(2,1)S(1)}, bf16[3,1024,512]{2,1,0:T(8,128)(2,1)}, u32[]{:S(2)}) copy-start(bf16[3,1024,512]{2,1,0:T(8,128)(2,1)} %weight.1) | copy-start | bytes 9437188
  48.0 8.7 %collective-permute-start.2 = (bf16[4,2,128,128]{3,2,1,0:T(8,128)(2,1)S(1)}, bf16[4,2,128,128]{3,2,1,0:T(8,128)(2,1)S(1)}, u32[]{:S(2)}, u32[]{:S(2)}) collective-permute-start(bf16[4,2,128,128]{3,2,1,0:T(8,128)(2,1)S(1)} %get-tuple-element.14), channel_id=1, source_target_pairs={{0,4},{2,6},{4,0},{6,2},{8,12},{10,14},{12,8},{14,10},{16,20},{18,... | collective-permute-start | bytes 786440 | tf_op jit(solution)/shard_map/ppermute | solution.py:560
  48.1 12.0 %collective-permute-start.3 = (bf16[4,2,128,128]{3,2,1,0:T(8,128)(2,1)S(1)}, bf16[4,2,128,128]{3,2,1,0:T(8,128)(2,1)S(1)}, u32[]{:S(2)}, u32[]{:S(2)}) collective-permute-start(bf16[4,2,128,128]{3,2,1,0:T(8,128)(2,1)S(1)} %get-tuple-element.15), channel_id=1, source_target_pairs={{16,0},{18,2},{20,4},{22,6},{24,8},{26,10},{28,12},{30,14},{1,17},... | collective-permute-start | bytes 786440 | tf_op jit(solution)/shard_map/ppermute | solution.py:559
  60.1 19.3 %copy-start.2 = (bf16[1024,512]{1,0:T(8,128)(2,1)S(1)}, bf16[1024,512]{1,0:T(8,128)(2,1)}, u32[]{:S(2)}) copy-start(bf16[1024,512]{1,0:T(8,128)(2,1)} %adapter.1) | copy-start | bytes 3145732
  77.7 23.4 %copy-start.3 = (f32[256,512]{1,0:T(8,128)S(1)}, f32[256,512]{1,0:T(8,128)}, u32[]{:S(2)}) copy-start(f32[256,512]{1,0:T(8,128)} %table.1) | copy-start | bytes 1572868
  77.8 23.4 %copy-start.4 = (f32[256,512]{1,0:T(8,128)S(1)}, f32[256,512]{1,0:T(8,128)}, u32[]{:S(2)}) copy-start(f32[256,512]{1,0:T(8,128)} %moment_m.1) | copy-start | bytes 1572868
  77.8 23.4 %copy-start.5 = (f32[256,512]{1,0:T(8,128)S(1)}, f32[256,512]{1,0:T(8,128)}, u32[]{:S(2)}) copy-start(f32[256,512]{1,0:T(8,128)} %moment_v.1) | copy-start | bytes 1572868
  77.8 1.6 %collective-permute-start.4 = (bf16[128,1024]{1,0:T(8,128)(2,1)S(1)}, bf16[128,1024]{1,0:T(8,128)(2,1)S(1)}, u32[]{:S(2)}, u32[]{:S(2)}) collective-permute-start(bf16[128,1024]{1,0:T(8,128)(2,1)S(1)} %get-tuple-element.17), channel_id=1, source_target_pairs={{0,1},{1,0},{2,3},{3,2},{4,5},{5,4},{6,7},{7,6},{8,9},{9,8},{10,11... | collective-permute-start | bytes 786440 | tf_op jit(solution)/shard_map/ppermute | solution.py:576
  98.0 3.1 %collective-permute-start.5 = (bf16[16,32,128]{2,1,0:T(8,128)(2,1)S(1)}, bf16[16,32,128]{2,1,0:T(8,128)(2,1)S(1)}, u32[]{:S(2)}, u32[]{:S(2)}) collective-permute-start(bf16[16,32,128]{2,1,0:T(8,128)(2,1)S(1)} %slice.46), channel_id=1, source_target_pairs={{0,1},{1,0},{2,3},{3,2},{4,5},{5,4},{6,7},{7,6},{8,9},{9,8},{10,11... | collective-permute-start | bytes 393224 | tf_op jit(solution)/shard_map/ppermute | solution.py:589
  98.2 1.7 %copy-start = (bf16[2304,512]{1,0:T(8,128)(2,1)S(1)}, bf16[2304,512]{1,0:T(8,128)(2,1)}, u32[]{:S(2)}) copy-start(bf16[2304,512]{1,0:T(8,128)(2,1)} %all-gather.2.cloned.1.call-done.gathered) | copy-start | bytes 7077892
Sparse Core Ops, SparseCore 0:
  11.5 72.3 all-gather.1

commit v2 on v0

--- a/solution.py
+++ b/solution.py
@@ -1,8 +1,11 @@
+import functools
 import math
 
 import jax
 import jax.numpy as jnp
 from jax import lax
+from jax.experimental import pallas as pl
+from jax.experimental.pallas import tpu as pltpu
 from jax.sharding import PartitionSpec as P
 
 HD = 128
@@ -61,7 +64,7 @@
     )
 
 
-def per_device(
+def plain_device(
     queries,
     keys_values,
     attn_cot,
@@ -209,6 +212,435 @@
     return (adapter_grad, new_table, new_m, new_v)
 
 
+BLOCK = 128
+PAIR = 2 * BLOCK
+META = 16
+PART = PAIR + META
+ACROSS_Y = [(i, i ^ 2) for i in range(16)]
+FAR_OUT = [(i * 2, (i + 8) * 2) for i in range(8)] + [((i + 8) * 2 + 1, i * 2 + 1) for i in range(8)]
+FAR_BACK = [(b, a) for a, b in FAR_OUT]
+SWAP = [(0, 1), (1, 0)]
+ROUNDS = (8, 4, 1, 2)
+F32 = jnp.float32
+BF16 = jnp.bfloat16
+VMEM = pl.BlockSpec(memory_space=pltpu.VMEM)
+SMEM = pl.BlockSpec(memory_space=pltpu.SMEM)
+
+
+def dot(a, b, axis_a, axis_b):
+    return lax.dot_general(a, b, (((axis_a,), (axis_b,)), ((), ())), preferred_element_type=F32)
+
+
+def spot_of(me):
+    return me // 4 % 2 * 2 + me % 2
+
+
+def kernel_call(body, out_shape, operands, name, flops=0, in_bytes=0):
+    specs = [SMEM if o.dtype == jnp.int32 and o.ndim == 1 else VMEM for o in operands]
+    return pl.pallas_call(
+        body,
+        out_shape=out_shape,
+        in_specs=specs,
+        out_specs=jax.tree.map(lambda _: VMEM, out_shape),
+        compiler_params=pltpu.CompilerParams(vmem_limit_bytes=12 * 1024 * 1024),
+        cost_estimate=pl.CostEstimate(flops=flops, bytes_accessed=in_bytes, transcendentals=0),
+        name=name,
+    )(*operands)
+
+
+def deal_body(starts, queries, keys_values, cot, rows, own, by_x, by_zl, by_both, held_rows, sems):
+    core, me = lax.axis_index("head"), lax.axis_index("ctx")
+    outs = (own, by_x, by_zl, by_both)
+    start = starts[0]
+    row = lax.broadcasted_iota(jnp.int32, (META, BLOCK), 0)
+    meta = jnp.where(row == 0, start // BLOCK, jnp.where(row == 1, start % BLOCK, 0)).astype(F32).astype(BF16)
+    cols = held_rows.shape[1]
+
+    def copies(near, far, half):
+        moves = []
+        for flip, out in enumerate(outs):
+            head = jnp.bitwise_xor(spot_of(me), flip)
+            lanes = pl.ds(pl.multiple_of(head * BLOCK, BLOCK), BLOCK)
+            for base, pair in ((0, near), (PART, far)):
+                for at, source in enumerate(pair):
+                    moves.append((source.at[:, lanes], out.at[base + at * BLOCK : base + (at + 1) * BLOCK, :]))
+        moves.append((rows.at[:, half * cols : (half + 1) * cols], held_rows))
+        moves = [pltpu.make_async_copy(a, b, sems.at[k]) for k, (a, b) in enumerate(moves)]
+        for move in moves:
+            move.start()
+        for out in outs:
+            out[PAIR:PART, :] = meta
+            out[PART + PAIR :, :] = meta
+        for move in moves:
+            move.wait()
+
+    asks = (queries, cot)
+    gives = (keys_values.at[0], keys_values.at[1])
+
+    @pl.when(core == 0)
+    def _():
+        copies(asks, gives, 0)
+
+    @pl.when(core == 1)
+    def _():
+        copies(gives, asks, 1)
+
+
+def attend_body(
+    scale, seq_len, near_own, far_own, near_in, far_in, keep, near_out, far_out, near_1, near_2, far_1, far_2, near_1_sum, near_2_sum, far_1_sum, far_2_sum
+):
+    core, me = lax.axis_index("head"), lax.axis_index("ctx")
+    zh, y = me // 8, me // 2 % 2
+    spots = [jnp.bitwise_xor(spot_of(me), flip) for flip in range(4)]
+    places = [spot // 2 * 4 + spot % 2 for spot in spots]
+    wide = 4 * BLOCK
+
+    def lower_of(meta):
+        meta = meta.astype(F32)
+        return (meta[0:1] * BLOCK + meta[1:2]).astype(jnp.int32)
+
+    for side, (near, far) in enumerate(((near_own, far_own), (near_in, far_in))):
+        for spot in range(4):
+            rows = slice(spot * BLOCK, (spot + 1) * BLOCK)
+            place = slice((4 * side + spot) * BLOCK, (4 * side + spot + 1) * BLOCK)
+            near_1[place, :] = near[spot, :BLOCK, :]
+            near_2[place, :] = near[spot, BLOCK:PAIR, :]
+            far_1[side, rows, :] = far[spot, :BLOCK, :]
+            far_2[side, rows, :] = far[spot, BLOCK:PAIR, :]
+    near_1_sum[...] = jnp.zeros_like(near_1_sum)
+    near_2_sum[...] = jnp.zeros_like(near_2_sum)
+    lane = lax.broadcasted_iota(jnp.int32, (1, BLOCK), 1)
+    row_in = lax.broadcasted_iota(jnp.int32, (BLOCK, wide), 0)
+    grad_scale = scale * 0.5 / seq_len
+    never = 1 << 20
+
+    def work(role_q, side, carry):
+        far_zh = jnp.where(side == 0, zh, 1 - zh)
+        place = jnp.concatenate([lane + (far_zh * 8 + y * 2 + s) * BLOCK for s in places], axis=1)
+        base_1, base_2 = far_1[side], far_2[side]
+        if not role_q:
+            own = jnp.concatenate([lower_of(far_own[s, PAIR:PART, :]) for s in range(4)], axis=1)
+            other = jnp.concatenate([lower_of(far_in[s, PAIR:PART, :]) for s in range(4)], axis=1)
+            low = jnp.where(side == 0, own, other)
+        dscores, weights = [], []
+        for chunk in range(4):
+            rows = slice(chunk * PAIR, (chunk + 1) * PAIR)
+            half = dot(near_1[rows, :], base_1, 1, 1) * (0.5 * scale)
+            dprod = dot(near_2[rows, :], base_2, 1, 1)
+            near_ref, near_y = (near_own, y) if chunk < 2 else (near_in, 1 - y)
+            seen = []
+            for at in range(2):
+                start = (zh * 8 + near_y * 2 + places[chunk % 2 * 2 + at]) * BLOCK
+                if role_q:
+                    low = jnp.concatenate([lower_of(near_ref[chunk % 2 * 2 + at, PAIR:PART, :])] * 4, axis=1)
+                    seen.append(row_in >= jnp.where(place >= low, place - start, never))
+                else:
+                    seen.append((row_in >= low - start) & (row_in <= place - start))
+            seen = jnp.concatenate(seen, axis=0)
+            tanh = jnp.tanh(half)
+            twice = 1.0 + tanh
+            weight = half * twice
+            dscore = (dprod * twice) * (1.0 + half * (1.0 - tanh))
+            weight = jnp.where(seen, weight, 0.0).astype(BF16)
+            dscore = jnp.where(seen, dscore, 0.0).astype(BF16)
+            near_1_sum[rows, :] += dot(dscore, base_1, 1, 0)
+            if not role_q:
+                near_2_sum[rows, :] += dot(weight, base_2, 1, 0)
+            dscores.append(dscore)
+            weights.append(weight)
+        far_1_sum[side] = dot(jnp.concatenate(dscores, axis=0), near_1[...], 0, 0)
+        if role_q:
+            far_2_sum[side] = dot(jnp.concatenate(weights, axis=0), near_2[...], 0, 0)
+        return carry
+
+    for spot in range(4):
+        far_out[spot] = jnp.zeros((2, BLOCK, BLOCK), BF16)
+
+    @pl.when(core == 0)
+    def _():
+        lax.fori_loop(0, 1 + zh, functools.partial(work, True), 0)
+        for spot in range(4):
+            far_rows = slice(spot * BLOCK, (spot + 1) * BLOCK)
+            keep[spot, 1] = far_2_sum[0, far_rows] * (1.0 / seq_len)
+            far_out[spot, 1] = (far_2_sum[1, far_rows] * (1.0 / seq_len)).astype(BF16)
+
+    @pl.when(core == 1)
+    def _():
+        lax.fori_loop(0, 2 - zh, functools.partial(work, False), 0)
+        for spot in range(4):
+            rows = slice(spot * BLOCK, (spot + 1) * BLOCK)
+            keep[spot, 1] = near_2_sum[rows, :] * (1.0 / seq_len)
+
+    for spot in range(4):
+        rows = slice(spot * BLOCK, (spot + 1) * BLOCK)
+        other = slice((4 + spot) * BLOCK, (5 + spot) * BLOCK)
+        keep[spot, 0] = near_1_sum[rows, :] * grad_scale
+        near_out[spot, 0] = (near_1_sum[other, :] * grad_scale).astype(BF16)
+        near_out[spot, 1] = (near_2_sum[other, :] * (1.0 / seq_len)).astype(BF16)
+        keep[spot, 2] = far_1_sum[0, rows] * grad_scale
+        far_out[spot, 0] = (far_1_sum[1, rows] * grad_scale).astype(BF16)
+
+
+def project_body(own, by_x, by_zl, by_both, weight, partial, sent, held):
+    core, me = lax.axis_index("head"), lax.axis_index("ctx")
+    for flip, part in enumerate((own, by_x, by_zl, by_both)):
+        head = jnp.bitwise_xor(spot_of(me), flip)
+        for slot in range(3):
+            held[slot, :, pl.ds(pl.multiple_of(head * BLOCK, BLOCK), BLOCK)] = part[slot]
+    total = dot(held[1], weight[2], 1, 1)
+    total = total + dot(held[0], weight[core], 1, 1)
+    total = total + dot(held[2], weight[1 - core], 1, 1)
+    partial[...] = total
+    sent[...] = total.astype(BF16)
+
+
+def pack_body(own, other, adapter, placing, slots, out, grad, turned):
+    core = lax.axis_index("head")
+    n_ctx = out.shape[0]
+    head_cols = adapter.shape[1]
+    capacity = placing.shape[1] // n_ctx
+    tiles = head_cols // BLOCK
+    share = own.shape[1] // n_ctx // 2
+    total = own[...] + other[...].astype(F32)
+    grad[...] = total
+    rounded = total.astype(BF16)
+    turned[...] = jnp.transpose(rounded)
+    rows = grad[:, pl.ds(pl.multiple_of(core * head_cols, head_cols), head_cols)]
+    rows = rows + dot(rounded, adapter[...], 1, 0)
+    rows = jnp.concatenate([rows.astype(BF16), slots[...]], axis=1)
+    cells = dot(placing[...], rows, 0, 0).astype(BF16)
+    for p in range(n_ctx):
+        for tile in range(tiles + 1):
+            out[p, tile * capacity : (tile + 1) * capacity, :] = cells[
+                p * capacity : (p + 1) * capacity, tile * BLOCK : (tile + 1) * BLOCK
+            ]
+        first = pl.multiple_of(p * 2 * share + core * share, share)
+        out[p, (tiles + 1) * capacity :, :] = turned[pl.ds(first, share), :]
+
+
+def place_body(owners, slots, placing, marks):
+    count = owners.shape[1]
+    capacity = placing.shape[1] // 16
+    lane = lax.broadcasted_iota(jnp.int32, (count, BLOCK), 1)
+    row = lax.broadcasted_iota(jnp.int32, (count, BLOCK), 0)
+    owner_row = jnp.broadcast_to(owners[...].astype(F32), (count, BLOCK))
+    owner = jnp.transpose(owner_row)
+    same = jnp.where((owner == owner_row) & (lane < row), 1.0, 0.0)
+    ranking = jnp.sum(same, axis=1, keepdims=True)
+    cell = owner * capacity + ranking
+    for tile in range(placing.shape[1] // BLOCK):
+        hit = cell == (lane + tile * BLOCK).astype(F32)
+        placing[:, tile * BLOCK : (tile + 1) * BLOCK] = hit.astype(F32).astype(BF16)
+    mark = jnp.broadcast_to(slots[...] + 1, (count, BLOCK)).astype(F32)
+    marks[...] = jnp.transpose(mark).astype(BF16)
+
+
+def merge_body(keep, near, far, *outs):
+    for at, out in enumerate(outs):
+        out[0] = (keep[at, 0] + near[at, 0].astype(F32)).astype(BF16)
+        out[1] = (keep[at, 1] + near[at, 1].astype(F32) + far[at, 1].astype(F32)).astype(BF16)
+        out[2] = (keep[at, 2] + far[at, 0].astype(F32)).astype(BF16)
+
+
+def finish_body(got, other, *refs):
+    pieces, held, grad, targets = refs[:8], refs[8:11], refs[11], refs[12:15]
+    made, rows_held, in_sems, out_sems = refs[15:18], refs[18], refs[19], refs[20]
+    chunks = out_sems.shape[1]
+    span = held[0].shape[0] // chunks
+
+    def rows_of(c):
+        return slice(c * span, (c + 1) * span)
+
+    stores = [
+        [pltpu.make_async_copy(a.at[rows_of(c), :], b.at[rows_of(c), :], out_sems.at[k, c]) for k, (a, b) in enumerate(zip(made, targets))]
+        for c in range(chunks)
+    ]
+    part = rows_held.shape[0] // 8
+    loads = [pltpu.make_async_copy(p, rows_held.at[k * part : (k + 1) * part, :], in_sems.at[k]) for k, p in enumerate(pieces)]
+    for move in loads:
+        move.start()
+    core, me = lax.axis_index("head"), lax.axis_index("ctx")
+    share = other.shape[1]
+    tiles = held[0].shape[1] // BLOCK
+    table_rows = held[0].shape[0]
+    n_ctx = got.shape[0]
+    capacity = (got.shape[1] - share) // (tiles + 1)
+    marks = got[:, tiles * capacity : (tiles + 1) * capacity, :].reshape(n_ctx * capacity, BLOCK).astype(F32)
+    lane = lax.broadcasted_iota(jnp.int32, marks.shape, 1)
+    landing = [(marks == (lane + (at * BLOCK + 1)).astype(F32)).astype(F32) for at in range(table_rows // BLOCK)]
+    landing = jnp.concatenate(landing, axis=1).astype(BF16)
+    cells = [got[:, tile * capacity : (tile + 1) * capacity, :].reshape(n_ctx * capacity, BLOCK) for tile in range(tiles)]
+    cells = jnp.concatenate(cells + [jnp.ones(marks.shape, BF16)], axis=1)
+    summed_all = dot(landing, cells, 0, 0)
+    for c in range(chunks):
+        rows = rows_of(c)
+        summed = summed_all[rows, : tiles * BLOCK]
+        touched = jnp.concatenate([summed_all[rows, tiles * BLOCK :]] * tiles, axis=1) > 0.0
+        old, m, v = [ref[rows, :] for ref in held]
+        fresh_m = beta_first * m + (1.0 - beta_first) * summed
+        fresh_v = beta_second * v + (1.0 - beta_second) * summed * summed
+        update = learn_rate * (fresh_m / first_fix) / (jnp.sqrt(fresh_v / second_fix) + epsilon)
+        made[0][rows, :] = jnp.where(touched, old - update, old)
+        made[1][rows, :] = jnp.where(touched, fresh_m, m)
+        made[2][rows, :] = jnp.where(touched, fresh_v, v)
+        for move in stores[c]:
+            move.start()
+    masks = [0]
+    for bit in ROUNDS:
+        masks = masks + [mask ^ bit for mask in masks]
+    senders = [jnp.bitwise_xor(me, mask) for mask in masks]
+    width = (tiles + 1) * capacity
+    mine_t = jnp.concatenate([got[s, width:, :] for s in senders], axis=1)
+    other_t = jnp.concatenate([other[s] for s in senders], axis=1)
+    both_t = jnp.concatenate([mine_t, other_t], axis=0)
+    for move in loads:
+        move.wait()
+    both = dot(both_t, rows_held[...], 1, 0)
+    grad[pl.ds(pl.multiple_of(core * share, share), share), :] = both[:share]
+    grad[pl.ds(pl.multiple_of((1 - core) * share, share), share), :] = both[share:]
+    for store in stores:
+        for move in store:
+            move.wait()
+
+
+def dealt_device(
+    queries,
+    keys_values,
+    attn_cot,
+    event_rows,
+    adapter,
+    qkv_weight,
+    starts,
+    owners,
+    slots,
+    table,
+    moment_m,
+    moment_v,
+):
+    shape = jax.ShapeDtypeStruct
+    n_ctx = lax.axis_size("ctx")
+    rows_here = queries.shape[0]
+    seq_len = rows_here * n_ctx
+    head_cols = adapter.shape[1]
+    width = event_rows.shape[1]
+    capacity = max(2, 2 * rows_here // n_ctx)
+    dealt = shape((2 * PART, BLOCK), BF16)
+    *dealt, own_rows = pl.pallas_call(
+        deal_body,
+        out_shape=(dealt,) * 4 + (shape((rows_here, head_cols), BF16),),
+        in_specs=[SMEM] + [pl.BlockSpec(memory_space=pl.ANY)] * 4,
+        out_specs=(VMEM,) * 5,
+        scratch_shapes=[pltpu.SemaphoreType.DMA((17,))],
+        compiler_params=pltpu.CompilerParams(vmem_limit_bytes=56 * 1024 * 1024),
+        name="deal",
+    )(starts, queries, keys_values, attn_cot, event_rows)
+
+    def exchange(sent, bit):
+        return lax.ppermute(sent, "ctx", [(i, i ^ bit) for i in range(16)])
+
+    zh_rows = exchange(own_rows, ROUNDS[0])
+    parts = dealt[:1] + [exchange(part, bit) for part, bit in zip(dealt[1:], (1, 4, 5))]
+    *parts, zh_rows = lax.optimization_barrier((*parts, zh_rows))
+    two = jnp.concatenate([own_rows, zh_rows], axis=0)
+    near_own = jnp.stack([part[:PART] for part in parts])
+    far_own = jnp.stack([part[PART:] for part in parts])
+    far_in = lax.ppermute(far_own, ("ctx", "head"), FAR_OUT)
+    near_in = lax.ppermute(near_own, "ctx", ACROSS_Y)
+    zl_rows, x_rows, y_rows = [exchange(two, bit) for bit in ROUNDS[1:]]
+    keep, near_out, far_out = pl.pallas_call(
+        functools.partial(attend_body, 1.0 / math.sqrt(HD), float(seq_len)),
+        out_shape=(
+            shape((4, 3, BLOCK, BLOCK), F32),
+            shape((4, 2, BLOCK, BLOCK), BF16),
+            shape((4, 2, BLOCK, BLOCK), BF16),
+        ),
+        in_specs=[VMEM] * 4,
+        out_specs=(VMEM, VMEM, VMEM),
+        scratch_shapes=[
+            pltpu.VMEM((8 * BLOCK, BLOCK), BF16),
+            pltpu.VMEM((8 * BLOCK, BLOCK), BF16),
+            pltpu.VMEM((2, 4 * BLOCK, BLOCK), BF16),
+            pltpu.VMEM((2, 4 * BLOCK, BLOCK), BF16),
+            pltpu.VMEM((8 * BLOCK, BLOCK), F32),
+            pltpu.VMEM((8 * BLOCK, BLOCK), F32),
+            pltpu.VMEM((2, 4 * BLOCK, BLOCK), F32),
+            pltpu.VMEM((2, 4 * BLOCK, BLOCK), F32),
+        ],
+        compiler_params=pltpu.CompilerParams(vmem_limit_bytes=12 * 1024 * 1024),
+        cost_estimate=pl.CostEstimate(flops=2 * 10**9, bytes_accessed=2**21, transcendentals=0),
+        name="attend",
+    )(near_own, far_own, near_in, far_in)
+    near_out, far_out, zl_rows, x_rows, y_rows = lax.optimization_barrier(
+        (near_out, far_out, zl_rows, x_rows, y_rows)
+    )
+    zl_x_rows = exchange(zl_rows, ROUNDS[2])
+    zl_y_rows = exchange(zl_rows, ROUNDS[3])
+    far_back = lax.ppermute(far_out, ("ctx", "head"), FAR_BACK)
+    near_back = lax.ppermute(near_out, "ctx", ACROSS_Y)
+    own, *parts = kernel_call(
+        merge_body, (shape((3, BLOCK, BLOCK), BF16),) * 4, (keep, near_back, far_back), "merge"
+    )
+    own, *parts, zl_x_rows, zl_y_rows = lax.optimization_barrier((own, *parts, zl_x_rows, zl_y_rows))
+    x_y_rows, zl_x_y_rows = [exchange(rows, ROUNDS[3]) for rows in (x_rows, zl_x_rows)]
+    parts = [exchange(part, bit) for part, bit in zip(parts, (1, 4, 5))]
+    *parts, x_y_rows = lax.optimization_barrier((*parts, x_y_rows))
+    partial, sent = pl.pallas_call(
+        project_body,
+        out_shape=(shape((rows_here, width), F32), shape((rows_here, width), BF16)),
+        in_specs=[VMEM] * 5,
+        out_specs=(VMEM, VMEM),
+        scratch_shapes=[pltpu.VMEM((3, rows_here, queries.shape[1]), BF16)],
+        compiler_params=pltpu.CompilerParams(vmem_limit_bytes=12 * 1024 * 1024),
+        name="project",
+    )(own, *parts, qkv_weight)
+    sent, owners, slots = lax.optimization_barrier((sent, owners, slots))
+    placing, marks = kernel_call(
+        place_body,
+        (shape((rows_here, n_ctx * capacity), BF16), shape((rows_here, BLOCK), BF16)),
+        (owners.reshape(1, rows_here), slots.reshape(1, rows_here)),
+        "place",
+    )
+    other = lax.ppermute(sent, "head", SWAP)
+    other, zl_x_y_rows = lax.optimization_barrier((other, zl_x_y_rows))
+    share = width // n_ctx // 2
+    packed_rows = capacity * (head_cols // BLOCK + 1)
+    packed = pl.pallas_call(
+        pack_body,
+        out_shape=shape((n_ctx, packed_rows + share, BLOCK), BF16),
+        in_specs=[VMEM] * 5,
+        out_specs=VMEM,
+        scratch_shapes=[pltpu.VMEM((rows_here, width), F32), pltpu.VMEM((width, rows_here), BF16)],
+        compiler_params=pltpu.CompilerParams(vmem_limit_bytes=12 * 1024 * 1024),
+        name="pack",
+    )(partial, other, adapter, placing, marks)
+    got = lax.all_to_all(packed, "ctx", 0, 0, tiled=True)
+    other_share = lax.ppermute(got[:, packed_rows:], "head", SWAP)
+    held = shape(table.shape, F32)
+    pieces = (two, zl_rows, x_rows, zl_x_rows, y_rows, zl_y_rows, x_y_rows, zl_x_y_rows)
+    return pl.pallas_call(
+        finish_body,
+        out_shape=(shape((width // n_ctx, head_cols), F32), held, held, held),
+        in_specs=[VMEM] * 2 + [pl.BlockSpec(memory_space=pl.ANY)] * len(pieces) + [VMEM] * 3,
+        out_specs=(VMEM,) + (pl.BlockSpec(memory_space=pl.ANY),) * 3,
+        scratch_shapes=[pltpu.VMEM(table.shape, F32)] * 3
+        + [
+            pltpu.VMEM((n_ctx * rows_here, head_cols), BF16),
+            pltpu.SemaphoreType.DMA((len(pieces),)),
+            pltpu.SemaphoreType.DMA((3, 4)),
+        ],
+        compiler_params=pltpu.CompilerParams(vmem_limit_bytes=12 * 1024 * 1024),
+        name="finish",
+    )(got, other_share, *pieces, table, moment_m, moment_v)
+
+
+def per_device(*arrays):
+    rows_here, cols_here = arrays[0].shape
+    fits = lax.axis_size("ctx") == 16 and lax.axis_size("head") == 2
+    if fits and rows_here == BLOCK and cols_here == 4 * HD and arrays[9].shape[0] == 2 * BLOCK:
+        return dealt_device(*arrays)
+    return plain_device(*arrays)
+
+
 def solution(mesh):
     placed = (
         P("ctx", "head"),

time: 368 us -> 86.4 us (0.23)
  waiting for transfers between devices: 242 us -> 25.4 us
  matrix products: 27.9 us -> 0 us
  blocking collectives: 42.5 us -> 20 us
  local copies, waits for them, and re-layouts: 20.5 us -> 1.94 us
  starting transfers between devices: 10.5 us -> 27.6 us
  between operations: 14.6 us -> 1.48 us
  Pallas kernels: 0 us -> 9.62 us
  other arithmetic: 6.89 us -> 0.08 us
    all_gather x3 -> x0, waiting for transfers between devices: 152 us -> none  [the longest x1 69.1 us: per_device(): piece = lax.all_gather(keys_values, 'ctx', axis=1, tiled=True)]
    reduce_scatter x1 -> x0, waiting for transfers between devices: 48.4 us -> none  [per_device(): lax.psum_scatter(lax.dot_general(layer_grad_b, own_rows, (((0,), (0,)), (...]
    all_gather x1 -> x0, blocking collectives: 42.5 us -> none  [per_device(): lax.all_gather(lower, 'ctx', axis=0, tiled=True)]
    dot_general x10 -> x0, matrix products: 27.9 us -> none  [the longest x1 4.63 us: query_working(): jnp.einsum('hij,ihd->jhd', dscore, query_part, preferred_element_type=jnp...]
    ppermute x0 -> x20, starting transfers between devices: none -> 27.6 us  [the longest x14 18.4 us: exchange(): return lax.ppermute(sent, 'ctx', [(i, i ^ bit) for i in range(16)])]
    psum x1 -> x0, waiting for transfers between devices: 26.7 us -> none  [per_device(): lax.psum(partial_grad.astype(jnp.bfloat16), 'head').astype(jnp.float32)]
    ppermute x0 -> x20, waiting for transfers between devices: none -> 25.4 us  [the longest x14 13.2 us: exchange(): return lax.ppermute(sent, 'ctx', [(i, i ^ bit) for i in range(16)])]
    all_to_all x0 -> x1, blocking collectives: none -> 20 us  [dealt_device(): got = lax.all_to_all(packed, 'ctx', 0, 0, tiled=True)]
  transfers between devices with their start and end apart: 7 -> 20, of which waited for: 7 -> 11; matrix products, arithmetic and copies ran while one was open for 9% -> 1% of each run, Pallas kernels for 0% -> 5%
where the time goes in v2:
time: 86.4 us; the launch traced here: 86.2 us
  starting transfers between devices  27.6 us (32%)
  waiting for transfers between devices  25.4 us (29%)
  blocking collectives  20 us (23%)
  Pallas kernels  9.62 us (11%)
  local copies, waits for them, and re-layouts  1.94 us (2%)
  between operations  1.48 us (2%)
    all_to_all x1, blocking collectives, dealt_device(): got = lax.all_to_all(packed, 'ctx', 0, 0, tiled=True)  20 us
    ppermute x14, starting transfers between devices, exchange(): return lax.ppermute(sent, 'ctx', [(i, i ^ bit) for i in range(16)])  18.4 us
    ppermute x14, waiting for transfers between devices, exchange(): return lax.ppermute(sent, 'ctx', [(i, i ^ bit) for i in range(16)])  13.2 us
    ppermute x1, waiting for transfers between devices, dealt_device(): far_back = lax.ppermute(far_out, ('ctx', 'head'), FAR_BACK)  8.23 us
    ppermute x1, starting transfers between devices, dealt_device(): far_in = lax.ppermute(far_own, ('ctx', 'head'), FAR_OUT)  4.44 us
    pallas_call x1, Pallas kernels, dealt_device(): pl.pallas_call(functools.partial(attend_body, 1.0 / math.sqrt(HD), float(...  2.81 us
    pallas_call x1, Pallas kernels, dealt_device(): pl.pallas_call(finish_body, out_shape=(shape((width // n_ctx, head_cols),...  2.63 us
    pallas_call x1, Pallas kernels, dealt_device(): pl.pallas_call(deal_body, out_shape=(dealt,) * 4 + (shape((rows_here, hea...  2.21 us
  transfers between devices with their start and end apart: 20, of which 11 were waited for; matrix products, arithmetic and copies ran while one was open for 1% of the time, Pallas kernels for 5%

profile of v2, /device:TPU:0, one launch (start us, length us, event | category | flops | bytes accessed | tf_op | source)
XLA Modules:
  0.0 86.2 jit_solution(7912090032309400494)
XLA Ops:
  1.3 2.2 %deal.1 = (bf16[544,128]{1,0:T(8,128)(2,1)}, bf16[544,128]{1,0:T(8,128)(2,1)}, bf16[544,128]{1,0:T(8,128)(2,1)}, bf16[544,128]{1,0:T(8,128)(2,1)}, bf16[128,512]{1,0:T(8,128)(2,1)}) custom-call(s32[1]{0:T(128)S(6)} %copy.17.starts, bf16[128,512]{1,0:T(8,128)(2,1)} %queries.1, bf16[2,128,512]{2,1,0:T(8,128)(2,1)} %keys_values.1, bf16[128,512]{1,0:T(8,128)(2,1)} %cot.1, ...), custom_call_target="tpu_custom_call" | custom-call | tf_op jit(solution)/shard_map/deal/pallas_call | solution.py:528
  3.5 3.0 %collective-permute-start = (bf16[544,128]{1,0:T(8,128)(2,1)}, bf16[544,128]{1,0:T(8,128)(2,1)S(1)}, u32[]{:S(2)}, u32[]{:S(2)}) collective-permute-start(bf16[544,128]{1,0:T(8,128)(2,1)} %get-tuple-element.46), channel_id=1, source_target_pairs={{0,2},{2,0},{4,6},{6,4},{8,10},{10,8},{12,14},{14,12},{16,18},{18,... | collective-permute-start | bytes 417800 | tf_op jit(solution)/shard_map/ppermute | solution.py:539
  6.5 1.6 %collective-permute-start.1 = (bf16[544,128]{1,0:T(8,128)(2,1)}, bf16[544,128]{1,0:T(8,128)(2,1)S(1)}, u32[]{:S(2)}, u32[]{:S(2)}) collective-permute-start(bf16[544,128]{1,0:T(8,128)(2,1)} %get-tuple-element.47), channel_id=1, source_target_pairs={{0,8},{2,10},{4,12},{6,14},{8,0},{10,2},{12,4},{14,6},{16,24},{18,... | collective-permute-start | bytes 417800 | tf_op jit(solution)/shard_map/ppermute | solution.py:539
  8.1 0.0 collective-permute-start.2
  8.1 3.0 %collective-permute-start.3 = (bf16[128,512]{1,0:T(8,128)(2,1)}, bf16[128,512]{1,0:T(8,128)(2,1)S(1)}, u32[]{:S(2)}, u32[]{:S(2)}) collective-permute-start(bf16[128,512]{1,0:T(8,128)(2,1)} %get-tuple-element.49), channel_id=1, source_target_pairs={{0,16},{2,18},{4,20},{6,22},{8,24},{10,26},{12,28},{14,30},{16,0},... | collective-permute-start | bytes 393224 | tf_op jit(solution)/shard_map/ppermute | solution.py:539
  11.1 5.8 %collective-permute-done.3 = bf16[128,512]{1,0:T(8,128)(2,1)S(1)} collective-permute-done((bf16[128,512]{1,0:T(8,128)(2,1)}, bf16[128,512]{1,0:T(8,128)(2,1)S(1)}, u32[]{:S(2)}, u32[]{:S(2)}) %collective-permute-start.3) | collective-permute-done | bytes 131104 | tf_op jit(solution)/shard_map/ppermute | solution.py:539
  16.8 0.0 collective-permute-done
  16.9 0.0 collective-permute-done.1
  16.9 0.6 collective-permute-done.2
  17.5 0.9 %slice_bitcast_fusion.2 = (bf16[1,272,128]{2,1,0:T(8,128)(2,1)S(1)}, bf16[1,272,128]{2,1,0:T(8,128)(2,1)S(1)}, bf16[1,272,128]{2,1,0:T(8,128)(2,1)S(1)}, bf16[1,272,128]{2,1,0:T(8,128)(2,1)S(1)}) fusion(bf16[544,128]{1,0:T(8,128)(2,1)S(1)} %collective-permute-done, bf16[544,128]{1,0:T(8,128)(2,1)} %get-tuple-element.50), kind=kLoop, calls=%fused_computation.4 | loop fusion | bytes 557056 | tf_op jit(solution)/shard_map/stack | solution.py:546
  18.5 1.8 %collective-permute-start.4 = (bf16[4,272,128]{2,1,0:T(8,128)(2,1)S(1)}, bf16[4,272,128]{2,1,0:T(8,128)(2,1)S(1)}, u32[]{:S(2)}, u32[]{:S(2)}) collective-permute-start(bf16[4,272,128]{2,1,0:T(8,128)(2,1)S(1)} %pad_maximum_fusion.near_own), channel_id=1, source_target_pairs={{0,4},{2,6},{4,0},{6,2},{8,12},{10,14},{12,8},{14,10},{16,20},{18,... | collective-permute-start | bytes 835592 | tf_op jit(solution)/shard_map/ppermute | solution.py:548
  20.3 4.4 %collective-permute-start.5 = (bf16[4,272,128]{2,1,0:T(8,128)(2,1)S(1)}, bf16[4,272,128]{2,1,0:T(8,128)(2,1)S(1)}, u32[]{:S(2)}, u32[]{:S(2)}) collective-permute-start(bf16[4,272,128]{2,1,0:T(8,128)(2,1)S(1)} %pad_maximum_fusion.1.far_own), channel_id=1, source_target_pairs={{0,16},{2,18},{4,20},{6,22},{8,24},{10,26},{12,28},{14,30},{17,1},... | collective-permute-start | bytes 835592 | tf_op jit(solution)/shard_map/ppermute | solution.py:547
  24.7 0.9 %constant_dynamic-update-slice_fusion.1 = bf16[256,512]{1,0:T(8,128)(2,1)S(1)} fusion(bf16[128,512]{1,0:T(8,128)(2,1)} %get-tuple-element.49), kind=kLoop, calls=%fused_computation.11 | loop fusion | bytes 262144
  25.6 0.0 copy-start
  25.7 0.6 collective-permute-start.8
  26.2 0.5 collective-permute-start.7
  26.8 2.6 %collective-permute-start.6 = (bf16[256,512]{1,0:T(8,128)(2,1)S(1)}, bf16[256,512]{1,0:T(8,128)(2,1)S(1)}, u32[]{:S(2)}, u32[]{:S(2)}) collective-permute-start(bf16[256,512]{1,0:T(8,128)(2,1)S(1)} %constant_dynamic-update-slice_fusion.refs_0_), channel_id=1, source_target_pairs={{0,8},{2,10},{4,12},{6,14},{8,0},{10,2},{12,4},{14,6},{16,24},{18,... | collective-permute-start | bytes 786440 | tf_op jit(solution)/shard_map/ppermute | solution.py:539
  29.4 0.0 collective-permute-done.4.near_in
  29.4 1.1 %collective-permute-done.5.far_in = bf16[4,272,128]{2,1,0:T(8,128)(2,1)S(1)} collective-permute-done((bf16[4,272,128]{2,1,0:T(8,128)(2,1)S(1)}, bf16[4,272,128]{2,1,0:T(8,128)(2,1)S(1)}, u32[]{:S(2)}, u32[]{:S(2)}) %collective-permute-start.5) | collective-permute-done | bytes 278560 | tf_op jit(solution)/shard_map/ppermute | solution.py:547
  30.5 2.8 %attend.1 = (f32[4,3,128,128]{3,2,1,0:T(8,128)S(1)}, bf16[4,2,128,128]{3,2,1,0:T(8,128)(2,1)S(1)}, bf16[4,2,128,128]{3,2,1,0:T(8,128)(2,1)S(1)}) custom-call(bf16[4,272,128]{2,1,0:T(8,128)(2,1)S(1)} %pad_maximum_fusion.near_own, bf16[4,272,128]{2,1,0:T(8,128)(2,1)S(1)} %pad_maximum_fusion.1.far_own, bf16[4,272,128]{2,1,0:T(8,128)(2,1)S(1)} %collective-permute-done.4.near_in, ...), custom_call_target="tpu_custom_call" | custom-call | flops 2000000000 | bytes 2097152 | tf_op jit(solution)/shard_map/attend/pallas_call | solution.py:550
  33.3 0.0 copy-start.5
  33.3 0.0 copy-start.6
  33.3 0.0 copy-start.1
  33.3 0.0 collective-permute-done.8.refs_4_
  33.3 0.0 collective-permute-done.7.refs_2_
  33.4 0.4 collective-permute-done.6.refs_1_
  33.7 1.5 %collective-permute-start.9 = (bf16[4,2,128,128]{3,2,1,0:T(8,128)(2,1)S(1)}, bf16[4,2,128,128]{3,2,1,0:T(8,128)(2,1)S(1)}, u32[]{:S(2)}, u32[]{:S(2)}) collective-permute-start(bf16[4,2,128,128]{3,2,1,0:T(8,128)(2,1)S(1)} %get-tuple-element.58), channel_id=1, source_target_pairs={{0,4},{2,6},{4,0},{6,2},{8,12},{10,14},{12,8},{14,10},{16,20},{18,... | collective-permute-start | bytes 786440 | tf_op jit(solution)/shard_map/ppermute | solution.py:579
  35.2 1.3 %collective-permute-start.10 = (bf16[4,2,128,128]{3,2,1,0:T(8,128)(2,1)S(1)}, bf16[4,2,128,128]{3,2,1,0:T(8,128)(2,1)S(1)}, u32[]{:S(2)}, u32[]{:S(2)}) collective-permute-start(bf16[4,2,128,128]{3,2,1,0:T(8,128)(2,1)S(1)} %get-tuple-element.59), channel_id=1, source_target_pairs={{16,0},{18,2},{20,4},{22,6},{24,8},{26,10},{28,12},{30,14},{1,17},... | collective-permute-start | bytes 786440 | tf_op jit(solution)/shard_map/ppermute | solution.py:578
  36.5 0.6 collective-permute-start.12
  37.1 0.9 %collective-permute-start.11 = (bf16[256,512]{1,0:T(8,128)(2,1)S(1)}, bf16[256,512]{1,0:T(8,128)(2,1)S(1)}, u32[]{:S(2)}, u32[]{:S(2)}) collective-permute-start(bf16[256,512]{1,0:T(8,128)(2,1)S(1)} %collective-permute-done.6.refs_1_), channel_id=1, source_target_pairs={{0,2},{2,0},{4,6},{6,4},{8,10},{10,8},{12,14},{14,12},{16,18},{18,... | collective-permute-start | bytes 786440 | tf_op jit(solution)/shard_map/ppermute | solution.py:539
  38.0 1.5 %collective-permute-start.16 = (bf16[256,512]{1,0:T(8,128)(2,1)S(1)}, bf16[256,512]{1,0:T(8,128)(2,1)S(1)}, u32[]{:S(2)}, u32[]{:S(2)}) collective-permute-start(bf16[256,512]{1,0:T(8,128)(2,1)S(1)} %collective-permute-done.7.refs_2_), channel_id=1, source_target_pairs={{0,4},{2,6},{4,0},{6,2},{8,12},{10,14},{12,8},{14,10},{16,20},{18,... | collective-permute-start | bytes 786440 | tf_op jit(solution)/shard_map/ppermute | solution.py:539
  39.5 1.5 %collective-permute-done.9.near = bf16[4,2,128,128]{3,2,1,0:T(8,128)(2,1)S(1)} collective-permute-done((bf16[4,2,128,128]{3,2,1,0:T(8,128)(2,1)S(1)}, bf16[4,2,128,128]{3,2,1,0:T(8,128)(2,1)S(1)}, u32[]{:S(2)}, u32[]{:S(2)}) %collective-permute-start.9) | collective-permute-done | bytes 262176 | tf_op jit(solution)/shard_map/ppermute | solution.py:579
  41.0 8.2 %collective-permute-done.10.far = bf16[4,2,128,128]{3,2,1,0:T(8,128)(2,1)S(1)} collective-permute-done((bf16[4,2,128,128]{3,2,1,0:T(8,128)(2,1)S(1)}, bf16[4,2,128,128]{3,2,1,0:T(8,128)(2,1)S(1)}, u32[]{:S(2)}, u32[]{:S(2)}) %collective-permute-start.10) | collective-permute-done | bytes 262176 | tf_op jit(solution)/shard_map/ppermute | solution.py:578
  49.2 0.1 merge.1
  49.3 0.0 collective-permute-done.12.refs_5_
  49.3 0.0 collective-permute-done.11.refs_3_
  49.3 0.0 copy-start.2
  49.4 0.0 copy-start.3
  49.4 0.0 copy-start.4
  49.4 0.8 collective-permute-start.13
  50.2 0.5 collective-permute-start.14
  50.7 2.2 %collective-permute-start.15 = (bf16[3,128,128]{2,1,0:T(8,128)(2,1)S(1)}, bf16[3,128,128]{2,1,0:T(8,128)(2,1)S(1)}, u32[]{:S(2)}, u32[]{:S(2)}) collective-permute-start(bf16[3,128,128]{2,1,0:T(8,128)(2,1)S(1)} %get-tuple-element.68), channel_id=1, source_target_pairs={{0,10},{2,8},{4,14},{6,12},{8,2},{10,0},{12,6},{14,4},{16,26},{18,... | collective-permute-start | bytes 294920 | tf_op jit(solution)/shard_map/ppermute | solution.py:539
  52.9 0.6 collective-permute-start.18
  53.5 0.0 collective-permute-done.16.refs_6_
  53.5 1.4 %collective-permute-done.13.by_x = bf16[3,128,128]{2,1,0:T(8,128)(2,1)S(1)} collective-permute-done((bf16[3,128,128]{2,1,0:T(8,128)(2,1)S(1)}, bf16[3,128,128]{2,1,0:T(8,128)(2,1)S(1)}, u32[]{:S(2)}, u32[]{:S(2)}) %collective-permute-start.13) | collective-permute-done | bytes 98336 | tf_op jit(solution)/shard_map/ppermute | solution.py:539
  54.9 0.9 %collective-permute-done.14.by_zl = bf16[3,128,128]{2,1,0:T(8,128)(2,1)S(1)} collective-permute-done((bf16[3,128,128]{2,1,0:T(8,128)(2,1)S(1)}, bf16[3,128,128]{2,1,0:T(8,128)(2,1)S(1)}, u32[]{:S(2)}, u32[]{:S(2)}) %collective-permute-start.14) | collective-permute-done | bytes 98336 | tf_op jit(solution)/shard_map/ppermute | solution.py:539
  55.8 2.8 %collective-permute-done.15.by_both = bf16[3,128,128]{2,1,0:T(8,128)(2,1)S(1)} collective-permute-done((bf16[3,128,128]{2,1,0:T(8,128)(2,1)S(1)}, bf16[3,128,128]{2,1,0:T(8,128)(2,1)S(1)}, u32[]{:S(2)}, u32[]{:S(2)}) %collective-permute-start.15) | collective-permute-done | bytes 98336 | tf_op jit(solution)/shard_map/ppermute | solution.py:539
  58.6 0.0 copy-done
  58.6 1.2 %project.1 = (f32[128,1024]{1,0:T(8,128)S(1)}, bf16[128,1024]{1,0:T(8,128)(2,1)S(1)}) custom-call(bf16[3,128,128]{2,1,0:T(8,128)(2,1)S(1)} %get-tuple-element.65.own, bf16[3,128,128]{2,1,0:T(8,128)(2,1)S(1)} %collective-permute-done.13.by_x, bf16[3,128,128]{2,1,0:T(8,128)(2,1)S(1)} %collective-permute-done.14.by_zl, ...), custom_call_target="tpu_custom_call" | custom-call | tf_op jit(solution)/shard_map/project/pallas_call | solution.py:587
  59.8 0.1 collective-permute-start.17
  59.9 0.0 copy-done.5
  59.9 0.0 copy-done.6
  59.9 0.2 place.1
  60.1 1.4 %collective-permute-done.18.refs_7_ = bf16[256,512]{1,0:T(8,128)(2,1)S(1)} collective-permute-done((bf16[256,512]{1,0:T(8,128)(2,1)S(1)}, bf16[256,512]{1,0:T(8,128)(2,1)S(1)}, u32[]{:S(2)}, u32[]{:S(2)}) %collective-permute-start.18) | collective-permute-done | bytes 262176 | tf_op jit(solution)/shard_map/ppermute | solution.py:539
  61.5 0.0 collective-permute-done.17.other
  61.5 0.0 copy-done.1
  61.5 0.6 pack.1
  62.1 20.0 %all_to_all.5.got = bf16[16,112,128]{2,1,0:T(8,128)(2,1)S(1)} all-to-all(bf16[16,112,128]{2,1,0:T(8,128)(2,1)S(1)} %pack.1), channel_id=1, replica_groups=mesh['ctx'=16,'head'=2] {'ctx'}, dimensions={0} | all-to-all | bytes 917504 | tf_op jit(solution)/shard_map/all_to_all | solution.py:616
  82.1 0.1 collective-permute-start.19
  82.2 1.3 %collective-permute-done.19.other = bf16[16,32,128]{2,1,0:T(8,128)(2,1)S(1)} collective-permute-done((bf16[16,32,128]{2,1,0:T(8,128)(2,1)S(1)}, bf16[16,32,128]{2,1,0:T(8,128)(2,1)S(1)}, u32[]{:S(2)}, u32[]{:S(2)}) %collective-permute-start.19) | collective-permute-done | bytes 131104 | tf_op jit(solution)/shard_map/ppermute | solution.py:617
  83.5 0.0 copy-done.2
  83.5 0.0 copy-done.3
  83.5 0.0 copy-done.4
  83.5 2.6 %finish.1 = (f32[64,512]{1,0:T(8,128)}, f32[256,512]{1,0:T(8,128)}, f32[256,512]{1,0:T(8,128)}, f32[256,512]{1,0:T(8,128)}) custom-call(bf16[16,112,128]{2,1,0:T(8,128)(2,1)S(1)} %all_to_all.5.got, bf16[16,32,128]{2,1,0:T(8,128)(2,1)S(1)} %collective-permute-done.19.other, bf16[256,512]{1,0:T(8,128)(2,1)S(1)} %constant_dynamic-update-slice_fusion.refs_0_, ...), custom_call_target="tpu_custom_call" | custom-call | tf_op jit(solution)/shard_map/finish/pallas_call | solution.py:620
  (5 shorter events, 0.1 us)
Async XLA Ops:
  3.5 13.3 %collective-permute-start = (bf16[544,128]{1,0:T(8,128)(2,1)}, bf16[544,128]{1,0:T(8,128)(2,1)S(1)}, u32[]{:S(2)}, u32[]{:S(2)}) collective-permute-start(bf16[544,128]{1,0:T(8,128)(2,1)} %get-tuple-element.46), channel_id=1, source_target_pairs={{0,2},{2,0},{4,6},{6,4},{8,10},{10,8},{12,14},{14,12},{16,18},{18,... | collective-permute-start | bytes 417800 | tf_op jit(solution)/shard_map/ppermute | solution.py:539
  6.5 10.3 %collective-permute-start.1 = (bf16[544,128]{1,0:T(8,128)(2,1)}, bf16[544,128]{1,0:T(8,128)(2,1)S(1)}, u32[]{:S(2)}, u32[]{:S(2)}) collective-permute-start(bf16[544,128]{1,0:T(8,128)(2,1)} %get-tuple-element.47), channel_id=1, source_target_pairs={{0,8},{2,10},{4,12},{6,14},{8,0},{10,2},{12,4},{14,6},{16,24},{18,... | collective-permute-start | bytes 417800 | tf_op jit(solution)/shard_map/ppermute | solution.py:539
  8.1 9.4 %collective-permute-start.2 = (bf16[544,128]{1,0:T(8,128)(2,1)}, bf16[544,128]{1,0:T(8,128)(2,1)S(1)}, u32[]{:S(2)}, u32[]{:S(2)}) collective-permute-start(bf16[544,128]{1,0:T(8,128)(2,1)} %get-tuple-element.48), channel_id=1, source_target_pairs={{0,10},{2,8},{4,14},{6,12},{8,2},{10,0},{12,6},{14,4},{16,26},{18,... | collective-permute-start | bytes 417800 | tf_op jit(solution)/shard_map/ppermute | solution.py:539
  8.1 8.8 %collective-permute-start.3 = (bf16[128,512]{1,0:T(8,128)(2,1)}, bf16[128,512]{1,0:T(8,128)(2,1)S(1)}, u32[]{:S(2)}, u32[]{:S(2)}) collective-permute-start(bf16[128,512]{1,0:T(8,128)(2,1)} %get-tuple-element.49), channel_id=1, source_target_pairs={{0,16},{2,18},{4,20},{6,22},{8,24},{10,26},{12,28},{14,30},{16,0},... | collective-permute-start | bytes 393224 | tf_op jit(solution)/shard_map/ppermute | solution.py:539
  18.5 10.9 %collective-permute-start.4 = (bf16[4,272,128]{2,1,0:T(8,128)(2,1)S(1)}, bf16[4,272,128]{2,1,0:T(8,128)(2,1)S(1)}, u32[]{:S(2)}, u32[]{:S(2)}) collective-permute-start(bf16[4,272,128]{2,1,0:T(8,128)(2,1)S(1)} %pad_maximum_fusion.near_own), channel_id=1, source_target_pairs={{0,4},{2,6},{4,0},{6,2},{8,12},{10,14},{12,8},{14,10},{16,20},{18,... | collective-permute-start | bytes 835592 | tf_op jit(solution)/shard_map/ppermute | solution.py:548
  20.3 10.2 %collective-permute-start.5 = (bf16[4,272,128]{2,1,0:T(8,128)(2,1)S(1)}, bf16[4,272,128]{2,1,0:T(8,128)(2,1)S(1)}, u32[]{:S(2)}, u32[]{:S(2)}) collective-permute-start(bf16[4,272,128]{2,1,0:T(8,128)(2,1)S(1)} %pad_maximum_fusion.1.far_own), channel_id=1, source_target_pairs={{0,16},{2,18},{4,20},{6,22},{8,24},{10,26},{12,28},{14,30},{17,1},... | collective-permute-start | bytes 835592 | tf_op jit(solution)/shard_map/ppermute | solution.py:547
  25.6 33.0 %copy-start = (bf16[3,1024,512]{2,1,0:T(8,128)(2,1)S(1)}, bf16[3,1024,512]{2,1,0:T(8,128)(2,1)}, u32[]{:S(2)}) copy-start(bf16[3,1024,512]{2,1,0:T(8,128)(2,1)} %weight.1) | copy-start | bytes 9437188
  25.7 7.7 %collective-permute-start.8 = (bf16[256,512]{1,0:T(8,128)(2,1)S(1)}, bf16[256,512]{1,0:T(8,128)(2,1)S(1)}, u32[]{:S(2)}, u32[]{:S(2)}) collective-permute-start(bf16[256,512]{1,0:T(8,128)(2,1)S(1)} %constant_dynamic-update-slice_fusion.refs_0_), channel_id=1, source_target_pairs={{0,4},{2,6},{4,0},{6,2},{8,12},{10,14},{12,8},{14,10},{16,20},{18,... | collective-permute-start | bytes 786440 | tf_op jit(solution)/shard_map/ppermute | solution.py:539
  26.2 7.1 %collective-permute-start.7 = (bf16[256,512]{1,0:T(8,128)(2,1)S(1)}, bf16[256,512]{1,0:T(8,128)(2,1)S(1)}, u32[]{:S(2)}, u32[]{:S(2)}) collective-permute-start(bf16[256,512]{1,0:T(8,128)(2,1)S(1)} %constant_dynamic-update-slice_fusion.refs_0_), channel_id=1, source_target_pairs={{0,2},{2,0},{4,6},{6,4},{8,10},{10,8},{12,14},{14,12},{16,18},{18,... | collective-permute-start | bytes 786440 | tf_op jit(solution)/shard_map/ppermute | solution.py:539
  26.8 6.9 %collective-permute-start.6 = (bf16[256,512]{1,0:T(8,128)(2,1)S(1)}, bf16[256,512]{1,0:T(8,128)(2,1)S(1)}, u32[]{:S(2)}, u32[]{:S(2)}) collective-permute-start(bf16[256,512]{1,0:T(8,128)(2,1)S(1)} %constant_dynamic-update-slice_fusion.refs_0_), channel_id=1, source_target_pairs={{0,8},{2,10},{4,12},{6,14},{8,0},{10,2},{12,4},{14,6},{16,24},{18,... | collective-permute-start | bytes 786440 | tf_op jit(solution)/shard_map/ppermute | solution.py:539
  33.3 26.6 %copy-start.5 = (s32[128,1]{0,1:T(1,128)S(1)}, s32[128,1]{0,1:T(1,128)}, u32[]{:S(2)}) copy-start(s32[128,1]{0,1:T(1,128)} %param.19) | copy-start | bytes 1540
  33.3 26.6 %copy-start.6 = (s32[128]{0:T(128)S(1)}, s32[128]{0:T(128)}, u32[]{:S(2)}) copy-start(s32[128]{0:T(128)} %param.20) | copy-start | bytes 1540
  33.3 28.2 %copy-start.1 = (bf16[1024,512]{1,0:T(8,128)(2,1)S(1)}, bf16[1024,512]{1,0:T(8,128)(2,1)}, u32[]{:S(2)}) copy-start(bf16[1024,512]{1,0:T(8,128)(2,1)} %adapter.1) | copy-start | bytes 3145732
  33.7 7.3 %collective-permute-start.9 = (bf16[4,2,128,128]{3,2,1,0:T(8,128)(2,1)S(1)}, bf16[4,2,128,128]{3,2,1,0:T(8,128)(2,1)S(1)}, u32[]{:S(2)}, u32[]{:S(2)}) collective-permute-start(bf16[4,2,128,128]{3,2,1,0:T(8,128)(2,1)S(1)} %get-tuple-element.58), channel_id=1, source_target_pairs={{0,4},{2,6},{4,0},{6,2},{8,12},{10,14},{12,8},{14,10},{16,20},{18,... | collective-permute-start | bytes 786440 | tf_op jit(solution)/shard_map/ppermute | solution.py:579
  35.2 14.0 %collective-permute-start.10 = (bf16[4,2,128,128]{3,2,1,0:T(8,128)(2,1)S(1)}, bf16[4,2,128,128]{3,2,1,0:T(8,128)(2,1)S(1)}, u32[]{:S(2)}, u32[]{:S(2)}) collective-permute-start(bf16[4,2,128,128]{3,2,1,0:T(8,128)(2,1)S(1)} %get-tuple-element.59), channel_id=1, source_target_pairs={{16,0},{18,2},{20,4},{22,6},{24,8},{26,10},{28,12},{30,14},{1,17},... | collective-permute-start | bytes 786440 | tf_op jit(solution)/shard_map/ppermute | solution.py:578
  36.5 12.8 %collective-permute-start.12 = (bf16[256,512]{1,0:T(8,128)(2,1)S(1)}, bf16[256,512]{1,0:T(8,128)(2,1)S(1)}, u32[]{:S(2)}, u32[]{:S(2)}) collective-permute-start(bf16[256,512]{1,0:T(8,128)(2,1)S(1)} %collective-permute-done.6.refs_1_), channel_id=1, source_target_pairs={{0,4},{2,6},{4,0},{6,2},{8,12},{10,14},{12,8},{14,10},{16,20},{18,... | collective-permute-start | bytes 786440 | tf_op jit(solution)/shard_map/ppermute | solution.py:539
  37.1 12.2 %collective-permute-start.11 = (bf16[256,512]{1,0:T(8,128)(2,1)S(1)}, bf16[256,512]{1,0:T(8,128)(2,1)S(1)}, u32[]{:S(2)}, u32[]{:S(2)}) collective-permute-start(bf16[256,512]{1,0:T(8,128)(2,1)S(1)} %collective-permute-done.6.refs_1_), channel_id=1, source_target_pairs={{0,2},{2,0},{4,6},{6,4},{8,10},{10,8},{12,14},{14,12},{16,18},{18,... | collective-permute-start | bytes 786440 | tf_op jit(solution)/shard_map/ppermute | solution.py:539
  38.0 15.5 %collective-permute-start.16 = (bf16[256,512]{1,0:T(8,128)(2,1)S(1)}, bf16[256,512]{1,0:T(8,128)(2,1)S(1)}, u32[]{:S(2)}, u32[]{:S(2)}) collective-permute-start(bf16[256,512]{1,0:T(8,128)(2,1)S(1)} %collective-permute-done.7.refs_2_), channel_id=1, source_target_pairs={{0,4},{2,6},{4,0},{6,2},{8,12},{10,14},{12,8},{14,10},{16,20},{18,... | collective-permute-start | bytes 786440 | tf_op jit(solution)/shard_map/ppermute | solution.py:539
  49.3 34.2 %copy-start.2 = (f32[256,512]{1,0:T(8,128)S(1)}, f32[256,512]{1,0:T(8,128)}, u32[]{:S(2)}) copy-start(f32[256,512]{1,0:T(8,128)} %refs_8_.1) | copy-start | bytes 1572868
  49.4 34.2 %copy-start.3 = (f32[256,512]{1,0:T(8,128)S(1)}, f32[256,512]{1,0:T(8,128)}, u32[]{:S(2)}) copy-start(f32[256,512]{1,0:T(8,128)} %refs_9_.1) | copy-start | bytes 1572868
  49.4 34.1 %copy-start.4 = (f32[256,512]{1,0:T(8,128)S(1)}, f32[256,512]{1,0:T(8,128)}, u32[]{:S(2)}) copy-start(f32[256,512]{1,0:T(8,128)} %refs_10_.1) | copy-start | bytes 1572868
  49.4 5.5 %collective-permute-start.13 = (bf16[3,128,128]{2,1,0:T(8,128)(2,1)S(1)}, bf16[3,128,128]{2,1,0:T(8,128)(2,1)S(1)}, u32[]{:S(2)}, u32[]{:S(2)}) collective-permute-start(bf16[3,128,128]{2,1,0:T(8,128)(2,1)S(1)} %get-tuple-element.66), channel_id=1, source_target_pairs={{0,2},{2,0},{4,6},{6,4},{8,10},{10,8},{12,14},{14,12},{16,18},{18,... | collective-permute-start | bytes 294920 | tf_op jit(solution)/shard_map/ppermute | solution.py:539
  50.2 5.6 %collective-permute-start.14 = (bf16[3,128,128]{2,1,0:T(8,128)(2,1)S(1)}, bf16[3,128,128]{2,1,0:T(8,128)(2,1)S(1)}, u32[]{:S(2)}, u32[]{:S(2)}) collective-permute-start(bf16[3,128,128]{2,1,0:T(8,128)(2,1)S(1)} %get-tuple-element.67), channel_id=1, source_target_pairs={{0,8},{2,10},{4,12},{6,14},{8,0},{10,2},{12,4},{14,6},{16,24},{18,... | collective-permute-start | bytes 294920 | tf_op jit(solution)/shard_map/ppermute | solution.py:539
  50.7 7.9 %collective-permute-start.15 = (bf16[3,128,128]{2,1,0:T(8,128)(2,1)S(1)}, bf16[3,128,128]{2,1,0:T(8,128)(2,1)S(1)}, u32[]{:S(2)}, u32[]{:S(2)}) collective-permute-start(bf16[3,128,128]{2,1,0:T(8,128)(2,1)S(1)} %get-tuple-element.68), channel_id=1, source_target_pairs={{0,10},{2,8},{4,14},{6,12},{8,2},{10,0},{12,6},{14,4},{16,26},{18,... | collective-permute-start | bytes 294920 | tf_op jit(solution)/shard_map/ppermute | solution.py:539
  52.9 8.6 %collective-permute-start.18 = (bf16[256,512]{1,0:T(8,128)(2,1)S(1)}, bf16[256,512]{1,0:T(8,128)(2,1)S(1)}, u32[]{:S(2)}, u32[]{:S(2)}) collective-permute-start(bf16[256,512]{1,0:T(8,128)(2,1)S(1)} %collective-permute-done.11.refs_3_), channel_id=1, source_target_pairs={{0,4},{2,6},{4,0},{6,2},{8,12},{10,14},{12,8},{14,10},{16,20},{18,... | collective-permute-start | bytes 786440 | tf_op jit(solution)/shard_map/ppermute | solution.py:539
  59.8 1.7 %collective-permute-start.17 = (bf16[128,1024]{1,0:T(8,128)(2,1)S(1)}, bf16[128,1024]{1,0:T(8,128)(2,1)S(1)}, u32[]{:S(2)}, u32[]{:S(2)}) collective-permute-start(bf16[128,1024]{1,0:T(8,128)(2,1)S(1)} %get-tuple-element.75), channel_id=1, source_target_pairs={{0,1},{1,0},{2,3},{3,2},{4,5},{5,4},{6,7},{7,6},{8,9},{9,8},{10,11... | collective-permute-start | bytes 786440 | tf_op jit(solution)/shard_map/ppermute | solution.py:603
  82.1 1.4 %collective-permute-start.19 = (bf16[16,32,128]{2,1,0:T(8,128)(2,1)S(1)}, bf16[16,32,128]{2,1,0:T(8,128)(2,1)S(1)}, u32[]{:S(2)}, u32[]{:S(2)}) collective-permute-start(bf16[16,32,128]{2,1,0:T(8,128)(2,1)S(1)} %slice.36), channel_id=1, source_target_pairs={{0,1},{1,0},{2,3},{3,2},{4,5},{5,4},{6,7},{7,6},{8,9},{9,8},{10,11... | collective-permute-start | bytes 393224 | tf_op jit(solution)/shard_map/ppermute | solution.py:617

commit v3 on v2

--- a/solution.py
+++ b/solution.py
@@ -286,102 +286,134 @@
         copies(gives, asks, 1)
 
 
-def attend_body(
-    scale, seq_len, near_own, far_own, near_in, far_in, keep, near_out, far_out, near_1, near_2, far_1, far_2, near_1_sum, near_2_sum, far_1_sum, far_2_sum
-):
-    core, me = lax.axis_index("head"), lax.axis_index("ctx")
+def gather_body(own, rows_1, by_x, by_zl, by_both, rows_2, far, near, two):
+    for flip, part in enumerate((own, by_x, by_zl, by_both)):
+        near[flip] = part[:PART, :]
+        far[flip] = part[PART:, :]
+    count = rows_1.shape[0]
+    two[:count, :] = rows_1[...]
+    two[count:, :] = rows_2[...]
+
+
+def lower_of(meta):
+    meta = meta.astype(F32)
+    return (meta[0:1] * BLOCK + meta[1:2]).astype(jnp.int32)
+
+
+def attend(scale, role_q, crossing, nears, far, far_1, far_2, near_1_sum, near_2_sum, put_far_1, put_far_2):
+    me = lax.axis_index("ctx")
     zh, y = me // 8, me // 2 % 2
     spots = [jnp.bitwise_xor(spot_of(me), flip) for flip in range(4)]
     places = [spot // 2 * 4 + spot % 2 for spot in spots]
-    wide = 4 * BLOCK
-
-    def lower_of(meta):
-        meta = meta.astype(F32)
-        return (meta[0:1] * BLOCK + meta[1:2]).astype(jnp.int32)
-
-    for side, (near, far) in enumerate(((near_own, far_own), (near_in, far_in))):
-        for spot in range(4):
-            rows = slice(spot * BLOCK, (spot + 1) * BLOCK)
-            place = slice((4 * side + spot) * BLOCK, (4 * side + spot + 1) * BLOCK)
-            near_1[place, :] = near[spot, :BLOCK, :]
-            near_2[place, :] = near[spot, BLOCK:PAIR, :]
-            far_1[side, rows, :] = far[spot, :BLOCK, :]
-            far_2[side, rows, :] = far[spot, BLOCK:PAIR, :]
-    near_1_sum[...] = jnp.zeros_like(near_1_sum)
-    near_2_sum[...] = jnp.zeros_like(near_2_sum)
     lane = lax.broadcasted_iota(jnp.int32, (1, BLOCK), 1)
-    row_in = lax.broadcasted_iota(jnp.int32, (BLOCK, wide), 0)
-    grad_scale = scale * 0.5 / seq_len
+    row_in = lax.broadcasted_iota(jnp.int32, (BLOCK, 4 * BLOCK), 0)
     never = 1 << 20
-
-    def work(role_q, side, carry):
-        far_zh = jnp.where(side == 0, zh, 1 - zh)
-        place = jnp.concatenate([lane + (far_zh * 8 + y * 2 + s) * BLOCK for s in places], axis=1)
-        base_1, base_2 = far_1[side], far_2[side]
+    far_zh = 1 - zh if crossing else zh
+    place = jnp.concatenate([lane + (far_zh * 8 + y * 2 + s) * BLOCK for s in places], axis=1)
+    base_1, base_2 = far_1[...], far_2[...]
+    if not role_q:
+        low = jnp.concatenate([lower_of(far[s, PAIR:PART, :]) for s in range(4)], axis=1)
+    dscores, weights, firsts, seconds = [], [], [], []
+    for chunk in range(4):
+        rows = slice(chunk * PAIR, (chunk + 1) * PAIR)
+        near_ref, near_y = nears[chunk // 2], (y, 1 - y)[chunk // 2]
+        pair = (chunk % 2 * 2, chunk % 2 * 2 + 1)
+        first = jnp.concatenate([near_ref[s, :BLOCK, :] for s in pair], axis=0)
+        second = jnp.concatenate([near_ref[s, BLOCK:PAIR, :] for s in pair], axis=0)
+        half = dot(first, base_1, 1, 1) * (0.5 * scale)
+        dprod = dot(second, base_2, 1, 1)
+        seen = []
+        for s in pair:
+            start = (zh * 8 + near_y * 2 + places[s]) * BLOCK
+            if role_q:
+                low = jnp.concatenate([lower_of(near_ref[s, PAIR:PART, :])] * 4, axis=1)
+                seen.append(row_in >= jnp.where(place >= low, place - start, never))
+            else:
+                seen.append((row_in >= low - start) & (row_in <= place - start))
+        seen = jnp.concatenate(seen, axis=0)
+        tanh = jnp.tanh(half)
+        twice = 1.0 + tanh
+        weight = half * twice
+        dscore = (dprod * twice) * (1.0 + half * (1.0 - tanh))
+        weight = jnp.where(seen, weight, 0.0).astype(BF16)
+        dscore = jnp.where(seen, dscore, 0.0).astype(BF16)
+        grad_1 = dot(dscore, base_1, 1, 0)
+        near_1_sum[rows, :] = near_1_sum[rows, :] + grad_1 if crossing else grad_1
         if not role_q:
-            own = jnp.concatenate([lower_of(far_own[s, PAIR:PART, :]) for s in range(4)], axis=1)
-            other = jnp.concatenate([lower_of(far_in[s, PAIR:PART, :]) for s in range(4)], axis=1)
-            low = jnp.where(side == 0, own, other)
-        dscores, weights = [], []
-        for chunk in range(4):
-            rows = slice(chunk * PAIR, (chunk + 1) * PAIR)
-            half = dot(near_1[rows, :], base_1, 1, 1) * (0.5 * scale)
-            dprod = dot(near_2[rows, :], base_2, 1, 1)
-            near_ref, near_y = (near_own, y) if chunk < 2 else (near_in, 1 - y)
-            seen = []
-            for at in range(2):
-                start = (zh * 8 + near_y * 2 + places[chunk % 2 * 2 + at]) * BLOCK
-                if role_q:
-                    low = jnp.concatenate([lower_of(near_ref[chunk % 2 * 2 + at, PAIR:PART, :])] * 4, axis=1)
-                    seen.append(row_in >= jnp.where(place >= low, place - start, never))
-                else:
-                    seen.append((row_in >= low - start) & (row_in <= place - start))
-            seen = jnp.concatenate(seen, axis=0)
-            tanh = jnp.tanh(half)
-            twice = 1.0 + tanh
-            weight = half * twice
-            dscore = (dprod * twice) * (1.0 + half * (1.0 - tanh))
-            weight = jnp.where(seen, weight, 0.0).astype(BF16)
-            dscore = jnp.where(seen, dscore, 0.0).astype(BF16)
-            near_1_sum[rows, :] += dot(dscore, base_1, 1, 0)
-            if not role_q:
-                near_2_sum[rows, :] += dot(weight, base_2, 1, 0)
-            dscores.append(dscore)
-            weights.append(weight)
-        far_1_sum[side] = dot(jnp.concatenate(dscores, axis=0), near_1[...], 0, 0)
-        if role_q:
-            far_2_sum[side] = dot(jnp.concatenate(weights, axis=0), near_2[...], 0, 0)
-        return carry
-
+            grad_2 = dot(weight, base_2, 1, 0)
+            near_2_sum[rows, :] = near_2_sum[rows, :] + grad_2 if crossing else grad_2
+        dscores.append(dscore)
+        weights.append(weight)
+        firsts.append(first)
+        seconds.append(second)
+    put_far_1(dot(jnp.concatenate(dscores, axis=0), jnp.concatenate(firsts, axis=0), 0, 0))
+    if role_q:
+        put_far_2(dot(jnp.concatenate(weights, axis=0), jnp.concatenate(seconds, axis=0), 0, 0))
+
+
+def gather_far(far, far_1, far_2):
     for spot in range(4):
-        far_out[spot] = jnp.zeros((2, BLOCK, BLOCK), BF16)
+        rows = slice(spot * BLOCK, (spot + 1) * BLOCK)
+        far_1[rows, :] = far[spot, :BLOCK, :]
+        far_2[rows, :] = far[spot, BLOCK:PAIR, :]
+
+
+def attend_own_body(scale, near_own, far_own, near_in, near_1_sum, near_2_sum, far_sum, far_1, far_2):
+    gather_far(far_own, far_1, far_2)
+    core = lax.axis_index("head")
+
+    def put(at):
+        def store(value):
+            far_sum[at] = value
+
+        return store
+
+    rest = ((near_own, near_in), far_own, far_1, far_2, near_1_sum, near_2_sum, put(0), put(1))
 
     @pl.when(core == 0)
     def _():
-        lax.fori_loop(0, 1 + zh, functools.partial(work, True), 0)
-        for spot in range(4):
-            far_rows = slice(spot * BLOCK, (spot + 1) * BLOCK)
-            keep[spot, 1] = far_2_sum[0, far_rows] * (1.0 / seq_len)
-            far_out[spot, 1] = (far_2_sum[1, far_rows] * (1.0 / seq_len)).astype(BF16)
+        near_2_sum[...] = jnp.zeros_like(near_2_sum)
+        attend(scale, True, False, *rest)
 
     @pl.when(core == 1)
     def _():
-        lax.fori_loop(0, 2 - zh, functools.partial(work, False), 0)
-        for spot in range(4):
-            rows = slice(spot * BLOCK, (spot + 1) * BLOCK)
-            keep[spot, 1] = near_2_sum[rows, :] * (1.0 / seq_len)
-
+        far_sum[1] = jnp.zeros((4 * BLOCK, BLOCK), F32)
+        attend(scale, False, False, *rest)
+
+
+def attend_far_body(scale, seq_len, near_own, near_in, far_in, _1, _2, near_1_sum, near_2_sum, far_out, far_1, far_2):
+    core, zh = lax.axis_index("head"), lax.axis_index("ctx") // 8
+    far_out[...] = jnp.zeros_like(far_out)
+
+    def put(at, factor):
+        def store(value):
+            for spot in range(4):
+                far_out[spot, at] = (value[spot * BLOCK : (spot + 1) * BLOCK] * factor).astype(BF16)
+
+        return store
+
+    puts = (put(0, scale * 0.5 / seq_len), put(1, 1.0 / seq_len))
+    rest = ((near_own, near_in), far_in, far_1, far_2, near_1_sum, near_2_sum, *puts)
+
+    @pl.when((core == 0) & (zh == 1))
+    def _():
+        gather_far(far_in, far_1, far_2)
+        attend(scale, True, True, *rest)
+
+    @pl.when((core == 1) & (zh == 0))
+    def _():
+        gather_far(far_in, far_1, far_2)
+        attend(scale, False, True, *rest)
+
+
+def near_body(scale, seq_len, near_1_sum, near_2_sum, out):
     for spot in range(4):
-        rows = slice(spot * BLOCK, (spot + 1) * BLOCK)
-        other = slice((4 + spot) * BLOCK, (5 + spot) * BLOCK)
-        keep[spot, 0] = near_1_sum[rows, :] * grad_scale
-        near_out[spot, 0] = (near_1_sum[other, :] * grad_scale).astype(BF16)
-        near_out[spot, 1] = (near_2_sum[other, :] * (1.0 / seq_len)).astype(BF16)
-        keep[spot, 2] = far_1_sum[0, rows] * grad_scale
-        far_out[spot, 0] = (far_1_sum[1, rows] * grad_scale).astype(BF16)
-
-
-def project_body(own, by_x, by_zl, by_both, weight, partial, sent, held):
+        rows = slice((4 + spot) * BLOCK, (5 + spot) * BLOCK)
+        out[spot, 0] = (near_1_sum[rows, :] * (scale * 0.5 / seq_len)).astype(BF16)
+        out[spot, 1] = (near_2_sum[rows, :] * (1.0 / seq_len)).astype(BF16)
+
+
+def project_body(by_both, by_zl, by_x, own, weight, partial, sent, held):
     core, me = lax.axis_index("head"), lax.axis_index("ctx")
     for flip, part in enumerate((own, by_x, by_zl, by_both)):
         head = jnp.bitwise_xor(spot_of(me), flip)
@@ -435,11 +467,14 @@
     marks[...] = jnp.transpose(mark).astype(BF16)
 
 
-def merge_body(keep, near, far, *outs):
-    for at, out in enumerate(outs):
-        out[0] = (keep[at, 0] + near[at, 0].astype(F32)).astype(BF16)
-        out[1] = (keep[at, 1] + near[at, 1].astype(F32) + far[at, 1].astype(F32)).astype(BF16)
-        out[2] = (keep[at, 2] + far[at, 0].astype(F32)).astype(BF16)
+def merge_body(flips, scale, seq_len, far, near, near_1_sum, near_2_sum, far_sum, *outs):
+    grad_scale, weight_scale = scale * 0.5 / seq_len, 1.0 / seq_len
+    for flip, out in zip(flips, outs):
+        rows = slice(flip * BLOCK, (flip + 1) * BLOCK)
+        out[0] = (near_1_sum[rows, :] * grad_scale + near[flip, 0].astype(F32)).astype(BF16)
+        both = (near_2_sum[rows, :] + far_sum[1, rows, :]) * weight_scale
+        out[1] = (both + near[flip, 1].astype(F32) + far[flip, 1].astype(F32)).astype(BF16)
+        out[2] = (far_sum[0, rows, :] * grad_scale + far[flip, 0].astype(F32)).astype(BF16)
 
 
 def finish_body(got, other, *refs):
@@ -528,10 +563,10 @@
     *dealt, own_rows = pl.pallas_call(
         deal_body,
         out_shape=(dealt,) * 4 + (shape((rows_here, head_cols), BF16),),
-        in_specs=[SMEM] + [pl.BlockSpec(memory_space=pl.ANY)] * 4,
+        in_specs=[SMEM] + [pl.BlockSpec(memory_space=pltpu.HBM)] * 4,
         out_specs=(VMEM,) * 5,
         scratch_shapes=[pltpu.SemaphoreType.DMA((17,))],
-        compiler_params=pltpu.CompilerParams(vmem_limit_bytes=56 * 1024 * 1024),
+        compiler_params=pltpu.CompilerParams(vmem_limit_bytes=12 * 1024 * 1024),
         name="deal",
     )(starts, queries, keys_values, attn_cot, event_rows)
 
@@ -539,51 +574,61 @@
         return lax.ppermute(sent, "ctx", [(i, i ^ bit) for i in range(16)])
 
     zh_rows = exchange(own_rows, ROUNDS[0])
-    parts = dealt[:1] + [exchange(part, bit) for part, bit in zip(dealt[1:], (1, 4, 5))]
-    *parts, zh_rows = lax.optimization_barrier((*parts, zh_rows))
-    two = jnp.concatenate([own_rows, zh_rows], axis=0)
-    near_own = jnp.stack([part[:PART] for part in parts])
-    far_own = jnp.stack([part[PART:] for part in parts])
+    both, by_zl, by_x = [exchange(part, bit) for part, bit in zip(dealt[:0:-1], (5, 4, 1))]
+    zh_rows, both, by_zl, by_x = lax.optimization_barrier((zh_rows, both, by_zl, by_x))
+    far_own, near_own, two = kernel_call(
+        gather_body,
+        (shape((4, PART, BLOCK), BF16),) * 2 + (shape((2 * rows_here, head_cols), BF16),),
+        (dealt[0], own_rows, by_x, by_zl, both, zh_rows),
+        "gather",
+    )
     far_in = lax.ppermute(far_own, ("ctx", "head"), FAR_OUT)
     near_in = lax.ppermute(near_own, "ctx", ACROSS_Y)
     zl_rows, x_rows, y_rows = [exchange(two, bit) for bit in ROUNDS[1:]]
-    keep, near_out, far_out = pl.pallas_call(
-        functools.partial(attend_body, 1.0 / math.sqrt(HD), float(seq_len)),
-        out_shape=(
-            shape((4, 3, BLOCK, BLOCK), F32),
-            shape((4, 2, BLOCK, BLOCK), BF16),
-            shape((4, 2, BLOCK, BLOCK), BF16),
-        ),
-        in_specs=[VMEM] * 4,
-        out_specs=(VMEM, VMEM, VMEM),
-        scratch_shapes=[
-            pltpu.VMEM((8 * BLOCK, BLOCK), BF16),
-            pltpu.VMEM((8 * BLOCK, BLOCK), BF16),
-            pltpu.VMEM((2, 4 * BLOCK, BLOCK), BF16),
-            pltpu.VMEM((2, 4 * BLOCK, BLOCK), BF16),
-            pltpu.VMEM((8 * BLOCK, BLOCK), F32),
-            pltpu.VMEM((8 * BLOCK, BLOCK), F32),
-            pltpu.VMEM((2, 4 * BLOCK, BLOCK), F32),
-            pltpu.VMEM((2, 4 * BLOCK, BLOCK), F32),
-        ],
+    scales = (1.0 / math.sqrt(HD), float(seq_len))
+    side_scratch = [pltpu.VMEM((4 * BLOCK, BLOCK), BF16)] * 2
+    near_sum = shape((8 * BLOCK, BLOCK), F32)
+    cost = pl.CostEstimate(flops=10**9, bytes_accessed=2**20, transcendentals=0)
+    near_1, near_2, far_sum = pl.pallas_call(
+        functools.partial(attend_own_body, scales[0]),
+        out_shape=(near_sum, near_sum, shape((2, 4 * BLOCK, BLOCK), F32)),
+        in_specs=[VMEM] * 3,
+        out_specs=(VMEM,) * 3,
+        scratch_shapes=side_scratch,
         compiler_params=pltpu.CompilerParams(vmem_limit_bytes=12 * 1024 * 1024),
-        cost_estimate=pl.CostEstimate(flops=2 * 10**9, bytes_accessed=2**21, transcendentals=0),
-        name="attend",
-    )(near_own, far_own, near_in, far_in)
-    near_out, far_out, zl_rows, x_rows, y_rows = lax.optimization_barrier(
-        (near_out, far_out, zl_rows, x_rows, y_rows)
+        cost_estimate=cost,
+        name="attend_own",
+    )(near_own, far_own, near_in)
+    near_1, near_2, far_out = pl.pallas_call(
+        functools.partial(attend_far_body, *scales),
+        out_shape=(near_sum, near_sum, shape((4, 2, BLOCK, BLOCK), BF16)),
+        in_specs=[VMEM] * 5,
+        out_specs=(VMEM,) * 3,
+        scratch_shapes=side_scratch,
+        input_output_aliases={3: 0, 4: 1},
+        compiler_params=pltpu.CompilerParams(vmem_limit_bytes=12 * 1024 * 1024),
+        cost_estimate=cost,
+        name="attend_far",
+    )(near_own, near_in, far_in, near_1, near_2)
+    near_1, near_2, far_out, zl_rows, x_rows, y_rows = lax.optimization_barrier(
+        (near_1, near_2, far_out, zl_rows, x_rows, y_rows)
+    )
+    near_out = kernel_call(
+        functools.partial(near_body, *scales), shape((4, 2, BLOCK, BLOCK), BF16), (near_1, near_2), "near"
     )
     zl_x_rows = exchange(zl_rows, ROUNDS[2])
     zl_y_rows = exchange(zl_rows, ROUNDS[3])
     far_back = lax.ppermute(far_out, ("ctx", "head"), FAR_BACK)
     near_back = lax.ppermute(near_out, "ctx", ACROSS_Y)
-    own, *parts = kernel_call(
-        merge_body, (shape((3, BLOCK, BLOCK), BF16),) * 4, (keep, near_back, far_back), "merge"
-    )
-    own, *parts, zl_x_rows, zl_y_rows = lax.optimization_barrier((own, *parts, zl_x_rows, zl_y_rows))
+    sums = (far_back, near_back, near_1, near_2, far_sum)
+    part = shape((3, BLOCK, BLOCK), BF16)
+    (both,) = kernel_call(functools.partial(merge_body, (3,), *scales), (part,), sums, "merge_both")
+    both, *sums = lax.optimization_barrier((both, *sums))
+    own, *parts = kernel_call(functools.partial(merge_body, (0, 1, 2), *scales), (part,) * 3, sums, "merge")
+    both, *parts, zl_x_rows, zl_y_rows = lax.optimization_barrier((both, *parts, zl_x_rows, zl_y_rows))
     x_y_rows, zl_x_y_rows = [exchange(rows, ROUNDS[3]) for rows in (x_rows, zl_x_rows)]
-    parts = [exchange(part, bit) for part, bit in zip(parts, (1, 4, 5))]
-    *parts, x_y_rows = lax.optimization_barrier((*parts, x_y_rows))
+    both, by_zl, by_x = [exchange(part, bit) for part, bit in zip((both, parts[1], parts[0]), (5, 4, 1))]
+    both, by_zl, by_x, x_y_rows = lax.optimization_barrier((both, by_zl, by_x, x_y_rows))
     partial, sent = pl.pallas_call(
         project_body,
         out_shape=(shape((rows_here, width), F32), shape((rows_here, width), BF16)),
@@ -592,7 +637,7 @@
         scratch_shapes=[pltpu.VMEM((3, rows_here, queries.shape[1]), BF16)],
         compiler_params=pltpu.CompilerParams(vmem_limit_bytes=12 * 1024 * 1024),
         name="project",
-    )(own, *parts, qkv_weight)
+    )(both, by_zl, by_x, own, qkv_weight)
     sent, owners, slots = lax.optimization_barrier((sent, owners, slots))
     placing, marks = kernel_call(
         place_body,

time: 86.4 us -> 84.2 us (0.975)
  waiting for transfers between devices: 25.4 us -> 22.3 us
  Pallas kernels: 9.62 us -> 7.6 us
  local copies, waits for them, and re-layouts: 1.94 us -> 3.75 us
  blocking collectives: 20 us -> 21.4 us
    unnamed x15 -> x22, local copies, waits for them, and re-layouts: 0.96 us -> 3.74 us
    ppermute x1, waiting for transfers between devices: 8.23 us -> 6.1 us  [dealt_device(): far_back = lax.ppermute(far_out, ('ctx', 'head'), FAR_BACK)]
    pallas_call x1, Pallas kernels: 2.21 us -> 0.32 us  [dealt_device(): pl.pallas_call(deal_body, out_shape=(dealt,) * 4 + (shape((rows_here, hea...]
    all_to_all x1, blocking collectives: 20 us -> 21.4 us  [dealt_device(): got = lax.all_to_all(packed, 'ctx', 0, 0, tiled=True)]
    ppermute x1, waiting for transfers between devices: 1.11 us -> 0.01 us  [dealt_device(): far_in = lax.ppermute(far_own, ('ctx', 'head'), FAR_OUT)]
    another operation x2 -> x0, local copies, waits for them, and re-layouts: 0.96 us -> none  [dealt_device(): far_own = jnp.stack([part[PART:] for part in parts])]
    ppermute x1, starting transfers between devices: 1.52 us -> 0.57 us  [dealt_device(): near_back = lax.ppermute(near_out, 'ctx', ACROSS_Y)]
    pallas_call x1 -> x2, Pallas kernels: 2.81 us -> 2.55 us  [the longest x1 2.51 us: dealt_device(): pl.pallas_call(functools.partial(attend_own_body, scales[0]), out_shape=(...]
  transfers between devices with their start and end apart: 20 -> 20, of which waited for: 11 -> 13; matrix products, arithmetic and copies ran while one was open for 1% -> 0% of each run, Pallas kernels for 5% -> 5%
where the time goes in v3:
time: 84.2 us; the launch traced here: 83.9 us
  starting transfers between devices  27.2 us (32%)
  waiting for transfers between devices  22.3 us (26%)
  blocking collectives  21.4 us (25%)
  Pallas kernels  7.6 us (9%)
  local copies, waits for them, and re-layouts  3.75 us (4%)
  between operations  1.65 us (2%)
    all_to_all x1, blocking collectives, dealt_device(): got = lax.all_to_all(packed, 'ctx', 0, 0, tiled=True)  21.4 us
    ppermute x14, starting transfers between devices, exchange(): return lax.ppermute(sent, 'ctx', [(i, i ^ bit) for i in range(16)])  19 us
    ppermute x14, waiting for transfers between devices, exchange(): return lax.ppermute(sent, 'ctx', [(i, i ^ bit) for i in range(16)])  13.6 us
    ppermute x1, waiting for transfers between devices, dealt_device(): far_back = lax.ppermute(far_out, ('ctx', 'head'), FAR_BACK)  6.1 us
    ppermute x1, starting transfers between devices, dealt_device(): far_in = lax.ppermute(far_own, ('ctx', 'head'), FAR_OUT)  4.5 us
    unnamed x22, local copies, waits for them, and re-layouts  3.74 us
    pallas_call x1, Pallas kernels, dealt_device(): pl.pallas_call(finish_body, out_shape=(shape((width // n_ctx, head_cols),...  2.63 us
    pallas_call x1, Pallas kernels, dealt_device(): pl.pallas_call(functools.partial(attend_own_body, scales[0]), out_shape=(...  2.51 us
  transfers between devices with their start and end apart: 20, of which 13 were waited for; matrix products, arithmetic and copies ran while one was open for 0% of the time, Pallas kernels for 5%

profile of v3, /device:TPU:0, one launch (start us, length us, event | category | flops | bytes accessed | tf_op | source)
XLA Modules:
  0.0 83.9 jit_solution(4355745583231324676)
XLA Ops:
  1.3 0.0 copy-start.5
  1.3 0.9 %copy-done.5 = bf16[2,128,512]{2,1,0:T(8,128)(2,1)S(1)} copy-done((bf16[2,128,512]{2,1,0:T(8,128)(2,1)S(1)}, bf16[2,128,512]{2,1,0:T(8,128)(2,1)}, u32[]{:S(2)}) %copy-start.5) | copy-done | bytes 262168
  2.2 0.9 %copy-done.6 = bf16[128,1024]{1,0:T(8,128)(2,1)S(1)} copy-done((bf16[128,1024]{1,0:T(8,128)(2,1)S(1)}, bf16[128,1024]{1,0:T(8,128)(2,1)}, u32[]{:S(2)}) %copy-start.6) | copy-done | bytes 262168
  3.2 0.9 %copy-done.7 = bf16[128,512]{1,0:T(8,128)(2,1)S(1)} copy-done((bf16[128,512]{1,0:T(8,128)(2,1)S(1)}, bf16[128,512]{1,0:T(8,128)(2,1)}, u32[]{:S(2)}) %copy-start.7) | copy-done | bytes 131096
  4.1 0.9 %copy-done.8 = bf16[128,512]{1,0:T(8,128)(2,1)S(1)} copy-done((bf16[128,512]{1,0:T(8,128)(2,1)S(1)}, bf16[128,512]{1,0:T(8,128)(2,1)}, u32[]{:S(2)}) %copy-start.8) | copy-done | bytes 131096
  5.0 0.3 deal.1
  5.3 4.0 %collective-permute-start.1 = (bf16[544,128]{1,0:T(8,128)(2,1)S(1)}, bf16[544,128]{1,0:T(8,128)(2,1)S(1)}, u32[]{:S(2)}, u32[]{:S(2)}) collective-permute-start(bf16[544,128]{1,0:T(8,128)(2,1)S(1)} %get-tuple-element.57), channel_id=1, source_target_pairs={{0,10},{2,8},{4,14},{6,12},{8,2},{10,0},{12,6},{14,4},{16,26},{18,... | collective-permute-start | bytes 417800 | tf_op jit(solution)/shard_map/ppermute | solution.py:574
  9.3 0.4 collective-permute-start.2
  9.8 0.2 collective-permute-start.3
  10.0 2.9 %collective-permute-start = (bf16[128,512]{1,0:T(8,128)(2,1)S(1)}, bf16[128,512]{1,0:T(8,128)(2,1)S(1)}, u32[]{:S(2)}, u32[]{:S(2)}) collective-permute-start(bf16[128,512]{1,0:T(8,128)(2,1)S(1)} %get-tuple-element.56.rows_1), channel_id=1, source_target_pairs={{0,16},{2,18},{4,20},{6,22},{8,24},{10,26},{12,28},{14,30},{16,0},... | collective-permute-start | bytes 393224 | tf_op jit(solution)/shard_map/ppermute | solution.py:574
  12.9 5.2 %collective-permute-done.rows_2 = bf16[128,512]{1,0:T(8,128)(2,1)S(1)} collective-permute-done((bf16[128,512]{1,0:T(8,128)(2,1)S(1)}, bf16[128,512]{1,0:T(8,128)(2,1)S(1)}, u32[]{:S(2)}, u32[]{:S(2)}) %collective-permute-start) | collective-permute-done | bytes 131104 | tf_op jit(solution)/shard_map/ppermute | solution.py:574
  18.1 0.0 collective-permute-done.1.by_both
  18.1 0.9 %collective-permute-done.2.by_zl = bf16[544,128]{1,0:T(8,128)(2,1)S(1)} collective-permute-done((bf16[544,128]{1,0:T(8,128)(2,1)S(1)}, bf16[544,128]{1,0:T(8,128)(2,1)S(1)}, u32[]{:S(2)}, u32[]{:S(2)}) %collective-permute-start.2) | collective-permute-done | bytes 139296 | tf_op jit(solution)/shard_map/ppermute | solution.py:574
  19.0 0.0 collective-permute-done.3.by_x
  19.0 0.1 gather.1
  19.0 1.6 %collective-permute-start.4 = (bf16[4,272,128]{2,1,0:T(8,128)(2,1)S(1)}, bf16[4,272,128]{2,1,0:T(8,128)(2,1)S(1)}, u32[]{:S(2)}, u32[]{:S(2)}) collective-permute-start(bf16[4,272,128]{2,1,0:T(8,128)(2,1)S(1)} %get-tuple-element.64.near_own), channel_id=1, source_target_pairs={{0,4},{2,6},{4,0},{6,2},{8,12},{10,14},{12,8},{14,10},{16,20},{18,... | collective-permute-start | bytes 835592 | tf_op jit(solution)/shard_map/ppermute | solution.py:586
  20.6 4.5 %collective-permute-start.5 = (bf16[4,272,128]{2,1,0:T(8,128)(2,1)S(1)}, bf16[4,272,128]{2,1,0:T(8,128)(2,1)S(1)}, u32[]{:S(2)}, u32[]{:S(2)}) collective-permute-start(bf16[4,272,128]{2,1,0:T(8,128)(2,1)S(1)} %get-tuple-element.65.far_own), channel_id=1, source_target_pairs={{0,16},{2,18},{4,20},{6,22},{8,24},{10,26},{12,28},{14,30},{17,1},... | collective-permute-start | bytes 835592 | tf_op jit(solution)/shard_map/ppermute | solution.py:585
  25.1 1.7 %collective-permute-start.6 = (bf16[256,512]{1,0:T(8,128)(2,1)S(1)}, bf16[256,512]{1,0:T(8,128)(2,1)S(1)}, u32[]{:S(2)}, u32[]{:S(2)}) collective-permute-start(bf16[256,512]{1,0:T(8,128)(2,1)S(1)} %get-tuple-element.71.refs_0_), channel_id=1, source_target_pairs={{0,8},{2,10},{4,12},{6,14},{8,0},{10,2},{12,4},{14,6},{16,24},{18,... | collective-permute-start | bytes 786440 | tf_op jit(solution)/shard_map/ppermute | solution.py:574
  26.8 1.0 %collective-permute-start.7 = (bf16[256,512]{1,0:T(8,128)(2,1)S(1)}, bf16[256,512]{1,0:T(8,128)(2,1)S(1)}, u32[]{:S(2)}, u32[]{:S(2)}) collective-permute-start(bf16[256,512]{1,0:T(8,128)(2,1)S(1)} %get-tuple-element.71.refs_0_), channel_id=1, source_target_pairs={{0,2},{2,0},{4,6},{6,4},{8,10},{10,8},{12,14},{14,12},{16,18},{18,... | collective-permute-start | bytes 786440 | tf_op jit(solution)/shard_map/ppermute | solution.py:574
  27.8 0.5 collective-permute-start.8
  28.3 0.0 collective-permute-done.4.near_in
  28.3 2.5 %attend_own.1 = (f32[1024,128]{1,0:T(8,128)S(1)}, f32[1024,128]{1,0:T(8,128)S(1)}, f32[2,512,128]{2,1,0:T(8,128)S(1)}) custom-call(bf16[4,272,128]{2,1,0:T(8,128)(2,1)S(1)} %get-tuple-element.64.near_own, bf16[4,272,128]{2,1,0:T(8,128)(2,1)S(1)} %get-tuple-element.65.far_own, bf16[4,272,128]{2,1,0:T(8,128)(2,1)S(1)} %collective-permute-done.4.near_in), custom_call_target="tpu_custom_call" | custom-call | flops 1000000000 | bytes 1048576 | tf_op jit(solution)/shard_map/attend_own/pallas_call | solution.py:592
  30.8 0.0 collective-permute-done.5.far_in
  30.9 0.0 copy-start
  30.9 1.8 %collective-permute-done.6.refs_1_ = bf16[256,512]{1,0:T(8,128)(2,1)S(1)} collective-permute-done((bf16[256,512]{1,0:T(8,128)(2,1)S(1)}, bf16[256,512]{1,0:T(8,128)(2,1)S(1)}, u32[]{:S(2)}, u32[]{:S(2)}) %collective-permute-start.6) | collective-permute-done | bytes 262176 | tf_op jit(solution)/shard_map/ppermute | solution.py:574
  32.7 0.5 collective-permute-done.7.refs_2_
  33.2 1.0 %collective-permute-done.8.refs_4_ = bf16[256,512]{1,0:T(8,128)(2,1)S(1)} collective-permute-done((bf16[256,512]{1,0:T(8,128)(2,1)S(1)}, bf16[256,512]{1,0:T(8,128)(2,1)S(1)}, u32[]{:S(2)}, u32[]{:S(2)}) %collective-permute-start.8) | collective-permute-done | bytes 262176 | tf_op jit(solution)/shard_map/ppermute | solution.py:574
  34.2 0.6 collective-permute-start.10
  34.8 1.5 %collective-permute-start.9 = (bf16[4,2,128,128]{3,2,1,0:T(8,128)(2,1)S(1)}, bf16[4,2,128,128]{3,2,1,0:T(8,128)(2,1)S(1)}, u32[]{:S(2)}, u32[]{:S(2)}) collective-permute-start(bf16[4,2,128,128]{3,2,1,0:T(8,128)(2,1)S(1)} %get-tuple-element.72), channel_id=1, source_target_pairs={{16,0},{18,2},{20,4},{22,6},{24,8},{26,10},{28,12},{30,14},{1,17},... | collective-permute-start | bytes 786440 | tf_op jit(solution)/shard_map/ppermute | solution.py:621
  36.3 1.1 %collective-permute-start.11 = (bf16[256,512]{1,0:T(8,128)(2,1)S(1)}, bf16[256,512]{1,0:T(8,128)(2,1)S(1)}, u32[]{:S(2)}, u32[]{:S(2)}) collective-permute-start(bf16[256,512]{1,0:T(8,128)(2,1)S(1)} %collective-permute-done.6.refs_1_), channel_id=1, source_target_pairs={{0,2},{2,0},{4,6},{6,4},{8,10},{10,8},{12,14},{14,12},{16,18},{18,... | collective-permute-start | bytes 786440 | tf_op jit(solution)/shard_map/ppermute | solution.py:574
  37.3 1.5 %collective-permute-start.12 = (bf16[256,512]{1,0:T(8,128)(2,1)S(1)}, bf16[256,512]{1,0:T(8,128)(2,1)S(1)}, u32[]{:S(2)}, u32[]{:S(2)}) collective-permute-start(bf16[256,512]{1,0:T(8,128)(2,1)S(1)} %collective-permute-done.6.refs_1_), channel_id=1, source_target_pairs={{0,4},{2,6},{4,0},{6,2},{8,12},{10,14},{12,8},{14,10},{16,20},{18,... | collective-permute-start | bytes 786440 | tf_op jit(solution)/shard_map/ppermute | solution.py:574
  38.9 0.5 collective-permute-start.16
  39.4 1.3 %collective-permute-done.10.near = bf16[4,2,128,128]{3,2,1,0:T(8,128)(2,1)S(1)} collective-permute-done((bf16[4,2,128,128]{3,2,1,0:T(8,128)(2,1)S(1)}, bf16[4,2,128,128]{3,2,1,0:T(8,128)(2,1)S(1)}, u32[]{:S(2)}, u32[]{:S(2)}) %collective-permute-start.10) | collective-permute-done | bytes 262176 | tf_op jit(solution)/shard_map/ppermute | solution.py:622
  40.7 6.1 %collective-permute-done.9.far = bf16[4,2,128,128]{3,2,1,0:T(8,128)(2,1)S(1)} collective-permute-done((bf16[4,2,128,128]{3,2,1,0:T(8,128)(2,1)S(1)}, bf16[4,2,128,128]{3,2,1,0:T(8,128)(2,1)S(1)}, u32[]{:S(2)}, u32[]{:S(2)}) %collective-permute-start.9) | collective-permute-done | bytes 262176 | tf_op jit(solution)/shard_map/ppermute | solution.py:621
  46.8 0.0 copy-start.9
  46.8 0.0 copy-start.10
  46.8 0.0 copy-start.1
  46.8 0.1 merge.1
  46.9 0.0 collective-permute-done.11.refs_3_
  46.9 0.0 collective-permute-done.12.refs_5_
  47.0 2.1 %collective-permute-start.13 = (bf16[3,128,128]{2,1,0:T(8,128)(2,1)S(1)}, bf16[3,128,128]{2,1,0:T(8,128)(2,1)S(1)}, u32[]{:S(2)}, u32[]{:S(2)}) collective-permute-start(bf16[3,128,128]{2,1,0:T(8,128)(2,1)S(1)} %merge_both.1), channel_id=1, source_target_pairs={{0,10},{2,8},{4,14},{6,12},{8,2},{10,0},{12,6},{14,4},{16,26},{18,... | collective-permute-start | bytes 294920 | tf_op jit(solution)/shard_map/ppermute | solution.py:574
  49.0 0.7 collective-permute-start.14
  49.7 1.5 %collective-permute-start.15 = (bf16[3,128,128]{2,1,0:T(8,128)(2,1)S(1)}, bf16[3,128,128]{2,1,0:T(8,128)(2,1)S(1)}, u32[]{:S(2)}, u32[]{:S(2)}) collective-permute-start(bf16[3,128,128]{2,1,0:T(8,128)(2,1)S(1)} %get-tuple-element.87), channel_id=1, source_target_pairs={{0,2},{2,0},{4,6},{6,4},{8,10},{10,8},{12,14},{14,12},{16,18},{18,... | collective-permute-start | bytes 294920 | tf_op jit(solution)/shard_map/ppermute | solution.py:574
  51.1 0.9 %collective-permute-start.18 = (bf16[256,512]{1,0:T(8,128)(2,1)S(1)}, bf16[256,512]{1,0:T(8,128)(2,1)S(1)}, u32[]{:S(2)}, u32[]{:S(2)}) collective-permute-start(bf16[256,512]{1,0:T(8,128)(2,1)S(1)} %collective-permute-done.11.refs_3_), channel_id=1, source_target_pairs={{0,4},{2,6},{4,0},{6,2},{8,12},{10,14},{12,8},{14,10},{16,20},{18,... | collective-permute-start | bytes 786440 | tf_op jit(solution)/shard_map/ppermute | solution.py:574
  52.0 0.1 collective-permute-done.16.refs_6_
  52.1 1.2 %collective-permute-done.13.by_both = bf16[3,128,128]{2,1,0:T(8,128)(2,1)S(1)} collective-permute-done((bf16[3,128,128]{2,1,0:T(8,128)(2,1)S(1)}, bf16[3,128,128]{2,1,0:T(8,128)(2,1)S(1)}, u32[]{:S(2)}, u32[]{:S(2)}) %collective-permute-start.13) | collective-permute-done | bytes 98336 | tf_op jit(solution)/shard_map/ppermute | solution.py:574
  53.3 1.1 %collective-permute-done.14.by_zl = bf16[3,128,128]{2,1,0:T(8,128)(2,1)S(1)} collective-permute-done((bf16[3,128,128]{2,1,0:T(8,128)(2,1)S(1)}, bf16[3,128,128]{2,1,0:T(8,128)(2,1)S(1)}, u32[]{:S(2)}, u32[]{:S(2)}) %collective-permute-start.14) | collective-permute-done | bytes 98336 | tf_op jit(solution)/shard_map/ppermute | solution.py:574
  54.4 0.3 collective-permute-done.15.by_x
  54.6 0.0 copy-done
  54.7 1.2 %project.1 = (f32[128,1024]{1,0:T(8,128)S(1)}, bf16[128,1024]{1,0:T(8,128)(2,1)S(1)}) custom-call(bf16[3,128,128]{2,1,0:T(8,128)(2,1)S(1)} %collective-permute-done.13.by_both, bf16[3,128,128]{2,1,0:T(8,128)(2,1)S(1)} %collective-permute-done.14.by_zl, bf16[3,128,128]{2,1,0:T(8,128)(2,1)S(1)} %collective-permute-done.15.by_x, ...), custom_call_target="tpu_custom_call" | custom-call | tf_op jit(solution)/shard_map/project/pallas_call | solution.py:632
  55.8 0.1 collective-permute-start.17
  55.9 0.0 copy-done.9
  55.9 0.0 copy-done.10
  55.9 0.2 place.1
  56.1 1.7 %collective-permute-done.18.refs_7_ = bf16[256,512]{1,0:T(8,128)(2,1)S(1)} collective-permute-done((bf16[256,512]{1,0:T(8,128)(2,1)S(1)}, bf16[256,512]{1,0:T(8,128)(2,1)S(1)}, u32[]{:S(2)}, u32[]{:S(2)}) %collective-permute-start.18) | collective-permute-done | bytes 262176 | tf_op jit(solution)/shard_map/ppermute | solution.py:574
  57.8 0.0 collective-permute-done.17.other
  57.8 0.0 copy-done.1
  57.8 0.5 pack.1
  58.3 21.4 %all_to_all.5.got = bf16[16,112,128]{2,1,0:T(8,128)(2,1)S(1)} all-to-all(bf16[16,112,128]{2,1,0:T(8,128)(2,1)S(1)} %pack.1), channel_id=1, replica_groups=mesh['ctx'=16,'head'=2] {'ctx'}, dimensions={0} | all-to-all | bytes 917504 | tf_op jit(solution)/shard_map/all_to_all | solution.py:661
  79.7 0.1 collective-permute-start.19
  79.8 1.3 %collective-permute-done.19.other = bf16[16,32,128]{2,1,0:T(8,128)(2,1)S(1)} collective-permute-done((bf16[16,32,128]{2,1,0:T(8,128)(2,1)S(1)}, bf16[16,32,128]{2,1,0:T(8,128)(2,1)S(1)}, u32[]{:S(2)}, u32[]{:S(2)}) %collective-permute-start.19) | collective-permute-done | bytes 131104 | tf_op jit(solution)/shard_map/ppermute | solution.py:662
  81.1 0.0 copy-done.2
  81.1 0.0 copy-done.4
  81.1 2.6 %finish.1 = (f32[64,512]{1,0:T(8,128)}, f32[256,512]{1,0:T(8,128)}, f32[256,512]{1,0:T(8,128)}, f32[256,512]{1,0:T(8,128)}) custom-call(bf16[16,112,128]{2,1,0:T(8,128)(2,1)S(1)} %all_to_all.5.got, bf16[16,32,128]{2,1,0:T(8,128)(2,1)S(1)} %collective-permute-done.19.other, bf16[256,512]{1,0:T(8,128)(2,1)S(1)} %get-tuple-element.71.refs_0_, ...), custom_call_target="tpu_custom_call" | custom-call | tf_op jit(solution)/shard_map/finish/pallas_call | solution.py:665
  (11 shorter events, 0.1 us)
Async XLA Ops:
  1.3 1.0 %copy-start.5 = (bf16[2,128,512]{2,1,0:T(8,128)(2,1)S(1)}, bf16[2,128,512]{2,1,0:T(8,128)(2,1)}, u32[]{:S(2)}) copy-start(bf16[2,128,512]{2,1,0:T(8,128)(2,1)} %keys_values.1) | copy-start | bytes 786436
  2.2 0.9 %copy-start.6 = (bf16[128,1024]{1,0:T(8,128)(2,1)S(1)}, bf16[128,1024]{1,0:T(8,128)(2,1)}, u32[]{:S(2)}) copy-start(bf16[128,1024]{1,0:T(8,128)(2,1)} %rows.1) | copy-start | bytes 786436
  3.2 0.9 %copy-start.7 = (bf16[128,512]{1,0:T(8,128)(2,1)S(1)}, bf16[128,512]{1,0:T(8,128)(2,1)}, u32[]{:S(2)}) copy-start(bf16[128,512]{1,0:T(8,128)(2,1)} %queries.1) | copy-start | bytes 393220
  4.1 0.9 %copy-start.8 = (bf16[128,512]{1,0:T(8,128)(2,1)S(1)}, bf16[128,512]{1,0:T(8,128)(2,1)}, u32[]{:S(2)}) copy-start(bf16[128,512]{1,0:T(8,128)(2,1)} %cot.1) | copy-start | bytes 393220
  5.3 12.8 %collective-permute-start.1 = (bf16[544,128]{1,0:T(8,128)(2,1)S(1)}, bf16[544,128]{1,0:T(8,128)(2,1)S(1)}, u32[]{:S(2)}, u32[]{:S(2)}) collective-permute-start(bf16[544,128]{1,0:T(8,128)(2,1)S(1)} %get-tuple-element.57), channel_id=1, source_target_pairs={{0,10},{2,8},{4,14},{6,12},{8,2},{10,0},{12,6},{14,4},{16,26},{18,... | collective-permute-start | bytes 417800 | tf_op jit(solution)/shard_map/ppermute | solution.py:574
  9.3 9.6 %collective-permute-start.2 = (bf16[544,128]{1,0:T(8,128)(2,1)S(1)}, bf16[544,128]{1,0:T(8,128)(2,1)S(1)}, u32[]{:S(2)}, u32[]{:S(2)}) collective-permute-start(bf16[544,128]{1,0:T(8,128)(2,1)S(1)} %get-tuple-element.58), channel_id=1, source_target_pairs={{0,8},{2,10},{4,12},{6,14},{8,0},{10,2},{12,4},{14,6},{16,24},{18,... | collective-permute-start | bytes 417800 | tf_op jit(solution)/shard_map/ppermute | solution.py:574
  9.8 9.2 %collective-permute-start.3 = (bf16[544,128]{1,0:T(8,128)(2,1)S(1)}, bf16[544,128]{1,0:T(8,128)(2,1)S(1)}, u32[]{:S(2)}, u32[]{:S(2)}) collective-permute-start(bf16[544,128]{1,0:T(8,128)(2,1)S(1)} %get-tuple-element.59), channel_id=1, source_target_pairs={{0,2},{2,0},{4,6},{6,4},{8,10},{10,8},{12,14},{14,12},{16,18},{18,... | collective-permute-start | bytes 417800 | tf_op jit(solution)/shard_map/ppermute | solution.py:574
  10.0 8.1 %collective-permute-start = (bf16[128,512]{1,0:T(8,128)(2,1)S(1)}, bf16[128,512]{1,0:T(8,128)(2,1)S(1)}, u32[]{:S(2)}, u32[]{:S(2)}) collective-permute-start(bf16[128,512]{1,0:T(8,128)(2,1)S(1)} %get-tuple-element.56.rows_1), channel_id=1, source_target_pairs={{0,16},{2,18},{4,20},{6,22},{8,24},{10,26},{12,28},{14,30},{16,0},... | collective-permute-start | bytes 393224 | tf_op jit(solution)/shard_map/ppermute | solution.py:574
  19.0 9.3 %collective-permute-start.4 = (bf16[4,272,128]{2,1,0:T(8,128)(2,1)S(1)}, bf16[4,272,128]{2,1,0:T(8,128)(2,1)S(1)}, u32[]{:S(2)}, u32[]{:S(2)}) collective-permute-start(bf16[4,272,128]{2,1,0:T(8,128)(2,1)S(1)} %get-tuple-element.64.near_own), channel_id=1, source_target_pairs={{0,4},{2,6},{4,0},{6,2},{8,12},{10,14},{12,8},{14,10},{16,20},{18,... | collective-permute-start | bytes 835592 | tf_op jit(solution)/shard_map/ppermute | solution.py:586
  20.6 10.2 %collective-permute-start.5 = (bf16[4,272,128]{2,1,0:T(8,128)(2,1)S(1)}, bf16[4,272,128]{2,1,0:T(8,128)(2,1)S(1)}, u32[]{:S(2)}, u32[]{:S(2)}) collective-permute-start(bf16[4,272,128]{2,1,0:T(8,128)(2,1)S(1)} %get-tuple-element.65.far_own), channel_id=1, source_target_pairs={{0,16},{2,18},{4,20},{6,22},{8,24},{10,26},{12,28},{14,30},{17,1},... | collective-permute-start | bytes 835592 | tf_op jit(solution)/shard_map/ppermute | solution.py:585
  25.1 7.6 %collective-permute-start.6 = (bf16[256,512]{1,0:T(8,128)(2,1)S(1)}, bf16[256,512]{1,0:T(8,128)(2,1)S(1)}, u32[]{:S(2)}, u32[]{:S(2)}) collective-permute-start(bf16[256,512]{1,0:T(8,128)(2,1)S(1)} %get-tuple-element.71.refs_0_), channel_id=1, source_target_pairs={{0,8},{2,10},{4,12},{6,14},{8,0},{10,2},{12,4},{14,6},{16,24},{18,... | collective-permute-start | bytes 786440 | tf_op jit(solution)/shard_map/ppermute | solution.py:574
  26.8 6.4 %collective-permute-start.7 = (bf16[256,512]{1,0:T(8,128)(2,1)S(1)}, bf16[256,512]{1,0:T(8,128)(2,1)S(1)}, u32[]{:S(2)}, u32[]{:S(2)}) collective-permute-start(bf16[256,512]{1,0:T(8,128)(2,1)S(1)} %get-tuple-element.71.refs_0_), channel_id=1, source_target_pairs={{0,2},{2,0},{4,6},{6,4},{8,10},{10,8},{12,14},{14,12},{16,18},{18,... | collective-permute-start | bytes 786440 | tf_op jit(solution)/shard_map/ppermute | solution.py:574
  27.8 6.4 %collective-permute-start.8 = (bf16[256,512]{1,0:T(8,128)(2,1)S(1)}, bf16[256,512]{1,0:T(8,128)(2,1)S(1)}, u32[]{:S(2)}, u32[]{:S(2)}) collective-permute-start(bf16[256,512]{1,0:T(8,128)(2,1)S(1)} %get-tuple-element.71.refs_0_), channel_id=1, source_target_pairs={{0,4},{2,6},{4,0},{6,2},{8,12},{10,14},{12,8},{14,10},{16,20},{18,... | collective-permute-start | bytes 786440 | tf_op jit(solution)/shard_map/ppermute | solution.py:574
  30.9 23.7 %copy-start = (bf16[3,1024,512]{2,1,0:T(8,128)(2,1)S(1)}, bf16[3,1024,512]{2,1,0:T(8,128)(2,1)}, u32[]{:S(2)}) copy-start(bf16[3,1024,512]{2,1,0:T(8,128)(2,1)} %weight.1) | copy-start | bytes 9437188
  34.2 6.4 %collective-permute-start.10 = (bf16[4,2,128,128]{3,2,1,0:T(8,128)(2,1)S(1)}, bf16[4,2,128,128]{3,2,1,0:T(8,128)(2,1)S(1)}, u32[]{:S(2)}, u32[]{:S(2)}) collective-permute-start(bf16[4,2,128,128]{3,2,1,0:T(8,128)(2,1)S(1)} %near.1), channel_id=1, source_target_pairs={{0,4},{2,6},{4,0},{6,2},{8,12},{10,14},{12,8},{14,10},{16,20},{18,... | collective-permute-start | bytes 786440 | tf_op jit(solution)/shard_map/ppermute | solution.py:622
  34.8 12.0 %collective-permute-start.9 = (bf16[4,2,128,128]{3,2,1,0:T(8,128)(2,1)S(1)}, bf16[4,2,128,128]{3,2,1,0:T(8,128)(2,1)S(1)}, u32[]{:S(2)}, u32[]{:S(2)}) collective-permute-start(bf16[4,2,128,128]{3,2,1,0:T(8,128)(2,1)S(1)} %get-tuple-element.72), channel_id=1, source_target_pairs={{16,0},{18,2},{20,4},{22,6},{24,8},{26,10},{28,12},{30,14},{1,17},... | collective-permute-start | bytes 786440 | tf_op jit(solution)/shard_map/ppermute | solution.py:621
  36.3 10.7 %collective-permute-start.11 = (bf16[256,512]{1,0:T(8,128)(2,1)S(1)}, bf16[256,512]{1,0:T(8,128)(2,1)S(1)}, u32[]{:S(2)}, u32[]{:S(2)}) collective-permute-start(bf16[256,512]{1,0:T(8,128)(2,1)S(1)} %collective-permute-done.6.refs_1_), channel_id=1, source_target_pairs={{0,2},{2,0},{4,6},{6,4},{8,10},{10,8},{12,14},{14,12},{16,18},{18,... | collective-permute-start | bytes 786440 | tf_op jit(solution)/shard_map/ppermute | solution.py:574
  37.3 9.6 %collective-permute-start.12 = (bf16[256,512]{1,0:T(8,128)(2,1)S(1)}, bf16[256,512]{1,0:T(8,128)(2,1)S(1)}, u32[]{:S(2)}, u32[]{:S(2)}) collective-permute-start(bf16[256,512]{1,0:T(8,128)(2,1)S(1)} %collective-permute-done.6.refs_1_), channel_id=1, source_target_pairs={{0,4},{2,6},{4,0},{6,2},{8,12},{10,14},{12,8},{14,10},{16,20},{18,... | collective-permute-start | bytes 786440 | tf_op jit(solution)/shard_map/ppermute | solution.py:574
  38.9 13.3 %collective-permute-start.16 = (bf16[256,512]{1,0:T(8,128)(2,1)S(1)}, bf16[256,512]{1,0:T(8,128)(2,1)S(1)}, u32[]{:S(2)}, u32[]{:S(2)}) collective-permute-start(bf16[256,512]{1,0:T(8,128)(2,1)S(1)} %collective-permute-done.7.refs_2_), channel_id=1, source_target_pairs={{0,4},{2,6},{4,0},{6,2},{8,12},{10,14},{12,8},{14,10},{16,20},{18,... | collective-permute-start | bytes 786440 | tf_op jit(solution)/shard_map/ppermute | solution.py:574
  46.8 9.1 %copy-start.9 = (s32[128,1]{0,1:T(1,128)S(1)}, s32[128,1]{0,1:T(1,128)}, u32[]{:S(2)}) copy-start(s32[128,1]{0,1:T(1,128)} %param.19) | copy-start | bytes 1540
  46.8 9.1 %copy-start.10 = (s32[128]{0:T(128)S(1)}, s32[128]{0:T(128)}, u32[]{:S(2)}) copy-start(s32[128]{0:T(128)} %param.20) | copy-start | bytes 1540
  46.8 11.0 %copy-start.1 = (bf16[1024,512]{1,0:T(8,128)(2,1)S(1)}, bf16[1024,512]{1,0:T(8,128)(2,1)}, u32[]{:S(2)}) copy-start(bf16[1024,512]{1,0:T(8,128)(2,1)} %adapter.1) | copy-start | bytes 3145732
  47.0 6.3 %collective-permute-start.13 = (bf16[3,128,128]{2,1,0:T(8,128)(2,1)S(1)}, bf16[3,128,128]{2,1,0:T(8,128)(2,1)S(1)}, u32[]{:S(2)}, u32[]{:S(2)}) collective-permute-start(bf16[3,128,128]{2,1,0:T(8,128)(2,1)S(1)} %merge_both.1), channel_id=1, source_target_pairs={{0,10},{2,8},{4,14},{6,12},{8,2},{10,0},{12,6},{14,4},{16,26},{18,... | collective-permute-start | bytes 294920 | tf_op jit(solution)/shard_map/ppermute | solution.py:574
  49.0 5.4 %collective-permute-start.14 = (bf16[3,128,128]{2,1,0:T(8,128)(2,1)S(1)}, bf16[3,128,128]{2,1,0:T(8,128)(2,1)S(1)}, u32[]{:S(2)}, u32[]{:S(2)}) collective-permute-start(bf16[3,128,128]{2,1,0:T(8,128)(2,1)S(1)} %get-tuple-element.86), channel_id=1, source_target_pairs={{0,8},{2,10},{4,12},{6,14},{8,0},{10,2},{12,4},{14,6},{16,24},{18,... | collective-permute-start | bytes 294920 | tf_op jit(solution)/shard_map/ppermute | solution.py:574
  49.7 5.0 %collective-permute-start.15 = (bf16[3,128,128]{2,1,0:T(8,128)(2,1)S(1)}, bf16[3,128,128]{2,1,0:T(8,128)(2,1)S(1)}, u32[]{:S(2)}, u32[]{:S(2)}) collective-permute-start(bf16[3,128,128]{2,1,0:T(8,128)(2,1)S(1)} %get-tuple-element.87), channel_id=1, source_target_pairs={{0,2},{2,0},{4,6},{6,4},{8,10},{10,8},{12,14},{14,12},{16,18},{18,... | collective-permute-start | bytes 294920 | tf_op jit(solution)/shard_map/ppermute | solution.py:574
  51.1 6.6 %collective-permute-start.18 = (bf16[256,512]{1,0:T(8,128)(2,1)S(1)}, bf16[256,512]{1,0:T(8,128)(2,1)S(1)}, u32[]{:S(2)}, u32[]{:S(2)}) collective-permute-start(bf16[256,512]{1,0:T(8,128)(2,1)S(1)} %collective-permute-done.11.refs_3_), channel_id=1, source_target_pairs={{0,4},{2,6},{4,0},{6,2},{8,12},{10,14},{12,8},{14,10},{16,20},{18,... | collective-permute-start | bytes 786440 | tf_op jit(solution)/shard_map/ppermute | solution.py:574
  54.6 26.5 %copy-start.2 = (f32[256,512]{1,0:T(8,128)S(1)}, f32[256,512]{1,0:T(8,128)}, u32[]{:S(2)}) copy-start(f32[256,512]{1,0:T(8,128)} %refs_8_.1) | copy-start | bytes 1572868
  54.6 26.5 %copy-start.3 = (f32[256,512]{1,0:T(8,128)S(1)}, f32[256,512]{1,0:T(8,128)}, u32[]{:S(2)}) copy-start(f32[256,512]{1,0:T(8,128)} %refs_9_.1) | copy-start | bytes 1572868
  54.6 26.5 %copy-start.4 = (f32[256,512]{1,0:T(8,128)S(1)}, f32[256,512]{1,0:T(8,128)}, u32[]{:S(2)}) copy-start(f32[256,512]{1,0:T(8,128)} %refs_10_.1) | copy-start | bytes 1572868
  55.8 1.9 %collective-permute-start.17 = (bf16[128,1024]{1,0:T(8,128)(2,1)S(1)}, bf16[128,1024]{1,0:T(8,128)(2,1)S(1)}, u32[]{:S(2)}, u32[]{:S(2)}) collective-permute-start(bf16[128,1024]{1,0:T(8,128)(2,1)S(1)} %get-tuple-element.95), channel_id=1, source_target_pairs={{0,1},{1,0},{2,3},{3,2},{4,5},{5,4},{6,7},{7,6},{8,9},{9,8},{10,11... | collective-permute-start | bytes 786440 | tf_op jit(solution)/shard_map/ppermute | solution.py:648
  79.7 1.4 %collective-permute-start.19 = (bf16[16,32,128]{2,1,0:T(8,128)(2,1)S(1)}, bf16[16,32,128]{2,1,0:T(8,128)(2,1)S(1)}, u32[]{:S(2)}, u32[]{:S(2)}) collective-permute-start(bf16[16,32,128]{2,1,0:T(8,128)(2,1)S(1)} %slice.4), channel_id=1, source_target_pairs={{0,1},{1,0},{2,3},{3,2},{4,5},{5,4},{6,7},{7,6},{8,9},{9,8},{10,11... | collective-permute-start | bytes 393224 | tf_op jit(solution)/shard_map/ppermute | solution.py:662

commit v4 on v3

--- a/solution.py
+++ b/solution.py
@@ -216,6 +216,7 @@
 PAIR = 2 * BLOCK
 META = 16
 PART = PAIR + META
+FAR_PART = PART + META
 ACROSS_Y = [(i, i ^ 2) for i in range(16)]
 FAR_OUT = [(i * 2, (i + 8) * 2) for i in range(8)] + [((i + 8) * 2 + 1, i * 2 + 1) for i in range(8)]
 FAR_BACK = [(b, a) for a, b in FAR_OUT]
@@ -264,13 +265,15 @@
             for base, pair in ((0, near), (PART, far)):
                 for at, source in enumerate(pair):
                     moves.append((source.at[:, lanes], out.at[base + at * BLOCK : base + (at + 1) * BLOCK, :]))
-        moves.append((rows.at[:, half * cols : (half + 1) * cols], held_rows))
+        moves.append((rows.at[:, half * cols : (half + 1) * cols], held_rows.at[:BLOCK, :]))
         moves = [pltpu.make_async_copy(a, b, sems.at[k]) for k, (a, b) in enumerate(moves)]
         for move in moves:
             move.start()
+        held_rows[BLOCK:, :] = jnp.zeros((META, cols), BF16)
         for out in outs:
             out[PAIR:PART, :] = meta
-            out[PART + PAIR :, :] = meta
+            out[PART + PAIR : PART + PART, :] = meta
+            out[PART + PART :, :] = jnp.zeros((META, BLOCK), BF16)
         for move in moves:
             move.wait()
 
@@ -290,9 +293,9 @@
     for flip, part in enumerate((own, by_x, by_zl, by_both)):
         near[flip] = part[:PART, :]
         far[flip] = part[PART:, :]
-    count = rows_1.shape[0]
-    two[:count, :] = rows_1[...]
-    two[count:, :] = rows_2[...]
+    count = two.shape[0] // 2
+    two[:count, :] = rows_1[:count, :]
+    two[count:, :] = rows_2[:count, :]
 
 
 def lower_of(meta):
@@ -388,7 +391,7 @@
     def put(at, factor):
         def store(value):
             for spot in range(4):
-                far_out[spot, at] = (value[spot * BLOCK : (spot + 1) * BLOCK] * factor).astype(BF16)
+                far_out[spot, at * BLOCK : (at + 1) * BLOCK, :] = (value[spot * BLOCK : (spot + 1) * BLOCK] * factor).astype(BF16)
 
         return store
 
@@ -473,8 +476,8 @@
         rows = slice(flip * BLOCK, (flip + 1) * BLOCK)
         out[0] = (near_1_sum[rows, :] * grad_scale + near[flip, 0].astype(F32)).astype(BF16)
         both = (near_2_sum[rows, :] + far_sum[1, rows, :]) * weight_scale
-        out[1] = (both + near[flip, 1].astype(F32) + far[flip, 1].astype(F32)).astype(BF16)
-        out[2] = (far_sum[0, rows, :] * grad_scale + far[flip, 0].astype(F32)).astype(BF16)
+        out[1] = (both + near[flip, 1].astype(F32) + far[flip, BLOCK:PAIR, :].astype(F32)).astype(BF16)
+        out[2] = (far_sum[0, rows, :] * grad_scale + far[flip, :BLOCK, :].astype(F32)).astype(BF16)
 
 
 def finish_body(got, other, *refs):
@@ -559,10 +562,10 @@
     head_cols = adapter.shape[1]
     width = event_rows.shape[1]
     capacity = max(2, 2 * rows_here // n_ctx)
-    dealt = shape((2 * PART, BLOCK), BF16)
+    dealt = shape((PART + FAR_PART, BLOCK), BF16)
     *dealt, own_rows = pl.pallas_call(
         deal_body,
-        out_shape=(dealt,) * 4 + (shape((rows_here, head_cols), BF16),),
+        out_shape=(dealt,) * 4 + (shape((rows_here + META, head_cols), BF16),),
         in_specs=[SMEM] + [pl.BlockSpec(memory_space=pltpu.HBM)] * 4,
         out_specs=(VMEM,) * 5,
         scratch_shapes=[pltpu.SemaphoreType.DMA((17,))],
@@ -578,7 +581,7 @@
     zh_rows, both, by_zl, by_x = lax.optimization_barrier((zh_rows, both, by_zl, by_x))
     far_own, near_own, two = kernel_call(
         gather_body,
-        (shape((4, PART, BLOCK), BF16),) * 2 + (shape((2 * rows_here, head_cols), BF16),),
+        (shape((4, FAR_PART, BLOCK), BF16), shape((4, PART, BLOCK), BF16), shape((2 * rows_here, head_cols), BF16)),
         (dealt[0], own_rows, by_x, by_zl, both, zh_rows),
         "gather",
     )
@@ -601,7 +604,7 @@
     )(near_own, far_own, near_in)
     near_1, near_2, far_out = pl.pallas_call(
         functools.partial(attend_far_body, *scales),
-        out_shape=(near_sum, near_sum, shape((4, 2, BLOCK, BLOCK), BF16)),
+        out_shape=(near_sum, near_sum, shape((4, PART, BLOCK), BF16)),
         in_specs=[VMEM] * 5,
         out_specs=(VMEM,) * 3,
         scratch_shapes=side_scratch,
@@ -625,10 +628,10 @@
     (both,) = kernel_call(functools.partial(merge_body, (3,), *scales), (part,), sums, "merge_both")
     both, *sums = lax.optimization_barrier((both, *sums))
     own, *parts = kernel_call(functools.partial(merge_body, (0, 1, 2), *scales), (part,) * 3, sums, "merge")
-    both, *parts, zl_x_rows, zl_y_rows = lax.optimization_barrier((both, *parts, zl_x_rows, zl_y_rows))
-    x_y_rows, zl_x_y_rows = [exchange(rows, ROUNDS[3]) for rows in (x_rows, zl_x_rows)]
+    both, *parts, zl_x_rows = lax.optimization_barrier((both, *parts, zl_x_rows))
+    x_y_rows, zl_x_y_rows = exchange(y_rows, ROUNDS[2]), exchange(zl_x_rows, ROUNDS[3])
     both, by_zl, by_x = [exchange(part, bit) for part, bit in zip((both, parts[1], parts[0]), (5, 4, 1))]
-    both, by_zl, by_x, x_y_rows = lax.optimization_barrier((both, by_zl, by_x, x_y_rows))
+    both, by_zl, by_x, zl_y_rows, zl_x_y_rows = lax.optimization_barrier((both, by_zl, by_x, zl_y_rows, zl_x_y_rows))
     partial, sent = pl.pallas_call(
         project_body,
         out_shape=(shape((rows_here, width), F32), shape((rows_here, width), BF16)),
@@ -646,7 +649,7 @@
         "place",
     )
     other = lax.ppermute(sent, "head", SWAP)
-    other, zl_x_y_rows = lax.optimization_barrier((other, zl_x_y_rows))
+    other, x_y_rows = lax.optimization_barrier((other, x_y_rows))
     share = width // n_ctx // 2
     packed_rows = capacity * (head_cols // BLOCK + 1)
     packed = pl.pallas_call(

time: 84.2 us -> 81.8 us (0.971)
  blocking collectives: 21.4 us -> 16.1 us
  waiting for transfers between devices: 22.3 us -> 26.2 us
  starting transfers between devices: 27.2 us -> 26.3 us
    all_to_all x1, blocking collectives: 21.4 us -> 16.1 us  [dealt_device(): got = lax.all_to_all(packed, 'ctx', 0, 0, tiled=True)]
    ppermute x1, waiting for transfers between devices: 6.1 us -> 2.53 us  [dealt_device(): far_back = lax.ppermute(far_out, ('ctx', 'head'), FAR_BACK)]
    ppermute x1, waiting for transfers between devices: 1.29 us -> 4.69 us  [dealt_device(): near_back = lax.ppermute(near_out, 'ctx', ACROSS_Y)]
    ppermute x14, waiting for transfers between devices: 13.6 us -> 16 us  [exchange(): return lax.ppermute(sent, 'ctx', [(i, i ^ bit) for i in range(16)])]
    ppermute x1, starting transfers between devices: 4.5 us -> 2.47 us  [dealt_device(): far_in = lax.ppermute(far_own, ('ctx', 'head'), FAR_OUT)]
    ppermute x1, waiting for transfers between devices: 0.01 us -> 1.59 us  [dealt_device(): near_in = lax.ppermute(near_own, 'ctx', ACROSS_Y)]
where the time goes in v4:
time: 81.8 us; the launch traced here: 81.5 us
  starting transfers between devices  26.3 us (32%)
  waiting for transfers between devices  26.2 us (32%)
  blocking collectives  16.1 us (20%)
  Pallas kernels  7.6 us (9%)
  local copies, waits for them, and re-layouts  3.75 us (5%)
  between operations  1.62 us (2%)
    ppermute x14, starting transfers between devices, exchange(): return lax.ppermute(sent, 'ctx', [(i, i ^ bit) for i in range(16)])  19 us
    all_to_all x1, blocking collectives, dealt_device(): got = lax.all_to_all(packed, 'ctx', 0, 0, tiled=True)  16.1 us
    ppermute x14, waiting for transfers between devices, exchange(): return lax.ppermute(sent, 'ctx', [(i, i ^ bit) for i in range(16)])  16 us
    ppermute x1, waiting for transfers between devices, dealt_device(): near_back = lax.ppermute(near_out, 'ctx', ACROSS_Y)  4.69 us
    unnamed x22, local copies, waits for them, and re-layouts  3.74 us
    pallas_call x1, Pallas kernels, dealt_device(): pl.pallas_call(finish_body, out_shape=(shape((width // n_ctx, head_cols),...  2.63 us
    ppermute x1, waiting for transfers between devices, dealt_device(): far_back = lax.ppermute(far_out, ('ctx', 'head'), FAR_BACK)  2.53 us
    pallas_call x1, Pallas kernels, dealt_device(): pl.pallas_call(functools.partial(attend_own_body, scales[0]), out_shape=(...  2.51 us
  transfers between devices with their start and end apart: 20, of which 13 were waited for; matrix products, arithmetic and copies ran while one was open for 0% of the time, Pallas kernels for 5%

profile of v4, /device:TPU:0, one launch (start us, length us, event | category | flops | bytes accessed | tf_op | source)
XLA Modules:
  0.0 81.5 jit_solution(661463694671191715)
XLA Ops:
  1.3 0.0 copy-start.5
  1.3 0.9 %copy-done.5 = bf16[2,128,512]{2,1,0:T(8,128)(2,1)S(1)} copy-done((bf16[2,128,512]{2,1,0:T(8,128)(2,1)S(1)}, bf16[2,128,512]{2,1,0:T(8,128)(2,1)}, u32[]{:S(2)}) %copy-start.5) | copy-done | bytes 262168
  2.2 0.9 %copy-done.6 = bf16[128,1024]{1,0:T(8,128)(2,1)S(1)} copy-done((bf16[128,1024]{1,0:T(8,128)(2,1)S(1)}, bf16[128,1024]{1,0:T(8,128)(2,1)}, u32[]{:S(2)}) %copy-start.6) | copy-done | bytes 262168
  3.2 0.9 %copy-done.7 = bf16[128,512]{1,0:T(8,128)(2,1)S(1)} copy-done((bf16[128,512]{1,0:T(8,128)(2,1)S(1)}, bf16[128,512]{1,0:T(8,128)(2,1)}, u32[]{:S(2)}) %copy-start.7) | copy-done | bytes 131096
  4.1 0.9 %copy-done.8 = bf16[128,512]{1,0:T(8,128)(2,1)S(1)} copy-done((bf16[128,512]{1,0:T(8,128)(2,1)S(1)}, bf16[128,512]{1,0:T(8,128)(2,1)}, u32[]{:S(2)}) %copy-start.8) | copy-done | bytes 131096
  5.0 0.3 deal.1
  5.3 4.1 %collective-permute-start = (bf16[144,512]{1,0:T(8,128)(2,1)S(1)}, bf16[144,512]{1,0:T(8,128)(2,1)S(1)}, u32[]{:S(2)}, u32[]{:S(2)}) collective-permute-start(bf16[144,512]{1,0:T(8,128)(2,1)S(1)} %get-tuple-element.56.rows_1), channel_id=1, source_target_pairs={{0,16},{2,18},{4,20},{6,22},{8,24},{10,26},{12,28},{14,30},{16,0},... | collective-permute-start | bytes 442376 | tf_op jit(solution)/shard_map/ppermute | solution.py:577
  9.4 2.5 %collective-permute-start.1 = (bf16[560,128]{1,0:T(8,128)(2,1)S(1)}, bf16[560,128]{1,0:T(8,128)(2,1)S(1)}, u32[]{:S(2)}, u32[]{:S(2)}) collective-permute-start(bf16[560,128]{1,0:T(8,128)(2,1)S(1)} %get-tuple-element.57), channel_id=1, source_target_pairs={{0,10},{2,8},{4,14},{6,12},{8,2},{10,0},{12,6},{14,4},{16,26},{18,... | collective-permute-start | bytes 430088 | tf_op jit(solution)/shard_map/ppermute | solution.py:577
  11.9 0.4 collective-permute-start.2
  12.4 0.5 collective-permute-start.3
  12.9 6.1 %collective-permute-done.1.by_both = bf16[560,128]{1,0:T(8,128)(2,1)S(1)} collective-permute-done((bf16[560,128]{1,0:T(8,128)(2,1)S(1)}, bf16[560,128]{1,0:T(8,128)(2,1)S(1)}, u32[]{:S(2)}, u32[]{:S(2)}) %collective-permute-start.1) | collective-permute-done | bytes 143392 | tf_op jit(solution)/shard_map/ppermute | solution.py:577
  19.0 1.6 %collective-permute-done.2.by_zl = bf16[560,128]{1,0:T(8,128)(2,1)S(1)} collective-permute-done((bf16[560,128]{1,0:T(8,128)(2,1)S(1)}, bf16[560,128]{1,0:T(8,128)(2,1)S(1)}, u32[]{:S(2)}, u32[]{:S(2)}) %collective-permute-start.2) | collective-permute-done | bytes 143392 | tf_op jit(solution)/shard_map/ppermute | solution.py:577
  20.6 0.0 collective-permute-done.3.by_x
  20.6 0.0 collective-permute-done.rows_2
  20.6 0.1 gather.1
  20.7 1.6 %collective-permute-start.4 = (bf16[4,272,128]{2,1,0:T(8,128)(2,1)S(1)}, bf16[4,272,128]{2,1,0:T(8,128)(2,1)S(1)}, u32[]{:S(2)}, u32[]{:S(2)}) collective-permute-start(bf16[4,272,128]{2,1,0:T(8,128)(2,1)S(1)} %get-tuple-element.64.near_own), channel_id=1, source_target_pairs={{0,4},{2,6},{4,0},{6,2},{8,12},{10,14},{12,8},{14,10},{16,20},{18,... | collective-permute-start | bytes 835592 | tf_op jit(solution)/shard_map/ppermute | solution.py:589
  22.3 2.5 %collective-permute-start.5 = (bf16[4,288,128]{2,1,0:T(8,128)(2,1)S(1)}, bf16[4,288,128]{2,1,0:T(8,128)(2,1)S(1)}, u32[]{:S(2)}, u32[]{:S(2)}) collective-permute-start(bf16[4,288,128]{2,1,0:T(8,128)(2,1)S(1)} %get-tuple-element.65.far_own), channel_id=1, source_target_pairs={{0,16},{2,18},{4,20},{6,22},{8,24},{10,26},{12,28},{14,30},{17,1},... | collective-permute-start | bytes 884744 | tf_op jit(solution)/shard_map/ppermute | solution.py:588
  24.8 2.5 %collective-permute-start.6 = (bf16[256,512]{1,0:T(8,128)(2,1)S(1)}, bf16[256,512]{1,0:T(8,128)(2,1)S(1)}, u32[]{:S(2)}, u32[]{:S(2)}) collective-permute-start(bf16[256,512]{1,0:T(8,128)(2,1)S(1)} %get-tuple-element.71.refs_0_), channel_id=1, source_target_pairs={{0,8},{2,10},{4,12},{6,14},{8,0},{10,2},{12,4},{14,6},{16,24},{18,... | collective-permute-start | bytes 786440 | tf_op jit(solution)/shard_map/ppermute | solution.py:577
  27.4 0.5 collective-permute-start.7
  27.9 0.5 collective-permute-start.8
  28.4 1.6 %collective-permute-done.4.near_in = bf16[4,272,128]{2,1,0:T(8,128)(2,1)S(1)} collective-permute-done((bf16[4,272,128]{2,1,0:T(8,128)(2,1)S(1)}, bf16[4,272,128]{2,1,0:T(8,128)(2,1)S(1)}, u32[]{:S(2)}, u32[]{:S(2)}) %collective-permute-start.4) | collective-permute-done | bytes 278560 | tf_op jit(solution)/shard_map/ppermute | solution.py:589
  30.0 2.5 %attend_own.1 = (f32[1024,128]{1,0:T(8,128)S(1)}, f32[1024,128]{1,0:T(8,128)S(1)}, f32[2,512,128]{2,1,0:T(8,128)S(1)}) custom-call(bf16[4,272,128]{2,1,0:T(8,128)(2,1)S(1)} %get-tuple-element.64.near_own, bf16[4,288,128]{2,1,0:T(8,128)(2,1)S(1)} %get-tuple-element.65.far_own, bf16[4,272,128]{2,1,0:T(8,128)(2,1)S(1)} %collective-permute-done.4.near_in), custom_call_target="tpu_custom_call" | custom-call | flops 1000000000 | bytes 1048576 | tf_op jit(solution)/shard_map/attend_own/pallas_call | solution.py:595
  32.5 0.0 collective-permute-done.5.far_in
  32.6 0.0 copy-start
  32.6 1.3 %collective-permute-done.6.refs_1_ = bf16[256,512]{1,0:T(8,128)(2,1)S(1)} collective-permute-done((bf16[256,512]{1,0:T(8,128)(2,1)S(1)}, bf16[256,512]{1,0:T(8,128)(2,1)S(1)}, u32[]{:S(2)}, u32[]{:S(2)}) %collective-permute-start.6) | collective-permute-done | bytes 262176 | tf_op jit(solution)/shard_map/ppermute | solution.py:577
  33.9 0.0 collective-permute-done.7.refs_2_
  33.9 0.4 collective-permute-done.8.refs_4_
  34.3 1.5 %collective-permute-start.9 = (bf16[4,272,128]{2,1,0:T(8,128)(2,1)S(1)}, bf16[4,272,128]{2,1,0:T(8,128)(2,1)S(1)}, u32[]{:S(2)}, u32[]{:S(2)}) collective-permute-start(bf16[4,272,128]{2,1,0:T(8,128)(2,1)S(1)} %get-tuple-element.72), channel_id=1, source_target_pairs={{16,0},{18,2},{20,4},{22,6},{24,8},{26,10},{28,12},{30,14},{1,17},... | collective-permute-start | bytes 835592 | tf_op jit(solution)/shard_map/ppermute | solution.py:624
  35.8 1.3 %collective-permute-start.10 = (bf16[4,2,128,128]{3,2,1,0:T(8,128)(2,1)S(1)}, bf16[4,2,128,128]{3,2,1,0:T(8,128)(2,1)S(1)}, u32[]{:S(2)}, u32[]{:S(2)}) collective-permute-start(bf16[4,2,128,128]{3,2,1,0:T(8,128)(2,1)S(1)} %near.1), channel_id=1, source_target_pairs={{0,4},{2,6},{4,0},{6,2},{8,12},{10,14},{12,8},{14,10},{16,20},{18,... | collective-permute-start | bytes 786440 | tf_op jit(solution)/shard_map/ppermute | solution.py:625
  37.1 0.7 collective-permute-start.11
  37.9 1.5 %collective-permute-start.15 = (bf16[256,512]{1,0:T(8,128)(2,1)S(1)}, bf16[256,512]{1,0:T(8,128)(2,1)S(1)}, u32[]{:S(2)}, u32[]{:S(2)}) collective-permute-start(bf16[256,512]{1,0:T(8,128)(2,1)S(1)} %collective-permute-done.6.refs_1_), channel_id=1, source_target_pairs={{0,4},{2,6},{4,0},{6,2},{8,12},{10,14},{12,8},{14,10},{16,20},{18,... | collective-permute-start | bytes 786440 | tf_op jit(solution)/shard_map/ppermute | solution.py:577
  39.4 4.7 %collective-permute-done.10.near = bf16[4,2,128,128]{3,2,1,0:T(8,128)(2,1)S(1)} collective-permute-done((bf16[4,2,128,128]{3,2,1,0:T(8,128)(2,1)S(1)}, bf16[4,2,128,128]{3,2,1,0:T(8,128)(2,1)S(1)}, u32[]{:S(2)}, u32[]{:S(2)}) %collective-permute-start.10) | collective-permute-done | bytes 262176 | tf_op jit(solution)/shard_map/ppermute | solution.py:625
  44.1 2.5 %collective-permute-done.9.far = bf16[4,272,128]{2,1,0:T(8,128)(2,1)S(1)} collective-permute-done((bf16[4,272,128]{2,1,0:T(8,128)(2,1)S(1)}, bf16[4,272,128]{2,1,0:T(8,128)(2,1)S(1)}, u32[]{:S(2)}, u32[]{:S(2)}) %collective-permute-start.9) | collective-permute-done | bytes 278560 | tf_op jit(solution)/shard_map/ppermute | solution.py:624
  46.6 0.0 copy-start.9
  46.6 0.0 copy-start.10
  46.7 0.0 copy-start.1
  46.7 0.1 merge.1
  46.8 0.0 collective-permute-done.11.refs_3_
  46.8 1.3 %collective-permute-start.16 = (bf16[256,512]{1,0:T(8,128)(2,1)S(1)}, bf16[256,512]{1,0:T(8,128)(2,1)S(1)}, u32[]{:S(2)}, u32[]{:S(2)}) collective-permute-start(bf16[256,512]{1,0:T(8,128)(2,1)S(1)} %collective-permute-done.11.refs_3_), channel_id=1, source_target_pairs={{0,4},{2,6},{4,0},{6,2},{8,12},{10,14},{12,8},{14,10},{16,20},{18,... | collective-permute-start | bytes 786440 | tf_op jit(solution)/shard_map/ppermute | solution.py:577
  48.1 0.0 collective-permute-start.12
  48.2 2.1 %collective-permute-start.13 = (bf16[3,128,128]{2,1,0:T(8,128)(2,1)S(1)}, bf16[3,128,128]{2,1,0:T(8,128)(2,1)S(1)}, u32[]{:S(2)}, u32[]{:S(2)}) collective-permute-start(bf16[3,128,128]{2,1,0:T(8,128)(2,1)S(1)} %get-tuple-element.86), channel_id=1, source_target_pairs={{0,8},{2,10},{4,12},{6,14},{8,0},{10,2},{12,4},{14,6},{16,24},{18,... | collective-permute-start | bytes 294920 | tf_op jit(solution)/shard_map/ppermute | solution.py:577
  50.3 1.3 %collective-permute-start.14 = (bf16[3,128,128]{2,1,0:T(8,128)(2,1)S(1)}, bf16[3,128,128]{2,1,0:T(8,128)(2,1)S(1)}, u32[]{:S(2)}, u32[]{:S(2)}) collective-permute-start(bf16[3,128,128]{2,1,0:T(8,128)(2,1)S(1)} %get-tuple-element.87), channel_id=1, source_target_pairs={{0,2},{2,0},{4,6},{6,4},{8,10},{10,8},{12,14},{14,12},{16,18},{18,... | collective-permute-start | bytes 294920 | tf_op jit(solution)/shard_map/ppermute | solution.py:577
  51.6 0.0 collective-permute-done.15.refs_5_
  51.6 0.7 collective-permute-start.18
  52.3 1.4 %collective-permute-done.12.by_both = bf16[3,128,128]{2,1,0:T(8,128)(2,1)S(1)} collective-permute-done((bf16[3,128,128]{2,1,0:T(8,128)(2,1)S(1)}, bf16[3,128,128]{2,1,0:T(8,128)(2,1)S(1)}, u32[]{:S(2)}, u32[]{:S(2)}) %collective-permute-start.12) | collective-permute-done | bytes 98336 | tf_op jit(solution)/shard_map/ppermute | solution.py:577
  53.7 0.9 %collective-permute-done.13.by_zl = bf16[3,128,128]{2,1,0:T(8,128)(2,1)S(1)} collective-permute-done((bf16[3,128,128]{2,1,0:T(8,128)(2,1)S(1)}, bf16[3,128,128]{2,1,0:T(8,128)(2,1)S(1)}, u32[]{:S(2)}, u32[]{:S(2)}) %collective-permute-start.13) | collective-permute-done | bytes 98336 | tf_op jit(solution)/shard_map/ppermute | solution.py:577
  54.6 1.4 %collective-permute-done.14.by_x = bf16[3,128,128]{2,1,0:T(8,128)(2,1)S(1)} collective-permute-done((bf16[3,128,128]{2,1,0:T(8,128)(2,1)S(1)}, bf16[3,128,128]{2,1,0:T(8,128)(2,1)S(1)}, u32[]{:S(2)}, u32[]{:S(2)}) %collective-permute-start.14) | collective-permute-done | bytes 98336 | tf_op jit(solution)/shard_map/ppermute | solution.py:577
  56.0 0.1 collective-permute-done.16.refs_7_
  56.1 0.0 copy-done
  56.1 1.2 %project.1 = (f32[128,1024]{1,0:T(8,128)S(1)}, bf16[128,1024]{1,0:T(8,128)(2,1)S(1)}) custom-call(bf16[3,128,128]{2,1,0:T(8,128)(2,1)S(1)} %collective-permute-done.12.by_both, bf16[3,128,128]{2,1,0:T(8,128)(2,1)S(1)} %collective-permute-done.13.by_zl, bf16[3,128,128]{2,1,0:T(8,128)(2,1)S(1)} %collective-permute-done.14.by_x, ...), custom_call_target="tpu_custom_call" | custom-call | tf_op jit(solution)/shard_map/project/pallas_call | solution.py:635
  57.3 0.4 collective-permute-start.17
  57.6 0.0 copy-done.9
  57.6 0.0 copy-done.10
  57.6 0.2 place.1
  57.8 2.8 %collective-permute-done.18.refs_6_ = bf16[256,512]{1,0:T(8,128)(2,1)S(1)} collective-permute-done((bf16[256,512]{1,0:T(8,128)(2,1)S(1)}, bf16[256,512]{1,0:T(8,128)(2,1)S(1)}, u32[]{:S(2)}, u32[]{:S(2)}) %collective-permute-start.18) | collective-permute-done | bytes 262176 | tf_op jit(solution)/shard_map/ppermute | solution.py:577
  60.7 0.0 collective-permute-done.17.other
  60.7 0.0 copy-done.1
  60.7 0.5 pack.1
  61.2 16.1 %all_to_all.5.got = bf16[16,112,128]{2,1,0:T(8,128)(2,1)S(1)} all-to-all(bf16[16,112,128]{2,1,0:T(8,128)(2,1)S(1)} %pack.1), channel_id=1, replica_groups=mesh['ctx'=16,'head'=2] {'ctx'}, dimensions={0} | all-to-all | bytes 917504 | tf_op jit(solution)/shard_map/all_to_all | solution.py:664
  77.3 0.1 collective-permute-start.19
  77.4 1.3 %collective-permute-done.19.other = bf16[16,32,128]{2,1,0:T(8,128)(2,1)S(1)} collective-permute-done((bf16[16,32,128]{2,1,0:T(8,128)(2,1)S(1)}, bf16[16,32,128]{2,1,0:T(8,128)(2,1)S(1)}, u32[]{:S(2)}, u32[]{:S(2)}) %collective-permute-start.19) | collective-permute-done | bytes 131104 | tf_op jit(solution)/shard_map/ppermute | solution.py:665
  78.7 0.0 copy-done.2
  78.7 0.0 copy-done.4
  78.7 2.6 %finish.1 = (f32[64,512]{1,0:T(8,128)}, f32[256,512]{1,0:T(8,128)}, f32[256,512]{1,0:T(8,128)}, f32[256,512]{1,0:T(8,128)}) custom-call(bf16[16,112,128]{2,1,0:T(8,128)(2,1)S(1)} %all_to_all.5.got, bf16[16,32,128]{2,1,0:T(8,128)(2,1)S(1)} %collective-permute-done.19.other, bf16[256,512]{1,0:T(8,128)(2,1)S(1)} %get-tuple-element.71.refs_0_, ...), custom_call_target="tpu_custom_call" | custom-call | tf_op jit(solution)/shard_map/finish/pallas_call | solution.py:668
  (11 shorter events, 0.1 us)
Async XLA Ops:
  1.3 1.0 %copy-start.5 = (bf16[2,128,512]{2,1,0:T(8,128)(2,1)S(1)}, bf16[2,128,512]{2,1,0:T(8,128)(2,1)}, u32[]{:S(2)}) copy-start(bf16[2,128,512]{2,1,0:T(8,128)(2,1)} %keys_values.1) | copy-start | bytes 786436
  2.2 0.9 %copy-start.6 = (bf16[128,1024]{1,0:T(8,128)(2,1)S(1)}, bf16[128,1024]{1,0:T(8,128)(2,1)}, u32[]{:S(2)}) copy-start(bf16[128,1024]{1,0:T(8,128)(2,1)} %rows.1) | copy-start | bytes 786436
  3.2 0.9 %copy-start.7 = (bf16[128,512]{1,0:T(8,128)(2,1)S(1)}, bf16[128,512]{1,0:T(8,128)(2,1)}, u32[]{:S(2)}) copy-start(bf16[128,512]{1,0:T(8,128)(2,1)} %queries.1) | copy-start | bytes 393220
  4.1 0.9 %copy-start.8 = (bf16[128,512]{1,0:T(8,128)(2,1)S(1)}, bf16[128,512]{1,0:T(8,128)(2,1)}, u32[]{:S(2)}) copy-start(bf16[128,512]{1,0:T(8,128)(2,1)} %cot.1) | copy-start | bytes 393220
  5.3 15.3 %collective-permute-start = (bf16[144,512]{1,0:T(8,128)(2,1)S(1)}, bf16[144,512]{1,0:T(8,128)(2,1)S(1)}, u32[]{:S(2)}, u32[]{:S(2)}) collective-permute-start(bf16[144,512]{1,0:T(8,128)(2,1)S(1)} %get-tuple-element.56.rows_1), channel_id=1, source_target_pairs={{0,16},{2,18},{4,20},{6,22},{8,24},{10,26},{12,28},{14,30},{16,0},... | collective-permute-start | bytes 442376 | tf_op jit(solution)/shard_map/ppermute | solution.py:577
  9.4 9.6 %collective-permute-start.1 = (bf16[560,128]{1,0:T(8,128)(2,1)S(1)}, bf16[560,128]{1,0:T(8,128)(2,1)S(1)}, u32[]{:S(2)}, u32[]{:S(2)}) collective-permute-start(bf16[560,128]{1,0:T(8,128)(2,1)S(1)} %get-tuple-element.57), channel_id=1, source_target_pairs={{0,10},{2,8},{4,14},{6,12},{8,2},{10,0},{12,6},{14,4},{16,26},{18,... | collective-permute-start | bytes 430088 | tf_op jit(solution)/shard_map/ppermute | solution.py:577
  11.9 8.7 %collective-permute-start.2 = (bf16[560,128]{1,0:T(8,128)(2,1)S(1)}, bf16[560,128]{1,0:T(8,128)(2,1)S(1)}, u32[]{:S(2)}, u32[]{:S(2)}) collective-permute-start(bf16[560,128]{1,0:T(8,128)(2,1)S(1)} %get-tuple-element.58), channel_id=1, source_target_pairs={{0,8},{2,10},{4,12},{6,14},{8,0},{10,2},{12,4},{14,6},{16,24},{18,... | collective-permute-start | bytes 430088 | tf_op jit(solution)/shard_map/ppermute | solution.py:577
  12.4 8.3 %collective-permute-start.3 = (bf16[560,128]{1,0:T(8,128)(2,1)S(1)}, bf16[560,128]{1,0:T(8,128)(2,1)S(1)}, u32[]{:S(2)}, u32[]{:S(2)}) collective-permute-start(bf16[560,128]{1,0:T(8,128)(2,1)S(1)} %get-tuple-element.59), channel_id=1, source_target_pairs={{0,2},{2,0},{4,6},{6,4},{8,10},{10,8},{12,14},{14,12},{16,18},{18,... | collective-permute-start | bytes 430088 | tf_op jit(solution)/shard_map/ppermute | solution.py:577
  20.7 9.3 %collective-permute-start.4 = (bf16[4,272,128]{2,1,0:T(8,128)(2,1)S(1)}, bf16[4,272,128]{2,1,0:T(8,128)(2,1)S(1)}, u32[]{:S(2)}, u32[]{:S(2)}) collective-permute-start(bf16[4,272,128]{2,1,0:T(8,128)(2,1)S(1)} %get-tuple-element.64.near_own), channel_id=1, source_target_pairs={{0,4},{2,6},{4,0},{6,2},{8,12},{10,14},{12,8},{14,10},{16,20},{18,... | collective-permute-start | bytes 835592 | tf_op jit(solution)/shard_map/ppermute | solution.py:589
  22.3 10.2 %collective-permute-start.5 = (bf16[4,288,128]{2,1,0:T(8,128)(2,1)S(1)}, bf16[4,288,128]{2,1,0:T(8,128)(2,1)S(1)}, u32[]{:S(2)}, u32[]{:S(2)}) collective-permute-start(bf16[4,288,128]{2,1,0:T(8,128)(2,1)S(1)} %get-tuple-element.65.far_own), channel_id=1, source_target_pairs={{0,16},{2,18},{4,20},{6,22},{8,24},{10,26},{12,28},{14,30},{17,1},... | collective-permute-start | bytes 884744 | tf_op jit(solution)/shard_map/ppermute | solution.py:588
  24.8 9.1 %collective-permute-start.6 = (bf16[256,512]{1,0:T(8,128)(2,1)S(1)}, bf16[256,512]{1,0:T(8,128)(2,1)S(1)}, u32[]{:S(2)}, u32[]{:S(2)}) collective-permute-start(bf16[256,512]{1,0:T(8,128)(2,1)S(1)} %get-tuple-element.71.refs_0_), channel_id=1, source_target_pairs={{0,8},{2,10},{4,12},{6,14},{8,0},{10,2},{12,4},{14,6},{16,24},{18,... | collective-permute-start | bytes 786440 | tf_op jit(solution)/shard_map/ppermute | solution.py:577
  27.4 6.6 %collective-permute-start.7 = (bf16[256,512]{1,0:T(8,128)(2,1)S(1)}, bf16[256,512]{1,0:T(8,128)(2,1)S(1)}, u32[]{:S(2)}, u32[]{:S(2)}) collective-permute-start(bf16[256,512]{1,0:T(8,128)(2,1)S(1)} %get-tuple-element.71.refs_0_), channel_id=1, source_target_pairs={{0,2},{2,0},{4,6},{6,4},{8,10},{10,8},{12,14},{14,12},{16,18},{18,... | collective-permute-start | bytes 786440 | tf_op jit(solution)/shard_map/ppermute | solution.py:577
  27.9 6.4 %collective-permute-start.8 = (bf16[256,512]{1,0:T(8,128)(2,1)S(1)}, bf16[256,512]{1,0:T(8,128)(2,1)S(1)}, u32[]{:S(2)}, u32[]{:S(2)}) collective-permute-start(bf16[256,512]{1,0:T(8,128)(2,1)S(1)} %get-tuple-element.71.refs_0_), channel_id=1, source_target_pairs={{0,4},{2,6},{4,0},{6,2},{8,12},{10,14},{12,8},{14,10},{16,20},{18,... | collective-permute-start | bytes 786440 | tf_op jit(solution)/shard_map/ppermute | solution.py:577
  32.6 23.5 %copy-start = (bf16[3,1024,512]{2,1,0:T(8,128)(2,1)S(1)}, bf16[3,1024,512]{2,1,0:T(8,128)(2,1)}, u32[]{:S(2)}) copy-start(bf16[3,1024,512]{2,1,0:T(8,128)(2,1)} %weight.1) | copy-start | bytes 9437188
  34.3 12.3 %collective-permute-start.9 = (bf16[4,272,128]{2,1,0:T(8,128)(2,1)S(1)}, bf16[4,272,128]{2,1,0:T(8,128)(2,1)S(1)}, u32[]{:S(2)}, u32[]{:S(2)}) collective-permute-start(bf16[4,272,128]{2,1,0:T(8,128)(2,1)S(1)} %get-tuple-element.72), channel_id=1, source_target_pairs={{16,0},{18,2},{20,4},{22,6},{24,8},{26,10},{28,12},{30,14},{1,17},... | collective-permute-start | bytes 835592 | tf_op jit(solution)/shard_map/ppermute | solution.py:624
  35.8 8.3 %collective-permute-start.10 = (bf16[4,2,128,128]{3,2,1,0:T(8,128)(2,1)S(1)}, bf16[4,2,128,128]{3,2,1,0:T(8,128)(2,1)S(1)}, u32[]{:S(2)}, u32[]{:S(2)}) collective-permute-start(bf16[4,2,128,128]{3,2,1,0:T(8,128)(2,1)S(1)} %near.1), channel_id=1, source_target_pairs={{0,4},{2,6},{4,0},{6,2},{8,12},{10,14},{12,8},{14,10},{16,20},{18,... | collective-permute-start | bytes 786440 | tf_op jit(solution)/shard_map/ppermute | solution.py:625
  37.1 9.6 %collective-permute-start.11 = (bf16[256,512]{1,0:T(8,128)(2,1)S(1)}, bf16[256,512]{1,0:T(8,128)(2,1)S(1)}, u32[]{:S(2)}, u32[]{:S(2)}) collective-permute-start(bf16[256,512]{1,0:T(8,128)(2,1)S(1)} %collective-permute-done.6.refs_1_), channel_id=1, source_target_pairs={{0,2},{2,0},{4,6},{6,4},{8,10},{10,8},{12,14},{14,12},{16,18},{18,... | collective-permute-start | bytes 786440 | tf_op jit(solution)/shard_map/ppermute | solution.py:577
  37.9 13.8 %collective-permute-start.15 = (bf16[256,512]{1,0:T(8,128)(2,1)S(1)}, bf16[256,512]{1,0:T(8,128)(2,1)S(1)}, u32[]{:S(2)}, u32[]{:S(2)}) collective-permute-start(bf16[256,512]{1,0:T(8,128)(2,1)S(1)} %collective-permute-done.6.refs_1_), channel_id=1, source_target_pairs={{0,4},{2,6},{4,0},{6,2},{8,12},{10,14},{12,8},{14,10},{16,20},{18,... | collective-permute-start | bytes 786440 | tf_op jit(solution)/shard_map/ppermute | solution.py:577
  46.6 11.0 %copy-start.9 = (s32[128,1]{0,1:T(1,128)S(1)}, s32[128,1]{0,1:T(1,128)}, u32[]{:S(2)}) copy-start(s32[128,1]{0,1:T(1,128)} %param.19) | copy-start | bytes 1540
  46.6 11.0 %copy-start.10 = (s32[128]{0:T(128)S(1)}, s32[128]{0:T(128)}, u32[]{:S(2)}) copy-start(s32[128]{0:T(128)} %param.20) | copy-start | bytes 1540
  46.7 14.0 %copy-start.1 = (bf16[1024,512]{1,0:T(8,128)(2,1)S(1)}, bf16[1024,512]{1,0:T(8,128)(2,1)}, u32[]{:S(2)}) copy-start(bf16[1024,512]{1,0:T(8,128)(2,1)} %adapter.1) | copy-start | bytes 3145732
  46.8 9.3 %collective-permute-start.16 = (bf16[256,512]{1,0:T(8,128)(2,1)S(1)}, bf16[256,512]{1,0:T(8,128)(2,1)S(1)}, u32[]{:S(2)}, u32[]{:S(2)}) collective-permute-start(bf16[256,512]{1,0:T(8,128)(2,1)S(1)} %collective-permute-done.11.refs_3_), channel_id=1, source_target_pairs={{0,4},{2,6},{4,0},{6,2},{8,12},{10,14},{12,8},{14,10},{16,20},{18,... | collective-permute-start | bytes 786440 | tf_op jit(solution)/shard_map/ppermute | solution.py:577
  48.1 5.6 %collective-permute-start.12 = (bf16[3,128,128]{2,1,0:T(8,128)(2,1)S(1)}, bf16[3,128,128]{2,1,0:T(8,128)(2,1)S(1)}, u32[]{:S(2)}, u32[]{:S(2)}) collective-permute-start(bf16[3,128,128]{2,1,0:T(8,128)(2,1)S(1)} %merge_both.1), channel_id=1, source_target_pairs={{0,10},{2,8},{4,14},{6,12},{8,2},{10,0},{12,6},{14,4},{16,26},{18,... | collective-permute-start | bytes 294920 | tf_op jit(solution)/shard_map/ppermute | solution.py:577
  48.2 6.5 %collective-permute-start.13 = (bf16[3,128,128]{2,1,0:T(8,128)(2,1)S(1)}, bf16[3,128,128]{2,1,0:T(8,128)(2,1)S(1)}, u32[]{:S(2)}, u32[]{:S(2)}) collective-permute-start(bf16[3,128,128]{2,1,0:T(8,128)(2,1)S(1)} %get-tuple-element.86), channel_id=1, source_target_pairs={{0,8},{2,10},{4,12},{6,14},{8,0},{10,2},{12,4},{14,6},{16,24},{18,... | collective-permute-start | bytes 294920 | tf_op jit(solution)/shard_map/ppermute | solution.py:577
  50.3 5.7 %collective-permute-start.14 = (bf16[3,128,128]{2,1,0:T(8,128)(2,1)S(1)}, bf16[3,128,128]{2,1,0:T(8,128)(2,1)S(1)}, u32[]{:S(2)}, u32[]{:S(2)}) collective-permute-start(bf16[3,128,128]{2,1,0:T(8,128)(2,1)S(1)} %get-tuple-element.87), channel_id=1, source_target_pairs={{0,2},{2,0},{4,6},{6,4},{8,10},{10,8},{12,14},{14,12},{16,18},{18,... | collective-permute-start | bytes 294920 | tf_op jit(solution)/shard_map/ppermute | solution.py:577
  51.6 9.0 %collective-permute-start.18 = (bf16[256,512]{1,0:T(8,128)(2,1)S(1)}, bf16[256,512]{1,0:T(8,128)(2,1)S(1)}, u32[]{:S(2)}, u32[]{:S(2)}) collective-permute-start(bf16[256,512]{1,0:T(8,128)(2,1)S(1)} %collective-permute-done.8.refs_4_), channel_id=1, source_target_pairs={{0,2},{2,0},{4,6},{6,4},{8,10},{10,8},{12,14},{14,12},{16,18},{18,... | collective-permute-start | bytes 786440 | tf_op jit(solution)/shard_map/ppermute | solution.py:577
  56.1 22.6 %copy-start.2 = (f32[256,512]{1,0:T(8,128)S(1)}, f32[256,512]{1,0:T(8,128)}, u32[]{:S(2)}) copy-start(f32[256,512]{1,0:T(8,128)} %refs_8_.1) | copy-start | bytes 1572868
  56.1 22.6 %copy-start.3 = (f32[256,512]{1,0:T(8,128)S(1)}, f32[256,512]{1,0:T(8,128)}, u32[]{:S(2)}) copy-start(f32[256,512]{1,0:T(8,128)} %refs_9_.1) | copy-start | bytes 1572868
  56.1 22.6 %copy-start.4 = (f32[256,512]{1,0:T(8,128)S(1)}, f32[256,512]{1,0:T(8,128)}, u32[]{:S(2)}) copy-start(f32[256,512]{1,0:T(8,128)} %refs_10_.1) | copy-start | bytes 1572868
  57.3 3.4 %collective-permute-start.17 = (bf16[128,1024]{1,0:T(8,128)(2,1)S(1)}, bf16[128,1024]{1,0:T(8,128)(2,1)S(1)}, u32[]{:S(2)}, u32[]{:S(2)}) collective-permute-start(bf16[128,1024]{1,0:T(8,128)(2,1)S(1)} %get-tuple-element.95), channel_id=1, source_target_pairs={{0,1},{1,0},{2,3},{3,2},{4,5},{5,4},{6,7},{7,6},{8,9},{9,8},{10,11... | collective-permute-start | bytes 786440 | tf_op jit(solution)/shard_map/ppermute | solution.py:651
  77.3 1.4 %collective-permute-start.19 = (bf16[16,32,128]{2,1,0:T(8,128)(2,1)S(1)}, bf16[16,32,128]{2,1,0:T(8,128)(2,1)S(1)}, u32[]{:S(2)}, u32[]{:S(2)}) collective-permute-start(bf16[16,32,128]{2,1,0:T(8,128)(2,1)S(1)} %slice.4), channel_id=1, source_target_pairs={{0,1},{1,0},{2,3},{3,2},{4,5},{5,4},{6,7},{7,6},{8,9},{9,8},{10,11... | collective-permute-start | bytes 393224 | tf_op jit(solution)/shard_map/ppermute | solution.py:665

commit v5 on v4

--- a/solution.py
+++ b/solution.py
@@ -649,7 +649,6 @@
         "place",
     )
     other = lax.ppermute(sent, "head", SWAP)
-    other, x_y_rows = lax.optimization_barrier((other, x_y_rows))
     share = width // n_ctx // 2
     packed_rows = capacity * (head_cols // BLOCK + 1)
     packed = pl.pallas_call(

time: 81.8 us -> 84.6 us (1.034)
  blocking collectives: 16.1 us -> 0 us
  waiting for transfers between devices: 26.2 us -> 36.9 us
  starting transfers between devices: 26.3 us -> 30.9 us
  local copies, waits for them, and re-layouts: 3.75 us -> 6.35 us
    all_to_all x1 -> x0, blocking collectives: 16.1 us -> none  [dealt_device(): got = lax.all_to_all(packed, 'ctx', 0, 0, tiled=True)]
    all_to_all x0 -> x1, waiting for transfers between devices: none -> 12.4 us  [dealt_device(): got = lax.all_to_all(packed, 'ctx', 0, 0, tiled=True)]
    all_to_all x0 -> x1, starting transfers between devices: none -> 3.56 us  [dealt_device(): got = lax.all_to_all(packed, 'ctx', 0, 0, tiled=True)]
    ppermute x14, waiting for transfers between devices: 16 us -> 13.2 us  [exchange(): return lax.ppermute(sent, 'ctx', [(i, i ^ bit) for i in range(16)])]
    unnamed x22 -> x30, local copies, waits for them, and re-layouts: 3.74 us -> 6.34 us
    ppermute x1, waiting for transfers between devices: 0.01 us -> 1.23 us  [dealt_device(): other = lax.ppermute(sent, 'head', SWAP)]
    ppermute x14, starting transfers between devices: 19 us -> 20.1 us  [exchange(): return lax.ppermute(sent, 'ctx', [(i, i ^ bit) for i in range(16)])]
  transfers between devices with their start and end apart: 20 -> 21, of which waited for: 13 -> 14; matrix products, arithmetic and copies ran while one was open for 0% -> 0% of each run, Pallas kernels for 5% -> 3%
where the time goes in v5:
time: 84.6 us; the launch traced here: 84.2 us
  waiting for transfers between devices  36.9 us (44%)
  starting transfers between devices  30.9 us (37%)
  Pallas kernels  8.35 us (10%)
  local copies, waits for them, and re-layouts  6.35 us (8%)
  between operations  1.66 us (2%)
    ppermute x14, starting transfers between devices, exchange(): return lax.ppermute(sent, 'ctx', [(i, i ^ bit) for i in range(16)])  20.1 us
    ppermute x14, waiting for transfers between devices, exchange(): return lax.ppermute(sent, 'ctx', [(i, i ^ bit) for i in range(16)])  13.2 us
    all_to_all x1, waiting for transfers between devices, dealt_device(): got = lax.all_to_all(packed, 'ctx', 0, 0, tiled=True)  12.4 us
    unnamed x30, local copies, waits for them, and re-layouts  6.34 us
    ppermute x1, waiting for transfers between devices, dealt_device(): near_back = lax.ppermute(near_out, 'ctx', ACROSS_Y)  4.69 us
    all_to_all x1, starting transfers between devices, dealt_device(): got = lax.all_to_all(packed, 'ctx', 0, 0, tiled=True)  3.56 us
    pallas_call x1, Pallas kernels, dealt_device(): pl.pallas_call(finish_body, out_shape=(shape((width // n_ctx, head_cols),...  2.6 us
    ppermute x1, waiting for transfers between devices, dealt_device(): far_back = lax.ppermute(far_out, ('ctx', 'head'), FAR_BACK)  2.53 us
  transfers between devices with their start and end apart: 21, of which 14 were waited for; matrix products, arithmetic and copies ran while one was open for 0% of the time, Pallas kernels for 3%

profile of v5, /device:TPU:0, one launch (start us, length us, event | category | flops | bytes accessed | tf_op | source)
XLA Modules:
  0.0 84.2 jit_solution(14915144443849368728)
XLA Ops:
  1.3 0.9 %copy-done.9 = bf16[2,128,512]{2,1,0:T(8,128)(2,1)S(1)} copy-done((bf16[2,128,512]{2,1,0:T(8,128)(2,1)S(1)}, bf16[2,128,512]{2,1,0:T(8,128)(2,1)}, u32[]{:S(2)}) %copy-start.9) | copy-done | bytes 262168
  2.2 0.9 %copy-done.10 = bf16[128,1024]{1,0:T(8,128)(2,1)S(1)} copy-done((bf16[128,1024]{1,0:T(8,128)(2,1)S(1)}, bf16[128,1024]{1,0:T(8,128)(2,1)}, u32[]{:S(2)}) %copy-start.10) | copy-done | bytes 262168
  3.2 0.9 %copy-done.11 = bf16[128,512]{1,0:T(8,128)(2,1)S(1)} copy-done((bf16[128,512]{1,0:T(8,128)(2,1)S(1)}, bf16[128,512]{1,0:T(8,128)(2,1)}, u32[]{:S(2)}) %copy-start.11) | copy-done | bytes 131096
  4.1 0.9 %copy-done.12 = bf16[128,512]{1,0:T(8,128)(2,1)S(1)} copy-done((bf16[128,512]{1,0:T(8,128)(2,1)S(1)}, bf16[128,512]{1,0:T(8,128)(2,1)}, u32[]{:S(2)}) %copy-start.12) | copy-done | bytes 131096
  5.0 0.3 deal.1
  5.3 4.1 %collective-permute-start = (bf16[144,512]{1,0:T(8,128)(2,1)S(1)}, bf16[144,512]{1,0:T(8,128)(2,1)S(1)}, u32[]{:S(2)}, u32[]{:S(2)}) collective-permute-start(bf16[144,512]{1,0:T(8,128)(2,1)S(1)} %get-tuple-element.54.rows_1), channel_id=1, source_target_pairs={{0,16},{2,18},{4,20},{6,22},{8,24},{10,26},{12,28},{14,30},{16,0},... | collective-permute-start | bytes 442376 | tf_op jit(solution)/shard_map/ppermute | solution.py:577
  9.4 2.5 %collective-permute-start.1 = (bf16[560,128]{1,0:T(8,128)(2,1)S(1)}, bf16[560,128]{1,0:T(8,128)(2,1)S(1)}, u32[]{:S(2)}, u32[]{:S(2)}) collective-permute-start(bf16[560,128]{1,0:T(8,128)(2,1)S(1)} %get-tuple-element.55), channel_id=1, source_target_pairs={{0,10},{2,8},{4,14},{6,12},{8,2},{10,0},{12,6},{14,4},{16,26},{18,... | collective-permute-start | bytes 430088 | tf_op jit(solution)/shard_map/ppermute | solution.py:577
  11.9 0.4 collective-permute-start.2
  12.4 0.5 collective-permute-start.3
  12.9 6.1 %collective-permute-done.1.by_both = bf16[560,128]{1,0:T(8,128)(2,1)S(1)} collective-permute-done((bf16[560,128]{1,0:T(8,128)(2,1)S(1)}, bf16[560,128]{1,0:T(8,128)(2,1)S(1)}, u32[]{:S(2)}, u32[]{:S(2)}) %collective-permute-start.1) | collective-permute-done | bytes 143392 | tf_op jit(solution)/shard_map/ppermute | solution.py:577
  19.0 1.6 %collective-permute-done.2.by_zl = bf16[560,128]{1,0:T(8,128)(2,1)S(1)} collective-permute-done((bf16[560,128]{1,0:T(8,128)(2,1)S(1)}, bf16[560,128]{1,0:T(8,128)(2,1)S(1)}, u32[]{:S(2)}, u32[]{:S(2)}) %collective-permute-start.2) | collective-permute-done | bytes 143392 | tf_op jit(solution)/shard_map/ppermute | solution.py:577
  20.6 0.0 collective-permute-done.3.by_x
  20.6 0.0 collective-permute-done.rows_2
  20.6 0.1 gather.1
  20.7 1.6 %collective-permute-start.4 = (bf16[4,272,128]{2,1,0:T(8,128)(2,1)S(1)}, bf16[4,272,128]{2,1,0:T(8,128)(2,1)S(1)}, u32[]{:S(2)}, u32[]{:S(2)}) collective-permute-start(bf16[4,272,128]{2,1,0:T(8,128)(2,1)S(1)} %get-tuple-element.62.near_own), channel_id=1, source_target_pairs={{0,4},{2,6},{4,0},{6,2},{8,12},{10,14},{12,8},{14,10},{16,20},{18,... | collective-permute-start | bytes 835592 | tf_op jit(solution)/shard_map/ppermute | solution.py:589
  22.3 2.5 %collective-permute-start.5 = (bf16[4,288,128]{2,1,0:T(8,128)(2,1)S(1)}, bf16[4,288,128]{2,1,0:T(8,128)(2,1)S(1)}, u32[]{:S(2)}, u32[]{:S(2)}) collective-permute-start(bf16[4,288,128]{2,1,0:T(8,128)(2,1)S(1)} %get-tuple-element.63.far_own), channel_id=1, source_target_pairs={{0,16},{2,18},{4,20},{6,22},{8,24},{10,26},{12,28},{14,30},{17,1},... | collective-permute-start | bytes 884744 | tf_op jit(solution)/shard_map/ppermute | solution.py:588
  24.8 2.5 %collective-permute-start.6 = (bf16[256,512]{1,0:T(8,128)(2,1)S(1)}, bf16[256,512]{1,0:T(8,128)(2,1)S(1)}, u32[]{:S(2)}, u32[]{:S(2)}) collective-permute-start(bf16[256,512]{1,0:T(8,128)(2,1)S(1)} %get-tuple-element.69.refs_0_), channel_id=1, source_target_pairs={{0,8},{2,10},{4,12},{6,14},{8,0},{10,2},{12,4},{14,6},{16,24},{18,... | collective-permute-start | bytes 786440 | tf_op jit(solution)/shard_map/ppermute | solution.py:577
  27.4 0.5 collective-permute-start.7
  27.9 0.5 collective-permute-start.8
  28.4 1.6 %collective-permute-done.4.near_in = bf16[4,272,128]{2,1,0:T(8,128)(2,1)S(1)} collective-permute-done((bf16[4,272,128]{2,1,0:T(8,128)(2,1)S(1)}, bf16[4,272,128]{2,1,0:T(8,128)(2,1)S(1)}, u32[]{:S(2)}, u32[]{:S(2)}) %collective-permute-start.4) | collective-permute-done | bytes 278560 | tf_op jit(solution)/shard_map/ppermute | solution.py:589
  30.0 2.5 %attend_own.1 = (f32[1024,128]{1,0:T(8,128)S(1)}, f32[1024,128]{1,0:T(8,128)S(1)}, f32[2,512,128]{2,1,0:T(8,128)S(1)}) custom-call(bf16[4,272,128]{2,1,0:T(8,128)(2,1)S(1)} %get-tuple-element.62.near_own, bf16[4,288,128]{2,1,0:T(8,128)(2,1)S(1)} %get-tuple-element.63.far_own, bf16[4,272,128]{2,1,0:T(8,128)(2,1)S(1)} %collective-permute-done.4.near_in), custom_call_target="tpu_custom_call" | custom-call | flops 1000000000 | bytes 1048576 | tf_op jit(solution)/shard_map/attend_own/pallas_call | solution.py:595
  32.5 0.0 collective-permute-done.5.far_in
  32.6 0.0 copy-start
  32.6 1.3 %collective-permute-done.6.refs_1_ = bf16[256,512]{1,0:T(8,128)(2,1)S(1)} collective-permute-done((bf16[256,512]{1,0:T(8,128)(2,1)S(1)}, bf16[256,512]{1,0:T(8,128)(2,1)S(1)}, u32[]{:S(2)}, u32[]{:S(2)}) %collective-permute-start.6) | collective-permute-done | bytes 262176 | tf_op jit(solution)/shard_map/ppermute | solution.py:577
  33.9 0.0 collective-permute-done.7.refs_2_
  33.9 0.4 collective-permute-done.8.refs_4_
  34.3 1.5 %collective-permute-start.9 = (bf16[4,272,128]{2,1,0:T(8,128)(2,1)S(1)}, bf16[4,272,128]{2,1,0:T(8,128)(2,1)S(1)}, u32[]{:S(2)}, u32[]{:S(2)}) collective-permute-start(bf16[4,272,128]{2,1,0:T(8,128)(2,1)S(1)} %get-tuple-element.70), channel_id=1, source_target_pairs={{16,0},{18,2},{20,4},{22,6},{24,8},{26,10},{28,12},{30,14},{1,17},... | collective-permute-start | bytes 835592 | tf_op jit(solution)/shard_map/ppermute | solution.py:624
  35.8 1.3 %collective-permute-start.10 = (bf16[4,2,128,128]{3,2,1,0:T(8,128)(2,1)S(1)}, bf16[4,2,128,128]{3,2,1,0:T(8,128)(2,1)S(1)}, u32[]{:S(2)}, u32[]{:S(2)}) collective-permute-start(bf16[4,2,128,128]{3,2,1,0:T(8,128)(2,1)S(1)} %near.1), channel_id=1, source_target_pairs={{0,4},{2,6},{4,0},{6,2},{8,12},{10,14},{12,8},{14,10},{16,20},{18,... | collective-permute-start | bytes 786440 | tf_op jit(solution)/shard_map/ppermute | solution.py:625
  37.1 0.7 collective-permute-start.11
  37.9 1.5 %collective-permute-start.15 = (bf16[256,512]{1,0:T(8,128)(2,1)S(1)}, bf16[256,512]{1,0:T(8,128)(2,1)S(1)}, u32[]{:S(2)}, u32[]{:S(2)}) collective-permute-start(bf16[256,512]{1,0:T(8,128)(2,1)S(1)} %collective-permute-done.6.refs_1_), channel_id=1, source_target_pairs={{0,4},{2,6},{4,0},{6,2},{8,12},{10,14},{12,8},{14,10},{16,20},{18,... | collective-permute-start | bytes 786440 | tf_op jit(solution)/shard_map/ppermute | solution.py:577
  39.4 4.7 %collective-permute-done.10.near = bf16[4,2,128,128]{3,2,1,0:T(8,128)(2,1)S(1)} collective-permute-done((bf16[4,2,128,128]{3,2,1,0:T(8,128)(2,1)S(1)}, bf16[4,2,128,128]{3,2,1,0:T(8,128)(2,1)S(1)}, u32[]{:S(2)}, u32[]{:S(2)}) %collective-permute-start.10) | collective-permute-done | bytes 262176 | tf_op jit(solution)/shard_map/ppermute | solution.py:625
  44.1 2.5 %collective-permute-done.9.far = bf16[4,272,128]{2,1,0:T(8,128)(2,1)S(1)} collective-permute-done((bf16[4,272,128]{2,1,0:T(8,128)(2,1)S(1)}, bf16[4,272,128]{2,1,0:T(8,128)(2,1)S(1)}, u32[]{:S(2)}, u32[]{:S(2)}) %collective-permute-start.9) | collective-permute-done | bytes 278560 | tf_op jit(solution)/shard_map/ppermute | solution.py:624
  46.6 0.0 copy-start.13
  46.6 0.0 copy-start.14
  46.7 0.0 copy-start.1
  46.7 0.1 merge.1
  46.8 0.0 collective-permute-done.11.refs_3_
  46.8 1.3 %collective-permute-start.16 = (bf16[256,512]{1,0:T(8,128)(2,1)S(1)}, bf16[256,512]{1,0:T(8,128)(2,1)S(1)}, u32[]{:S(2)}, u32[]{:S(2)}) collective-permute-start(bf16[256,512]{1,0:T(8,128)(2,1)S(1)} %collective-permute-done.11.refs_3_), channel_id=1, source_target_pairs={{0,4},{2,6},{4,0},{6,2},{8,12},{10,14},{12,8},{14,10},{16,20},{18,... | collective-permute-start | bytes 786440 | tf_op jit(solution)/shard_map/ppermute | solution.py:577
  48.1 0.0 collective-permute-start.12
  48.2 2.1 %collective-permute-start.13 = (bf16[3,128,128]{2,1,0:T(8,128)(2,1)S(1)}, bf16[3,128,128]{2,1,0:T(8,128)(2,1)S(1)}, u32[]{:S(2)}, u32[]{:S(2)}) collective-permute-start(bf16[3,128,128]{2,1,0:T(8,128)(2,1)S(1)} %get-tuple-element.84), channel_id=1, source_target_pairs={{0,8},{2,10},{4,12},{6,14},{8,0},{10,2},{12,4},{14,6},{16,24},{18,... | collective-permute-start | bytes 294920 | tf_op jit(solution)/shard_map/ppermute | solution.py:577
  50.3 1.3 %collective-permute-start.14 = (bf16[3,128,128]{2,1,0:T(8,128)(2,1)S(1)}, bf16[3,128,128]{2,1,0:T(8,128)(2,1)S(1)}, u32[]{:S(2)}, u32[]{:S(2)}) collective-permute-start(bf16[3,128,128]{2,1,0:T(8,128)(2,1)S(1)} %get-tuple-element.85), channel_id=1, source_target_pairs={{0,2},{2,0},{4,6},{6,4},{8,10},{10,8},{12,14},{14,12},{16,18},{18,... | collective-permute-start | bytes 294920 | tf_op jit(solution)/shard_map/ppermute | solution.py:577
  51.6 0.0 collective-permute-done.15.refs_5_
  51.6 0.7 copy-done.5
  52.3 1.4 %collective-permute-done.12.by_both = bf16[3,128,128]{2,1,0:T(8,128)(2,1)S(1)} collective-permute-done((bf16[3,128,128]{2,1,0:T(8,128)(2,1)S(1)}, bf16[3,128,128]{2,1,0:T(8,128)(2,1)S(1)}, u32[]{:S(2)}, u32[]{:S(2)}) %collective-permute-start.12) | collective-permute-done | bytes 98336 | tf_op jit(solution)/shard_map/ppermute | solution.py:577
  53.7 0.9 %collective-permute-done.13.by_zl = bf16[3,128,128]{2,1,0:T(8,128)(2,1)S(1)} collective-permute-done((bf16[3,128,128]{2,1,0:T(8,128)(2,1)S(1)}, bf16[3,128,128]{2,1,0:T(8,128)(2,1)S(1)}, u32[]{:S(2)}, u32[]{:S(2)}) %collective-permute-start.13) | collective-permute-done | bytes 98336 | tf_op jit(solution)/shard_map/ppermute | solution.py:577
  54.6 0.4 collective-permute-done.14.by_x
  55.0 1.0 %collective-permute-done.16.refs_7_ = bf16[256,512]{1,0:T(8,128)(2,1)S(1)} collective-permute-done((bf16[256,512]{1,0:T(8,128)(2,1)S(1)}, bf16[256,512]{1,0:T(8,128)(2,1)S(1)}, u32[]{:S(2)}, u32[]{:S(2)}) %collective-permute-start.16) | collective-permute-done | bytes 262176 | tf_op jit(solution)/shard_map/ppermute | solution.py:577
  56.1 0.0 copy-start.4
  56.1 1.2 %project.1 = (f32[128,1024]{1,0:T(8,128)S(1)}, bf16[128,1024]{1,0:T(8,128)(2,1)S(1)}) custom-call(bf16[3,128,128]{2,1,0:T(8,128)(2,1)S(1)} %collective-permute-done.12.by_both, bf16[3,128,128]{2,1,0:T(8,128)(2,1)S(1)} %collective-permute-done.13.by_zl, bf16[3,128,128]{2,1,0:T(8,128)(2,1)S(1)} %collective-permute-done.14.by_x, ...), custom_call_target="tpu_custom_call" | custom-call | tf_op jit(solution)/shard_map/project/pallas_call | solution.py:635
  57.3 0.2 collective-permute-start.17
  57.5 0.2 place.1
  57.7 1.2 %collective-permute-done.17.other = bf16[128,1024]{1,0:T(8,128)(2,1)S(1)} collective-permute-done((bf16[128,1024]{1,0:T(8,128)(2,1)S(1)}, bf16[128,1024]{1,0:T(8,128)(2,1)S(1)}, u32[]{:S(2)}, u32[]{:S(2)}) %collective-permute-start.17) | collective-permute-done | bytes 262176 | tf_op jit(solution)/shard_map/ppermute | solution.py:651
  58.9 1.3 %pack.1 = bf16[16,112,128]{2,1,0:T(8,128)(2,1)} custom-call(f32[128,1024]{1,0:T(8,128)S(1)} %get-tuple-element.91.own, bf16[128,1024]{1,0:T(8,128)(2,1)S(1)} %collective-permute-done.17.other, bf16[1024,512]{1,0:T(8,128)(2,1)S(1)} %copy-done.1, bf16[128,256]{1,0:T(8,128)(2,1)S(1)} %get-tuple-element.96.placing, bf16[128,128]{1,0:T(8,128)(2,1)S(1)} %get-tuple-element.97.slots), custom_call_target="tpu_custom_call" | custom-call | tf_op jit(solution)/shard_map/pack/pallas_call | solution.py:654
  60.2 3.6 %all-to-all-start = ((bf16[16,112,128]{2,1,0:T(8,128)(2,1)}), bf16[16,112,128]{2,1,0:T(8,128)(2,1)S(1)}, u32[]{:S(2)}, u32[]{:S(2)}) async-start(bf16[16,112,128]{2,1,0:T(8,128)(2,1)} %pack.1), calls=%async_computation | async-start | bytes 917504 | tf_op jit(solution)/shard_map/all_to_all | solution.py:663
  63.8 1.9 %collective-permute-start.19 = (bf16[256,512]{1,0:T(8,128)(2,1)S(1)}, bf16[256,512]{1,0:T(8,128)(2,1)}, u32[]{:S(2)}, u32[]{:S(2)}) collective-permute-start(bf16[256,512]{1,0:T(8,128)(2,1)S(1)} %collective-permute-done.8.refs_4_), channel_id=1, source_target_pairs={{0,2},{2,0},{4,6},{6,4},{8,10},{10,8},{12,14},{14,12},{16,18},{18,... | collective-permute-start | bytes 786440 | tf_op jit(solution)/shard_map/ppermute | solution.py:577
  65.6 12.4 %all-to-all-done.got = bf16[16,112,128]{2,1,0:T(8,128)(2,1)S(1)} async-done(((bf16[16,112,128]{2,1,0:T(8,128)(2,1)}), bf16[16,112,128]{2,1,0:T(8,128)(2,1)S(1)}, u32[]{:S(2)}, u32[]{:S(2)}) %all-to-all-start) | async-done | bytes 458784 | tf_op jit(solution)/shard_map/all_to_all | solution.py:663
  78.1 0.1 collective-permute-start.18
  78.1 0.0 collective-permute-done.19.refs_6_
  78.1 1.3 %collective-permute-done.18.other = bf16[16,32,128]{2,1,0:T(8,128)(2,1)S(1)} collective-permute-done((bf16[16,32,128]{2,1,0:T(8,128)(2,1)S(1)}, bf16[16,32,128]{2,1,0:T(8,128)(2,1)S(1)}, u32[]{:S(2)}, u32[]{:S(2)}) %collective-permute-start.18) | collective-permute-done | bytes 131104 | tf_op jit(solution)/shard_map/ppermute | solution.py:664
  79.5 0.0 copy-done.3
  79.5 0.0 copy-start.6
  79.5 0.9 %copy-done.6 = bf16[256,512]{1,0:T(8,128)(2,1)S(1)} copy-done((bf16[256,512]{1,0:T(8,128)(2,1)S(1)}, bf16[256,512]{1,0:T(8,128)(2,1)}, u32[]{:S(2)}) %copy-start.6) | copy-done | bytes 262168
  80.4 0.9 %copy-done.8 = bf16[256,512]{1,0:T(8,128)(2,1)S(1)} copy-done((bf16[256,512]{1,0:T(8,128)(2,1)S(1)}, bf16[256,512]{1,0:T(8,128)(2,1)}, u32[]{:S(2)}) %copy-start.8) | copy-done | bytes 262168
  81.4 2.6 %finish.1 = (f32[64,512]{1,0:T(8,128)}, f32[256,512]{1,0:T(8,128)}, f32[256,512]{1,0:T(8,128)}, f32[256,512]{1,0:T(8,128)}) custom-call(bf16[16,112,128]{2,1,0:T(8,128)(2,1)S(1)} %all-to-all-done.got, bf16[16,32,128]{2,1,0:T(8,128)(2,1)S(1)} %collective-permute-done.18.other, bf16[256,512]{1,0:T(8,128)(2,1)S(1)} %get-tuple-element.69.refs_0_, ...), custom_call_target="tpu_custom_call" | custom-call | tf_op jit(solution)/shard_map/finish/pallas_call | solution.py:667
  (20 shorter events, 0.2 us)
Async XLA Ops:
  1.3 1.0 %copy-start.9 = (bf16[2,128,512]{2,1,0:T(8,128)(2,1)S(1)}, bf16[2,128,512]{2,1,0:T(8,128)(2,1)}, u32[]{:S(2)}) copy-start(bf16[2,128,512]{2,1,0:T(8,128)(2,1)} %keys_values.1) | copy-start | bytes 786436
  2.2 0.9 %copy-start.10 = (bf16[128,1024]{1,0:T(8,128)(2,1)S(1)}, bf16[128,1024]{1,0:T(8,128)(2,1)}, u32[]{:S(2)}) copy-start(bf16[128,1024]{1,0:T(8,128)(2,1)} %rows.1) | copy-start | bytes 786436
  3.2 0.9 %copy-start.11 = (bf16[128,512]{1,0:T(8,128)(2,1)S(1)}, bf16[128,512]{1,0:T(8,128)(2,1)}, u32[]{:S(2)}) copy-start(bf16[128,512]{1,0:T(8,128)(2,1)} %queries.1) | copy-start | bytes 393220
  4.1 0.9 %copy-start.12 = (bf16[128,512]{1,0:T(8,128)(2,1)S(1)}, bf16[128,512]{1,0:T(8,128)(2,1)}, u32[]{:S(2)}) copy-start(bf16[128,512]{1,0:T(8,128)(2,1)} %cot.1) | copy-start | bytes 393220
  5.3 15.3 %collective-permute-start = (bf16[144,512]{1,0:T(8,128)(2,1)S(1)}, bf16[144,512]{1,0:T(8,128)(2,1)S(1)}, u32[]{:S(2)}, u32[]{:S(2)}) collective-permute-start(bf16[144,512]{1,0:T(8,128)(2,1)S(1)} %get-tuple-element.54.rows_1), channel_id=1, source_target_pairs={{0,16},{2,18},{4,20},{6,22},{8,24},{10,26},{12,28},{14,30},{16,0},... | collective-permute-start | bytes 442376 | tf_op jit(solution)/shard_map/ppermute | solution.py:577
  9.4 9.6 %collective-permute-start.1 = (bf16[560,128]{1,0:T(8,128)(2,1)S(1)}, bf16[560,128]{1,0:T(8,128)(2,1)S(1)}, u32[]{:S(2)}, u32[]{:S(2)}) collective-permute-start(bf16[560,128]{1,0:T(8,128)(2,1)S(1)} %get-tuple-element.55), channel_id=1, source_target_pairs={{0,10},{2,8},{4,14},{6,12},{8,2},{10,0},{12,6},{14,4},{16,26},{18,... | collective-permute-start | bytes 430088 | tf_op jit(solution)/shard_map/ppermute | solution.py:577
  11.9 8.7 %collective-permute-start.2 = (bf16[560,128]{1,0:T(8,128)(2,1)S(1)}, bf16[560,128]{1,0:T(8,128)(2,1)S(1)}, u32[]{:S(2)}, u32[]{:S(2)}) collective-permute-start(bf16[560,128]{1,0:T(8,128)(2,1)S(1)} %get-tuple-element.56), channel_id=1, source_target_pairs={{0,8},{2,10},{4,12},{6,14},{8,0},{10,2},{12,4},{14,6},{16,24},{18,... | collective-permute-start | bytes 430088 | tf_op jit(solution)/shard_map/ppermute | solution.py:577
  12.4 8.3 %collective-permute-start.3 = (bf16[560,128]{1,0:T(8,128)(2,1)S(1)}, bf16[560,128]{1,0:T(8,128)(2,1)S(1)}, u32[]{:S(2)}, u32[]{:S(2)}) collective-permute-start(bf16[560,128]{1,0:T(8,128)(2,1)S(1)} %get-tuple-element.57), channel_id=1, source_target_pairs={{0,2},{2,0},{4,6},{6,4},{8,10},{10,8},{12,14},{14,12},{16,18},{18,... | collective-permute-start | bytes 430088 | tf_op jit(solution)/shard_map/ppermute | solution.py:577
  20.7 9.3 %collective-permute-start.4 = (bf16[4,272,128]{2,1,0:T(8,128)(2,1)S(1)}, bf16[4,272,128]{2,1,0:T(8,128)(2,1)S(1)}, u32[]{:S(2)}, u32[]{:S(2)}) collective-permute-start(bf16[4,272,128]{2,1,0:T(8,128)(2,1)S(1)} %get-tuple-element.62.near_own), channel_id=1, source_target_pairs={{0,4},{2,6},{4,0},{6,2},{8,12},{10,14},{12,8},{14,10},{16,20},{18,... | collective-permute-start | bytes 835592 | tf_op jit(solution)/shard_map/ppermute | solution.py:589
  22.3 10.2 %collective-permute-start.5 = (bf16[4,288,128]{2,1,0:T(8,128)(2,1)S(1)}, bf16[4,288,128]{2,1,0:T(8,128)(2,1)S(1)}, u32[]{:S(2)}, u32[]{:S(2)}) collective-permute-start(bf16[4,288,128]{2,1,0:T(8,128)(2,1)S(1)} %get-tuple-element.63.far_own), channel_id=1, source_target_pairs={{0,16},{2,18},{4,20},{6,22},{8,24},{10,26},{12,28},{14,30},{17,1},... | collective-permute-start | bytes 884744 | tf_op jit(solution)/shard_map/ppermute | solution.py:588
  24.8 9.1 %collective-permute-start.6 = (bf16[256,512]{1,0:T(8,128)(2,1)S(1)}, bf16[256,512]{1,0:T(8,128)(2,1)S(1)}, u32[]{:S(2)}, u32[]{:S(2)}) collective-permute-start(bf16[256,512]{1,0:T(8,128)(2,1)S(1)} %get-tuple-element.69.refs_0_), channel_id=1, source_target_pairs={{0,8},{2,10},{4,12},{6,14},{8,0},{10,2},{12,4},{14,6},{16,24},{18,... | collective-permute-start | bytes 786440 | tf_op jit(solution)/shard_map/ppermute | solution.py:577
  27.4 6.6 %collective-permute-start.7 = (bf16[256,512]{1,0:T(8,128)(2,1)S(1)}, bf16[256,512]{1,0:T(8,128)(2,1)S(1)}, u32[]{:S(2)}, u32[]{:S(2)}) collective-permute-start(bf16[256,512]{1,0:T(8,128)(2,1)S(1)} %get-tuple-element.69.refs_0_), channel_id=1, source_target_pairs={{0,2},{2,0},{4,6},{6,4},{8,10},{10,8},{12,14},{14,12},{16,18},{18,... | collective-permute-start | bytes 786440 | tf_op jit(solution)/shard_map/ppermute | solution.py:577
  27.9 6.4 %collective-permute-start.8 = (bf16[256,512]{1,0:T(8,128)(2,1)S(1)}, bf16[256,512]{1,0:T(8,128)(2,1)S(1)}, u32[]{:S(2)}, u32[]{:S(2)}) collective-permute-start(bf16[256,512]{1,0:T(8,128)(2,1)S(1)} %get-tuple-element.69.refs_0_), channel_id=1, source_target_pairs={{0,4},{2,6},{4,0},{6,2},{8,12},{10,14},{12,8},{14,10},{16,20},{18,... | collective-permute-start | bytes 786440 | tf_op jit(solution)/shard_map/ppermute | solution.py:577
  32.6 23.5 %copy-start = (bf16[3,1024,512]{2,1,0:T(8,128)(2,1)S(1)}, bf16[3,1024,512]{2,1,0:T(8,128)(2,1)}, u32[]{:S(2)}) copy-start(bf16[3,1024,512]{2,1,0:T(8,128)(2,1)} %weight.1) | copy-start | bytes 9437188
  34.3 12.3 %collective-permute-start.9 = (bf16[4,272,128]{2,1,0:T(8,128)(2,1)S(1)}, bf16[4,272,128]{2,1,0:T(8,128)(2,1)S(1)}, u32[]{:S(2)}, u32[]{:S(2)}) collective-permute-start(bf16[4,272,128]{2,1,0:T(8,128)(2,1)S(1)} %get-tuple-element.70), channel_id=1, source_target_pairs={{16,0},{18,2},{20,4},{22,6},{24,8},{26,10},{28,12},{30,14},{1,17},... | collective-permute-start | bytes 835592 | tf_op jit(solution)/shard_map/ppermute | solution.py:624
  35.8 8.3 %collective-permute-start.10 = (bf16[4,2,128,128]{3,2,1,0:T(8,128)(2,1)S(1)}, bf16[4,2,128,128]{3,2,1,0:T(8,128)(2,1)S(1)}, u32[]{:S(2)}, u32[]{:S(2)}) collective-permute-start(bf16[4,2,128,128]{3,2,1,0:T(8,128)(2,1)S(1)} %near.1), channel_id=1, source_target_pairs={{0,4},{2,6},{4,0},{6,2},{8,12},{10,14},{12,8},{14,10},{16,20},{18,... | collective-permute-start | bytes 786440 | tf_op jit(solution)/shard_map/ppermute | solution.py:625
  37.1 9.6 %collective-permute-start.11 = (bf16[256,512]{1,0:T(8,128)(2,1)S(1)}, bf16[256,512]{1,0:T(8,128)(2,1)S(1)}, u32[]{:S(2)}, u32[]{:S(2)}) collective-permute-start(bf16[256,512]{1,0:T(8,128)(2,1)S(1)} %collective-permute-done.6.refs_1_), channel_id=1, source_target_pairs={{0,2},{2,0},{4,6},{6,4},{8,10},{10,8},{12,14},{14,12},{16,18},{18,... | collective-permute-start | bytes 786440 | tf_op jit(solution)/shard_map/ppermute | solution.py:577
  37.9 13.8 %collective-permute-start.15 = (bf16[256,512]{1,0:T(8,128)(2,1)S(1)}, bf16[256,512]{1,0:T(8,128)(2,1)S(1)}, u32[]{:S(2)}, u32[]{:S(2)}) collective-permute-start(bf16[256,512]{1,0:T(8,128)(2,1)S(1)} %collective-permute-done.6.refs_1_), channel_id=1, source_target_pairs={{0,4},{2,6},{4,0},{6,2},{8,12},{10,14},{12,8},{14,10},{16,20},{18,... | collective-permute-start | bytes 786440 | tf_op jit(solution)/shard_map/ppermute | solution.py:577
  46.6 10.8 %copy-start.13 = (s32[128,1]{0,1:T(1,128)S(1)}, s32[128,1]{0,1:T(1,128)}, u32[]{:S(2)}) copy-start(s32[128,1]{0,1:T(1,128)} %param.19) | copy-start | bytes 1540
  46.6 10.8 %copy-start.14 = (s32[128]{0:T(128)S(1)}, s32[128]{0:T(128)}, u32[]{:S(2)}) copy-start(s32[128]{0:T(128)} %param.20) | copy-start | bytes 1540
  46.7 12.2 %copy-start.1 = (bf16[1024,512]{1,0:T(8,128)(2,1)S(1)}, bf16[1024,512]{1,0:T(8,128)(2,1)}, u32[]{:S(2)}) copy-start(bf16[1024,512]{1,0:T(8,128)(2,1)} %adapter.1) | copy-start | bytes 3145732
  46.8 9.3 %collective-permute-start.16 = (bf16[256,512]{1,0:T(8,128)(2,1)S(1)}, bf16[256,512]{1,0:T(8,128)(2,1)S(1)}, u32[]{:S(2)}, u32[]{:S(2)}) collective-permute-start(bf16[256,512]{1,0:T(8,128)(2,1)S(1)} %collective-permute-done.11.refs_3_), channel_id=1, source_target_pairs={{0,4},{2,6},{4,0},{6,2},{8,12},{10,14},{12,8},{14,10},{16,20},{18,... | collective-permute-start | bytes 786440 | tf_op jit(solution)/shard_map/ppermute | solution.py:577
  48.1 5.6 %collective-permute-start.12 = (bf16[3,128,128]{2,1,0:T(8,128)(2,1)S(1)}, bf16[3,128,128]{2,1,0:T(8,128)(2,1)S(1)}, u32[]{:S(2)}, u32[]{:S(2)}) collective-permute-start(bf16[3,128,128]{2,1,0:T(8,128)(2,1)S(1)} %merge_both.1), channel_id=1, source_target_pairs={{0,10},{2,8},{4,14},{6,12},{8,2},{10,0},{12,6},{14,4},{16,26},{18,... | collective-permute-start | bytes 294920 | tf_op jit(solution)/shard_map/ppermute | solution.py:577
  48.2 6.5 %collective-permute-start.13 = (bf16[3,128,128]{2,1,0:T(8,128)(2,1)S(1)}, bf16[3,128,128]{2,1,0:T(8,128)(2,1)S(1)}, u32[]{:S(2)}, u32[]{:S(2)}) collective-permute-start(bf16[3,128,128]{2,1,0:T(8,128)(2,1)S(1)} %get-tuple-element.84), channel_id=1, source_target_pairs={{0,8},{2,10},{4,12},{6,14},{8,0},{10,2},{12,4},{14,6},{16,24},{18,... | collective-permute-start | bytes 294920 | tf_op jit(solution)/shard_map/ppermute | solution.py:577
  50.3 4.8 %collective-permute-start.14 = (bf16[3,128,128]{2,1,0:T(8,128)(2,1)S(1)}, bf16[3,128,128]{2,1,0:T(8,128)(2,1)S(1)}, u32[]{:S(2)}, u32[]{:S(2)}) collective-permute-start(bf16[3,128,128]{2,1,0:T(8,128)(2,1)S(1)} %get-tuple-element.85), channel_id=1, source_target_pairs={{0,2},{2,0},{4,6},{6,4},{8,10},{10,8},{12,14},{14,12},{16,18},{18,... | collective-permute-start | bytes 294920 | tf_op jit(solution)/shard_map/ppermute | solution.py:577
  51.6 0.7 copy-start.5
  56.1 1.2 %copy-start.7 = (bf16[256,512]{1,0:T(8,128)(2,1)}, bf16[256,512]{1,0:T(8,128)(2,1)S(1)}, u32[]{:S(2)}) copy-start(bf16[256,512]{1,0:T(8,128)(2,1)S(1)} %collective-permute-done.16.refs_7_) | copy-start | bytes 786436
  56.1 23.4 %copy-start.2 = (f32[256,512]{1,0:T(8,128)S(1)}, f32[256,512]{1,0:T(8,128)}, u32[]{:S(2)}) copy-start(f32[256,512]{1,0:T(8,128)} %refs_8_.1) | copy-start | bytes 1572868
  56.1 23.4 %copy-start.3 = (f32[256,512]{1,0:T(8,128)S(1)}, f32[256,512]{1,0:T(8,128)}, u32[]{:S(2)}) copy-start(f32[256,512]{1,0:T(8,128)} %refs_9_.1) | copy-start | bytes 1572868
  56.1 23.4 %copy-start.4 = (f32[256,512]{1,0:T(8,128)S(1)}, f32[256,512]{1,0:T(8,128)}, u32[]{:S(2)}) copy-start(f32[256,512]{1,0:T(8,128)} %refs_10_.1) | copy-start | bytes 1572868
  57.3 1.6 %collective-permute-start.17 = (bf16[128,1024]{1,0:T(8,128)(2,1)S(1)}, bf16[128,1024]{1,0:T(8,128)(2,1)S(1)}, u32[]{:S(2)}, u32[]{:S(2)}) collective-permute-start(bf16[128,1024]{1,0:T(8,128)(2,1)S(1)} %get-tuple-element.93), channel_id=1, source_target_pairs={{0,1},{1,0},{2,3},{3,2},{4,5},{5,4},{6,7},{7,6},{8,9},{9,8},{10,11... | collective-permute-start | bytes 786440 | tf_op jit(solution)/shard_map/ppermute | solution.py:651
  60.2 17.8 %all-to-all-start = ((bf16[16,112,128]{2,1,0:T(8,128)(2,1)}), bf16[16,112,128]{2,1,0:T(8,128)(2,1)S(1)}, u32[]{:S(2)}, u32[]{:S(2)}) async-start(bf16[16,112,128]{2,1,0:T(8,128)(2,1)} %pack.1), calls=%async_computation | async-start | bytes 917504 | tf_op jit(solution)/shard_map/all_to_all | solution.py:663
  63.8 14.4 %collective-permute-start.19 = (bf16[256,512]{1,0:T(8,128)(2,1)S(1)}, bf16[256,512]{1,0:T(8,128)(2,1)}, u32[]{:S(2)}, u32[]{:S(2)}) collective-permute-start(bf16[256,512]{1,0:T(8,128)(2,1)S(1)} %collective-permute-done.8.refs_4_), channel_id=1, source_target_pairs={{0,2},{2,0},{4,6},{6,4},{8,10},{10,8},{12,14},{14,12},{16,18},{18,... | collective-permute-start | bytes 786440 | tf_op jit(solution)/shard_map/ppermute | solution.py:577
  78.1 1.4 %collective-permute-start.18 = (bf16[16,32,128]{2,1,0:T(8,128)(2,1)S(1)}, bf16[16,32,128]{2,1,0:T(8,128)(2,1)S(1)}, u32[]{:S(2)}, u32[]{:S(2)}) collective-permute-start(bf16[16,32,128]{2,1,0:T(8,128)(2,1)S(1)} %slice.4), channel_id=1, source_target_pairs={{0,1},{1,0},{2,3},{3,2},{4,5},{5,4},{6,7},{7,6},{8,9},{9,8},{10,11... | collective-permute-start | bytes 393224 | tf_op jit(solution)/shard_map/ppermute | solution.py:664
  79.5 1.0 %copy-start.6 = (bf16[256,512]{1,0:T(8,128)(2,1)S(1)}, bf16[256,512]{1,0:T(8,128)(2,1)}, u32[]{:S(2)}) copy-start(bf16[256,512]{1,0:T(8,128)(2,1)} %copy-done.5) | copy-start | bytes 786436
  80.4 0.9 %copy-start.8 = (bf16[256,512]{1,0:T(8,128)(2,1)S(1)}, bf16[256,512]{1,0:T(8,128)(2,1)}, u32[]{:S(2)}) copy-start(bf16[256,512]{1,0:T(8,128)(2,1)} %copy-done.7) | copy-start | bytes 786436

commit v6 on v4

--- a/solution.py
+++ b/solution.py
@@ -591,7 +591,7 @@
     scales = (1.0 / math.sqrt(HD), float(seq_len))
     side_scratch = [pltpu.VMEM((4 * BLOCK, BLOCK), BF16)] * 2
     near_sum = shape((8 * BLOCK, BLOCK), F32)
-    cost = pl.CostEstimate(flops=10**9, bytes_accessed=2**20, transcendentals=0)
+    cost = pl.CostEstimate(flops=10**8, bytes_accessed=2**16, transcendentals=0)
     near_1, near_2, far_sum = pl.pallas_call(
         functools.partial(attend_own_body, scales[0]),
         out_shape=(near_sum, near_sum, shape((2, 4 * BLOCK, BLOCK), F32)),

time: 81.8 us -> 84.6 us (1.034)
  waiting for transfers between devices: 26.2 us -> 29.4 us
  starting transfers between devices: 26.3 us -> 25.1 us
    ppermute x1, waiting for transfers between devices: 1.59 us -> 3.99 us  [dealt_device(): near_in = lax.ppermute(near_own, 'ctx', ACROSS_Y)]
    ppermute x14, starting transfers between devices: 19 us -> 17.7 us  [exchange(): return lax.ppermute(sent, 'ctx', [(i, i ^ bit) for i in range(16)])]
  transfers between devices with their start and end apart: 20 -> 20, of which waited for: 13 -> 11; matrix products, arithmetic and copies ran while one was open for 0% -> 0% of each run, Pallas kernels for 5% -> 5%
where the time goes in v6:
time: 84.6 us; the launch traced here: 84.3 us
  waiting for transfers between devices  29.4 us (35%)
  starting transfers between devices  25.1 us (30%)
  blocking collectives  16.8 us (20%)
  Pallas kernels  7.6 us (9%)
  local copies, waits for them, and re-layouts  3.75 us (4%)
  between operations  1.67 us (2%)
    ppermute x14, starting transfers between devices, exchange(): return lax.ppermute(sent, 'ctx', [(i, i ^ bit) for i in range(16)])  17.7 us
    all_to_all x1, blocking collectives, dealt_device(): got = lax.all_to_all(packed, 'ctx', 0, 0, tiled=True)  16.8 us
    ppermute x14, waiting for transfers between devices, exchange(): return lax.ppermute(sent, 'ctx', [(i, i ^ bit) for i in range(16)])  16 us
    ppermute x1, waiting for transfers between devices, dealt_device(): near_back = lax.ppermute(near_out, 'ctx', ACROSS_Y)  4.69 us
    ppermute x1, waiting for transfers between devices, dealt_device(): near_in = lax.ppermute(near_own, 'ctx', ACROSS_Y)  3.99 us
    unnamed x22, local copies, waits for them, and re-layouts  3.74 us
    ppermute x1, waiting for transfers between devices, dealt_device(): far_back = lax.ppermute(far_out, ('ctx', 'head'), FAR_BACK)  3.36 us
    pallas_call x1, Pallas kernels, dealt_device(): pl.pallas_call(finish_body, out_shape=(shape((width // n_ctx, head_cols),...  2.63 us
  transfers between devices with their start and end apart: 20, of which 11 were waited for; matrix products, arithmetic and copies ran while one was open for 0% of the time, Pallas kernels for 5%

profile of v6, /device:TPU:0, one launch (start us, length us, event | category | flops | bytes accessed | tf_op | source)
XLA Modules:
  0.0 84.3 jit_solution(9934107708777438216)
XLA Ops:
  1.3 0.0 copy-start.5
  1.3 0.9 %copy-done.5 = bf16[2,128,512]{2,1,0:T(8,128)(2,1)S(1)} copy-done((bf16[2,128,512]{2,1,0:T(8,128)(2,1)S(1)}, bf16[2,128,512]{2,1,0:T(8,128)(2,1)}, u32[]{:S(2)}) %copy-start.5) | copy-done | bytes 262168
  2.2 0.9 %copy-done.6 = bf16[128,1024]{1,0:T(8,128)(2,1)S(1)} copy-done((bf16[128,1024]{1,0:T(8,128)(2,1)S(1)}, bf16[128,1024]{1,0:T(8,128)(2,1)}, u32[]{:S(2)}) %copy-start.6) | copy-done | bytes 262168
  3.2 0.9 %copy-done.7 = bf16[128,512]{1,0:T(8,128)(2,1)S(1)} copy-done((bf16[128,512]{1,0:T(8,128)(2,1)S(1)}, bf16[128,512]{1,0:T(8,128)(2,1)}, u32[]{:S(2)}) %copy-start.7) | copy-done | bytes 131096
  4.1 0.9 %copy-done.8 = bf16[128,512]{1,0:T(8,128)(2,1)S(1)} copy-done((bf16[128,512]{1,0:T(8,128)(2,1)S(1)}, bf16[128,512]{1,0:T(8,128)(2,1)}, u32[]{:S(2)}) %copy-start.8) | copy-done | bytes 131096
  5.0 0.3 deal.1
  5.3 4.1 %collective-permute-start = (bf16[144,512]{1,0:T(8,128)(2,1)S(1)}, bf16[144,512]{1,0:T(8,128)(2,1)S(1)}, u32[]{:S(2)}, u32[]{:S(2)}) collective-permute-start(bf16[144,512]{1,0:T(8,128)(2,1)S(1)} %get-tuple-element.56.rows_1), channel_id=1, source_target_pairs={{0,16},{2,18},{4,20},{6,22},{8,24},{10,26},{12,28},{14,30},{16,0},... | collective-permute-start | bytes 442376 | tf_op jit(solution)/shard_map/ppermute | solution.py:577
  9.4 2.5 %collective-permute-start.1 = (bf16[560,128]{1,0:T(8,128)(2,1)S(1)}, bf16[560,128]{1,0:T(8,128)(2,1)S(1)}, u32[]{:S(2)}, u32[]{:S(2)}) collective-permute-start(bf16[560,128]{1,0:T(8,128)(2,1)S(1)} %get-tuple-element.57), channel_id=1, source_target_pairs={{0,10},{2,8},{4,14},{6,12},{8,2},{10,0},{12,6},{14,4},{16,26},{18,... | collective-permute-start | bytes 430088 | tf_op jit(solution)/shard_map/ppermute | solution.py:577
  11.9 0.4 collective-permute-start.2
  12.4 0.5 collective-permute-start.3
  12.9 6.1 %collective-permute-done.1.by_both = bf16[560,128]{1,0:T(8,128)(2,1)S(1)} collective-permute-done((bf16[560,128]{1,0:T(8,128)(2,1)S(1)}, bf16[560,128]{1,0:T(8,128)(2,1)S(1)}, u32[]{:S(2)}, u32[]{:S(2)}) %collective-permute-start.1) | collective-permute-done | bytes 143392 | tf_op jit(solution)/shard_map/ppermute | solution.py:577
  19.0 1.6 %collective-permute-done.2.by_zl = bf16[560,128]{1,0:T(8,128)(2,1)S(1)} collective-permute-done((bf16[560,128]{1,0:T(8,128)(2,1)S(1)}, bf16[560,128]{1,0:T(8,128)(2,1)S(1)}, u32[]{:S(2)}, u32[]{:S(2)}) %collective-permute-start.2) | collective-permute-done | bytes 143392 | tf_op jit(solution)/shard_map/ppermute | solution.py:577
  20.6 0.0 collective-permute-done.3.by_x
  20.6 0.0 collective-permute-done.rows_2
  20.6 0.1 gather.1
  20.7 2.5 %collective-permute-start.5 = (bf16[4,288,128]{2,1,0:T(8,128)(2,1)S(1)}, bf16[4,288,128]{2,1,0:T(8,128)(2,1)S(1)}, u32[]{:S(2)}, u32[]{:S(2)}) collective-permute-start(bf16[4,288,128]{2,1,0:T(8,128)(2,1)S(1)} %get-tuple-element.65.far_own), channel_id=1, source_target_pairs={{0,16},{2,18},{4,20},{6,22},{8,24},{10,26},{12,28},{14,30},{17,1},... | collective-permute-start | bytes 884744 | tf_op jit(solution)/shard_map/ppermute | solution.py:588
  23.2 1.6 %collective-permute-start.4 = (bf16[4,272,128]{2,1,0:T(8,128)(2,1)S(1)}, bf16[4,272,128]{2,1,0:T(8,128)(2,1)S(1)}, u32[]{:S(2)}, u32[]{:S(2)}) collective-permute-start(bf16[4,272,128]{2,1,0:T(8,128)(2,1)S(1)} %get-tuple-element.64.near_own), channel_id=1, source_target_pairs={{0,4},{2,6},{4,0},{6,2},{8,12},{10,14},{12,8},{14,10},{16,20},{18,... | collective-permute-start | bytes 835592 | tf_op jit(solution)/shard_map/ppermute | solution.py:589
  24.8 2.5 %collective-permute-start.6 = (bf16[256,512]{1,0:T(8,128)(2,1)S(1)}, bf16[256,512]{1,0:T(8,128)(2,1)S(1)}, u32[]{:S(2)}, u32[]{:S(2)}) collective-permute-start(bf16[256,512]{1,0:T(8,128)(2,1)S(1)} %get-tuple-element.71.refs_0_), channel_id=1, source_target_pairs={{0,8},{2,10},{4,12},{6,14},{8,0},{10,2},{12,4},{14,6},{16,24},{18,... | collective-permute-start | bytes 786440 | tf_op jit(solution)/shard_map/ppermute | solution.py:577
  27.3 0.5 collective-permute-start.7
  27.9 0.5 collective-permute-start.8
  28.4 4.0 %collective-permute-done.4.near_in = bf16[4,272,128]{2,1,0:T(8,128)(2,1)S(1)} collective-permute-done((bf16[4,272,128]{2,1,0:T(8,128)(2,1)S(1)}, bf16[4,272,128]{2,1,0:T(8,128)(2,1)S(1)}, u32[]{:S(2)}, u32[]{:S(2)}) %collective-permute-start.4) | collective-permute-done | bytes 278560 | tf_op jit(solution)/shard_map/ppermute | solution.py:589
  32.3 2.5 %attend_own.1 = (f32[1024,128]{1,0:T(8,128)S(1)}, f32[1024,128]{1,0:T(8,128)S(1)}, f32[2,512,128]{2,1,0:T(8,128)S(1)}) custom-call(bf16[4,272,128]{2,1,0:T(8,128)(2,1)S(1)} %get-tuple-element.64.near_own, bf16[4,288,128]{2,1,0:T(8,128)(2,1)S(1)} %get-tuple-element.65.far_own, bf16[4,272,128]{2,1,0:T(8,128)(2,1)S(1)} %collective-permute-done.4.near_in), custom_call_target="tpu_custom_call" | custom-call | flops 100000000 | bytes 65536 | tf_op jit(solution)/shard_map/attend_own/pallas_call | solution.py:595
  34.9 0.0 collective-permute-done.5.far_in
  34.9 0.0 copy-start
  34.9 0.0 collective-permute-done.6.refs_1_
  35.0 0.0 collective-permute-done.7.refs_2_
  35.0 0.2 collective-permute-done.8.refs_4_
  35.2 1.6 %collective-permute-start.9 = (bf16[4,272,128]{2,1,0:T(8,128)(2,1)S(1)}, bf16[4,272,128]{2,1,0:T(8,128)(2,1)S(1)}, u32[]{:S(2)}, u32[]{:S(2)}) collective-permute-start(bf16[4,272,128]{2,1,0:T(8,128)(2,1)S(1)} %get-tuple-element.72), channel_id=1, source_target_pairs={{16,0},{18,2},{20,4},{22,6},{24,8},{26,10},{28,12},{30,14},{1,17},... | collective-permute-start | bytes 835592 | tf_op jit(solution)/shard_map/ppermute | solution.py:624
  36.8 1.6 %collective-permute-start.10 = (bf16[4,2,128,128]{3,2,1,0:T(8,128)(2,1)S(1)}, bf16[4,2,128,128]{3,2,1,0:T(8,128)(2,1)S(1)}, u32[]{:S(2)}, u32[]{:S(2)}) collective-permute-start(bf16[4,2,128,128]{3,2,1,0:T(8,128)(2,1)S(1)} %near.1), channel_id=1, source_target_pairs={{0,4},{2,6},{4,0},{6,2},{8,12},{10,14},{12,8},{14,10},{16,20},{18,... | collective-permute-start | bytes 786440 | tf_op jit(solution)/shard_map/ppermute | solution.py:625
  38.4 0.3 collective-permute-start.11
  38.7 0.8 collective-permute-start.15
  39.6 4.7 %collective-permute-done.10.near = bf16[4,2,128,128]{3,2,1,0:T(8,128)(2,1)S(1)} collective-permute-done((bf16[4,2,128,128]{3,2,1,0:T(8,128)(2,1)S(1)}, bf16[4,2,128,128]{3,2,1,0:T(8,128)(2,1)S(1)}, u32[]{:S(2)}, u32[]{:S(2)}) %collective-permute-start.10) | collective-permute-done | bytes 262176 | tf_op jit(solution)/shard_map/ppermute | solution.py:625
  44.2 3.4 %collective-permute-done.9.far = bf16[4,272,128]{2,1,0:T(8,128)(2,1)S(1)} collective-permute-done((bf16[4,272,128]{2,1,0:T(8,128)(2,1)S(1)}, bf16[4,272,128]{2,1,0:T(8,128)(2,1)S(1)}, u32[]{:S(2)}, u32[]{:S(2)}) %collective-permute-start.9) | collective-permute-done | bytes 278560 | tf_op jit(solution)/shard_map/ppermute | solution.py:624
  47.6 0.0 copy-start.9
  47.6 0.0 copy-start.10
  47.7 0.0 copy-start.1
  47.7 0.1 merge.1
  47.8 0.0 collective-permute-done.11.refs_3_
  47.8 1.6 %collective-permute-start.16 = (bf16[256,512]{1,0:T(8,128)(2,1)S(1)}, bf16[256,512]{1,0:T(8,128)(2,1)S(1)}, u32[]{:S(2)}, u32[]{:S(2)}) collective-permute-start(bf16[256,512]{1,0:T(8,128)(2,1)S(1)} %collective-permute-done.11.refs_3_), channel_id=1, source_target_pairs={{0,4},{2,6},{4,0},{6,2},{8,12},{10,14},{12,8},{14,10},{16,20},{18,... | collective-permute-start | bytes 786440 | tf_op jit(solution)/shard_map/ppermute | solution.py:577
  49.4 0.0 collective-permute-start.12
  49.4 1.8 %collective-permute-start.13 = (bf16[3,128,128]{2,1,0:T(8,128)(2,1)S(1)}, bf16[3,128,128]{2,1,0:T(8,128)(2,1)S(1)}, u32[]{:S(2)}, u32[]{:S(2)}) collective-permute-start(bf16[3,128,128]{2,1,0:T(8,128)(2,1)S(1)} %get-tuple-element.86), channel_id=1, source_target_pairs={{0,8},{2,10},{4,12},{6,14},{8,0},{10,2},{12,4},{14,6},{16,24},{18,... | collective-permute-start | bytes 294920 | tf_op jit(solution)/shard_map/ppermute | solution.py:577
  51.2 1.7 %collective-permute-start.14 = (bf16[3,128,128]{2,1,0:T(8,128)(2,1)S(1)}, bf16[3,128,128]{2,1,0:T(8,128)(2,1)S(1)}, u32[]{:S(2)}, u32[]{:S(2)}) collective-permute-start(bf16[3,128,128]{2,1,0:T(8,128)(2,1)S(1)} %get-tuple-element.87), channel_id=1, source_target_pairs={{0,2},{2,0},{4,6},{6,4},{8,10},{10,8},{12,14},{14,12},{16,18},{18,... | collective-permute-start | bytes 294920 | tf_op jit(solution)/shard_map/ppermute | solution.py:577
  52.9 0.0 collective-permute-done.15.refs_5_
  52.9 0.3 collective-permute-start.18
  53.2 2.8 %collective-permute-done.12.by_both = bf16[3,128,128]{2,1,0:T(8,128)(2,1)S(1)} collective-permute-done((bf16[3,128,128]{2,1,0:T(8,128)(2,1)S(1)}, bf16[3,128,128]{2,1,0:T(8,128)(2,1)S(1)}, u32[]{:S(2)}, u32[]{:S(2)}) %collective-permute-start.12) | collective-permute-done | bytes 98336 | tf_op jit(solution)/shard_map/ppermute | solution.py:577
  56.0 0.6 collective-permute-done.13.by_zl
  56.6 0.9 %collective-permute-done.14.by_x = bf16[3,128,128]{2,1,0:T(8,128)(2,1)S(1)} collective-permute-done((bf16[3,128,128]{2,1,0:T(8,128)(2,1)S(1)}, bf16[3,128,128]{2,1,0:T(8,128)(2,1)S(1)}, u32[]{:S(2)}, u32[]{:S(2)}) %collective-permute-start.14) | collective-permute-done | bytes 98336 | tf_op jit(solution)/shard_map/ppermute | solution.py:577
  57.5 0.0 collective-permute-done.16.refs_7_
  57.5 0.0 copy-done
  57.5 0.0 copy-start.3
  57.5 0.0 copy-start.4
  57.5 1.2 %project.1 = (f32[128,1024]{1,0:T(8,128)S(1)}, bf16[128,1024]{1,0:T(8,128)(2,1)S(1)}) custom-call(bf16[3,128,128]{2,1,0:T(8,128)(2,1)S(1)} %collective-permute-done.12.by_both, bf16[3,128,128]{2,1,0:T(8,128)(2,1)S(1)} %collective-permute-done.13.by_zl, bf16[3,128,128]{2,1,0:T(8,128)(2,1)S(1)} %collective-permute-done.14.by_x, ...), custom_call_target="tpu_custom_call" | custom-call | tf_op jit(solution)/shard_map/project/pallas_call | solution.py:635
  58.7 0.1 collective-permute-start.17
  58.7 0.0 copy-done.9
  58.8 0.0 copy-done.10
  58.8 0.2 place.1
  58.9 3.8 %collective-permute-done.18.refs_6_ = bf16[256,512]{1,0:T(8,128)(2,1)S(1)} collective-permute-done((bf16[256,512]{1,0:T(8,128)(2,1)S(1)}, bf16[256,512]{1,0:T(8,128)(2,1)S(1)}, u32[]{:S(2)}, u32[]{:S(2)}) %collective-permute-start.18) | collective-permute-done | bytes 262176 | tf_op jit(solution)/shard_map/ppermute | solution.py:577
  62.8 0.0 collective-permute-done.17.other
  62.8 0.0 copy-done.1
  62.8 0.5 pack.1
  63.3 16.8 %all_to_all.5.got = bf16[16,112,128]{2,1,0:T(8,128)(2,1)S(1)} all-to-all(bf16[16,112,128]{2,1,0:T(8,128)(2,1)S(1)} %pack.1), channel_id=1, replica_groups=mesh['ctx'=16,'head'=2] {'ctx'}, dimensions={0} | all-to-all | bytes 917504 | tf_op jit(solution)/shard_map/all_to_all | solution.py:664
  80.1 0.1 collective-permute-start.19
  80.2 1.3 %collective-permute-done.19.other = bf16[16,32,128]{2,1,0:T(8,128)(2,1)S(1)} collective-permute-done((bf16[16,32,128]{2,1,0:T(8,128)(2,1)S(1)}, bf16[16,32,128]{2,1,0:T(8,128)(2,1)S(1)}, u32[]{:S(2)}, u32[]{:S(2)}) %collective-permute-start.19) | collective-permute-done | bytes 131104 | tf_op jit(solution)/shard_map/ppermute | solution.py:665
  81.5 2.6 %finish.1 = (f32[64,512]{1,0:T(8,128)}, f32[256,512]{1,0:T(8,128)}, f32[256,512]{1,0:T(8,128)}, f32[256,512]{1,0:T(8,128)}) custom-call(bf16[16,112,128]{2,1,0:T(8,128)(2,1)S(1)} %all_to_all.5.got, bf16[16,32,128]{2,1,0:T(8,128)(2,1)S(1)} %collective-permute-done.19.other, bf16[256,512]{1,0:T(8,128)(2,1)S(1)} %get-tuple-element.71.refs_0_, ...), custom_call_target="tpu_custom_call" | custom-call | tf_op jit(solution)/shard_map/finish/pallas_call | solution.py:668
  (11 shorter events, 0.1 us)
Async XLA Ops:
  1.3 1.0 %copy-start.5 = (bf16[2,128,512]{2,1,0:T(8,128)(2,1)S(1)}, bf16[2,128,512]{2,1,0:T(8,128)(2,1)}, u32[]{:S(2)}) copy-start(bf16[2,128,512]{2,1,0:T(8,128)(2,1)} %keys_values.1) | copy-start | bytes 786436
  2.2 0.9 %copy-start.6 = (bf16[128,1024]{1,0:T(8,128)(2,1)S(1)}, bf16[128,1024]{1,0:T(8,128)(2,1)}, u32[]{:S(2)}) copy-start(bf16[128,1024]{1,0:T(8,128)(2,1)} %rows.1) | copy-start | bytes 786436
  3.2 0.9 %copy-start.7 = (bf16[128,512]{1,0:T(8,128)(2,1)S(1)}, bf16[128,512]{1,0:T(8,128)(2,1)}, u32[]{:S(2)}) copy-start(bf16[128,512]{1,0:T(8,128)(2,1)} %queries.1) | copy-start | bytes 393220
  4.1 0.9 %copy-start.8 = (bf16[128,512]{1,0:T(8,128)(2,1)S(1)}, bf16[128,512]{1,0:T(8,128)(2,1)}, u32[]{:S(2)}) copy-start(bf16[128,512]{1,0:T(8,128)(2,1)} %cot.1) | copy-start | bytes 393220
  5.3 15.3 %collective-permute-start = (bf16[144,512]{1,0:T(8,128)(2,1)S(1)}, bf16[144,512]{1,0:T(8,128)(2,1)S(1)}, u32[]{:S(2)}, u32[]{:S(2)}) collective-permute-start(bf16[144,512]{1,0:T(8,128)(2,1)S(1)} %get-tuple-element.56.rows_1), channel_id=1, source_target_pairs={{0,16},{2,18},{4,20},{6,22},{8,24},{10,26},{12,28},{14,30},{16,0},... | collective-permute-start | bytes 442376 | tf_op jit(solution)/shard_map/ppermute | solution.py:577
  9.4 9.6 %collective-permute-start.1 = (bf16[560,128]{1,0:T(8,128)(2,1)S(1)}, bf16[560,128]{1,0:T(8,128)(2,1)S(1)}, u32[]{:S(2)}, u32[]{:S(2)}) collective-permute-start(bf16[560,128]{1,0:T(8,128)(2,1)S(1)} %get-tuple-element.57), channel_id=1, source_target_pairs={{0,10},{2,8},{4,14},{6,12},{8,2},{10,0},{12,6},{14,4},{16,26},{18,... | collective-permute-start | bytes 430088 | tf_op jit(solution)/shard_map/ppermute | solution.py:577
  11.9 8.7 %collective-permute-start.2 = (bf16[560,128]{1,0:T(8,128)(2,1)S(1)}, bf16[560,128]{1,0:T(8,128)(2,1)S(1)}, u32[]{:S(2)}, u32[]{:S(2)}) collective-permute-start(bf16[560,128]{1,0:T(8,128)(2,1)S(1)} %get-tuple-element.58), channel_id=1, source_target_pairs={{0,8},{2,10},{4,12},{6,14},{8,0},{10,2},{12,4},{14,6},{16,24},{18,... | collective-permute-start | bytes 430088 | tf_op jit(solution)/shard_map/ppermute | solution.py:577
  12.4 8.3 %collective-permute-start.3 = (bf16[560,128]{1,0:T(8,128)(2,1)S(1)}, bf16[560,128]{1,0:T(8,128)(2,1)S(1)}, u32[]{:S(2)}, u32[]{:S(2)}) collective-permute-start(bf16[560,128]{1,0:T(8,128)(2,1)S(1)} %get-tuple-element.59), channel_id=1, source_target_pairs={{0,2},{2,0},{4,6},{6,4},{8,10},{10,8},{12,14},{14,12},{16,18},{18,... | collective-permute-start | bytes 430088 | tf_op jit(solution)/shard_map/ppermute | solution.py:577
  20.7 14.2 %collective-permute-start.5 = (bf16[4,288,128]{2,1,0:T(8,128)(2,1)S(1)}, bf16[4,288,128]{2,1,0:T(8,128)(2,1)S(1)}, u32[]{:S(2)}, u32[]{:S(2)}) collective-permute-start(bf16[4,288,128]{2,1,0:T(8,128)(2,1)S(1)} %get-tuple-element.65.far_own), channel_id=1, source_target_pairs={{0,16},{2,18},{4,20},{6,22},{8,24},{10,26},{12,28},{14,30},{17,1},... | collective-permute-start | bytes 884744 | tf_op jit(solution)/shard_map/ppermute | solution.py:588
  23.2 9.1 %collective-permute-start.4 = (bf16[4,272,128]{2,1,0:T(8,128)(2,1)S(1)}, bf16[4,272,128]{2,1,0:T(8,128)(2,1)S(1)}, u32[]{:S(2)}, u32[]{:S(2)}) collective-permute-start(bf16[4,272,128]{2,1,0:T(8,128)(2,1)S(1)} %get-tuple-element.64.near_own), channel_id=1, source_target_pairs={{0,4},{2,6},{4,0},{6,2},{8,12},{10,14},{12,8},{14,10},{16,20},{18,... | collective-permute-start | bytes 835592 | tf_op jit(solution)/shard_map/ppermute | solution.py:589
  24.8 10.1 %collective-permute-start.6 = (bf16[256,512]{1,0:T(8,128)(2,1)S(1)}, bf16[256,512]{1,0:T(8,128)(2,1)S(1)}, u32[]{:S(2)}, u32[]{:S(2)}) collective-permute-start(bf16[256,512]{1,0:T(8,128)(2,1)S(1)} %get-tuple-element.71.refs_0_), channel_id=1, source_target_pairs={{0,8},{2,10},{4,12},{6,14},{8,0},{10,2},{12,4},{14,6},{16,24},{18,... | collective-permute-start | bytes 786440 | tf_op jit(solution)/shard_map/ppermute | solution.py:577
  27.3 7.6 %collective-permute-start.7 = (bf16[256,512]{1,0:T(8,128)(2,1)S(1)}, bf16[256,512]{1,0:T(8,128)(2,1)S(1)}, u32[]{:S(2)}, u32[]{:S(2)}) collective-permute-start(bf16[256,512]{1,0:T(8,128)(2,1)S(1)} %get-tuple-element.71.refs_0_), channel_id=1, source_target_pairs={{0,2},{2,0},{4,6},{6,4},{8,10},{10,8},{12,14},{14,12},{16,18},{18,... | collective-permute-start | bytes 786440 | tf_op jit(solution)/shard_map/ppermute | solution.py:577
  27.9 7.3 %collective-permute-start.8 = (bf16[256,512]{1,0:T(8,128)(2,1)S(1)}, bf16[256,512]{1,0:T(8,128)(2,1)S(1)}, u32[]{:S(2)}, u32[]{:S(2)}) collective-permute-start(bf16[256,512]{1,0:T(8,128)(2,1)S(1)} %get-tuple-element.71.refs_0_), channel_id=1, source_target_pairs={{0,4},{2,6},{4,0},{6,2},{8,12},{10,14},{12,8},{14,10},{16,20},{18,... | collective-permute-start | bytes 786440 | tf_op jit(solution)/shard_map/ppermute | solution.py:577
  34.9 22.5 %copy-start = (bf16[3,1024,512]{2,1,0:T(8,128)(2,1)S(1)}, bf16[3,1024,512]{2,1,0:T(8,128)(2,1)}, u32[]{:S(2)}) copy-start(bf16[3,1024,512]{2,1,0:T(8,128)(2,1)} %weight.1) | copy-start | bytes 9437188
  35.2 12.4 %collective-permute-start.9 = (bf16[4,272,128]{2,1,0:T(8,128)(2,1)S(1)}, bf16[4,272,128]{2,1,0:T(8,128)(2,1)S(1)}, u32[]{:S(2)}, u32[]{:S(2)}) collective-permute-start(bf16[4,272,128]{2,1,0:T(8,128)(2,1)S(1)} %get-tuple-element.72), channel_id=1, source_target_pairs={{16,0},{18,2},{20,4},{22,6},{24,8},{26,10},{28,12},{30,14},{1,17},... | collective-permute-start | bytes 835592 | tf_op jit(solution)/shard_map/ppermute | solution.py:624
  36.8 7.4 %collective-permute-start.10 = (bf16[4,2,128,128]{3,2,1,0:T(8,128)(2,1)S(1)}, bf16[4,2,128,128]{3,2,1,0:T(8,128)(2,1)S(1)}, u32[]{:S(2)}, u32[]{:S(2)}) collective-permute-start(bf16[4,2,128,128]{3,2,1,0:T(8,128)(2,1)S(1)} %near.1), channel_id=1, source_target_pairs={{0,4},{2,6},{4,0},{6,2},{8,12},{10,14},{12,8},{14,10},{16,20},{18,... | collective-permute-start | bytes 786440 | tf_op jit(solution)/shard_map/ppermute | solution.py:625
  38.4 9.3 %collective-permute-start.11 = (bf16[256,512]{1,0:T(8,128)(2,1)S(1)}, bf16[256,512]{1,0:T(8,128)(2,1)S(1)}, u32[]{:S(2)}, u32[]{:S(2)}) collective-permute-start(bf16[256,512]{1,0:T(8,128)(2,1)S(1)} %collective-permute-done.6.refs_1_), channel_id=1, source_target_pairs={{0,2},{2,0},{4,6},{6,4},{8,10},{10,8},{12,14},{14,12},{16,18},{18,... | collective-permute-start | bytes 786440 | tf_op jit(solution)/shard_map/ppermute | solution.py:577
  38.7 14.2 %collective-permute-start.15 = (bf16[256,512]{1,0:T(8,128)(2,1)S(1)}, bf16[256,512]{1,0:T(8,128)(2,1)S(1)}, u32[]{:S(2)}, u32[]{:S(2)}) collective-permute-start(bf16[256,512]{1,0:T(8,128)(2,1)S(1)} %collective-permute-done.6.refs_1_), channel_id=1, source_target_pairs={{0,4},{2,6},{4,0},{6,2},{8,12},{10,14},{12,8},{14,10},{16,20},{18,... | collective-permute-start | bytes 786440 | tf_op jit(solution)/shard_map/ppermute | solution.py:577
  47.6 11.1 %copy-start.9 = (s32[128,1]{0,1:T(1,128)S(1)}, s32[128,1]{0,1:T(1,128)}, u32[]{:S(2)}) copy-start(s32[128,1]{0,1:T(1,128)} %param.19) | copy-start | bytes 1540
  47.6 11.1 %copy-start.10 = (s32[128]{0:T(128)S(1)}, s32[128]{0:T(128)}, u32[]{:S(2)}) copy-start(s32[128]{0:T(128)} %param.20) | copy-start | bytes 1540
  47.7 15.1 %copy-start.1 = (bf16[1024,512]{1,0:T(8,128)(2,1)S(1)}, bf16[1024,512]{1,0:T(8,128)(2,1)}, u32[]{:S(2)}) copy-start(bf16[1024,512]{1,0:T(8,128)(2,1)} %adapter.1) | copy-start | bytes 3145732
  47.8 9.7 %collective-permute-start.16 = (bf16[256,512]{1,0:T(8,128)(2,1)S(1)}, bf16[256,512]{1,0:T(8,128)(2,1)S(1)}, u32[]{:S(2)}, u32[]{:S(2)}) collective-permute-start(bf16[256,512]{1,0:T(8,128)(2,1)S(1)} %collective-permute-done.11.refs_3_), channel_id=1, source_target_pairs={{0,4},{2,6},{4,0},{6,2},{8,12},{10,14},{12,8},{14,10},{16,20},{18,... | collective-permute-start | bytes 786440 | tf_op jit(solution)/shard_map/ppermute | solution.py:577
  49.4 6.6 %collective-permute-start.12 = (bf16[3,128,128]{2,1,0:T(8,128)(2,1)S(1)}, bf16[3,128,128]{2,1,0:T(8,128)(2,1)S(1)}, u32[]{:S(2)}, u32[]{:S(2)}) collective-permute-start(bf16[3,128,128]{2,1,0:T(8,128)(2,1)S(1)} %merge_both.1), channel_id=1, source_target_pairs={{0,10},{2,8},{4,14},{6,12},{8,2},{10,0},{12,6},{14,4},{16,26},{18,... | collective-permute-start | bytes 294920 | tf_op jit(solution)/shard_map/ppermute | solution.py:577
  49.4 7.2 %collective-permute-start.13 = (bf16[3,128,128]{2,1,0:T(8,128)(2,1)S(1)}, bf16[3,128,128]{2,1,0:T(8,128)(2,1)S(1)}, u32[]{:S(2)}, u32[]{:S(2)}) collective-permute-start(bf16[3,128,128]{2,1,0:T(8,128)(2,1)S(1)} %get-tuple-element.86), channel_id=1, source_target_pairs={{0,8},{2,10},{4,12},{6,14},{8,0},{10,2},{12,4},{14,6},{16,24},{18,... | collective-permute-start | bytes 294920 | tf_op jit(solution)/shard_map/ppermute | solution.py:577
  51.2 6.3 %collective-permute-start.14 = (bf16[3,128,128]{2,1,0:T(8,128)(2,1)S(1)}, bf16[3,128,128]{2,1,0:T(8,128)(2,1)S(1)}, u32[]{:S(2)}, u32[]{:S(2)}) collective-permute-start(bf16[3,128,128]{2,1,0:T(8,128)(2,1)S(1)} %get-tuple-element.87), channel_id=1, source_target_pairs={{0,2},{2,0},{4,6},{6,4},{8,10},{10,8},{12,14},{14,12},{16,18},{18,... | collective-permute-start | bytes 294920 | tf_op jit(solution)/shard_map/ppermute | solution.py:577
  52.9 9.9 %collective-permute-start.18 = (bf16[256,512]{1,0:T(8,128)(2,1)S(1)}, bf16[256,512]{1,0:T(8,128)(2,1)S(1)}, u32[]{:S(2)}, u32[]{:S(2)}) collective-permute-start(bf16[256,512]{1,0:T(8,128)(2,1)S(1)} %collective-permute-done.8.refs_4_), channel_id=1, source_target_pairs={{0,2},{2,0},{4,6},{6,4},{8,10},{10,8},{12,14},{14,12},{16,18},{18,... | collective-permute-start | bytes 786440 | tf_op jit(solution)/shard_map/ppermute | solution.py:577
  57.5 24.1 %copy-start.2 = (f32[256,512]{1,0:T(8,128)S(1)}, f32[256,512]{1,0:T(8,128)}, u32[]{:S(2)}) copy-start(f32[256,512]{1,0:T(8,128)} %refs_8_.1) | copy-start | bytes 1572868
  57.5 24.1 %copy-start.3 = (f32[256,512]{1,0:T(8,128)S(1)}, f32[256,512]{1,0:T(8,128)}, u32[]{:S(2)}) copy-start(f32[256,512]{1,0:T(8,128)} %refs_9_.1) | copy-start | bytes 1572868
  57.5 24.1 %copy-start.4 = (f32[256,512]{1,0:T(8,128)S(1)}, f32[256,512]{1,0:T(8,128)}, u32[]{:S(2)}) copy-start(f32[256,512]{1,0:T(8,128)} %refs_10_.1) | copy-start | bytes 1572868
  58.7 4.1 %collective-permute-start.17 = (bf16[128,1024]{1,0:T(8,128)(2,1)S(1)}, bf16[128,1024]{1,0:T(8,128)(2,1)S(1)}, u32[]{:S(2)}, u32[]{:S(2)}) collective-permute-start(bf16[128,1024]{1,0:T(8,128)(2,1)S(1)} %get-tuple-element.95), channel_id=1, source_target_pairs={{0,1},{1,0},{2,3},{3,2},{4,5},{5,4},{6,7},{7,6},{8,9},{9,8},{10,11... | collective-permute-start | bytes 786440 | tf_op jit(solution)/shard_map/ppermute | solution.py:651
  80.1 1.4 %collective-permute-start.19 = (bf16[16,32,128]{2,1,0:T(8,128)(2,1)S(1)}, bf16[16,32,128]{2,1,0:T(8,128)(2,1)S(1)}, u32[]{:S(2)}, u32[]{:S(2)}) collective-permute-start(bf16[16,32,128]{2,1,0:T(8,128)(2,1)S(1)} %slice.4), channel_id=1, source_target_pairs={{0,1},{1,0},{2,3},{3,2},{4,5},{5,4},{6,7},{7,6},{8,9},{9,8},{10,11... | collective-permute-start | bytes 393224 | tf_op jit(solution)/shard_map/ppermute | solution.py:665

commit v7 on v4

--- a/solution.py
+++ b/solution.py
@@ -587,7 +587,7 @@
     )
     far_in = lax.ppermute(far_own, ("ctx", "head"), FAR_OUT)
     near_in = lax.ppermute(near_own, "ctx", ACROSS_Y)
-    zl_rows, x_rows, y_rows = [exchange(two, bit) for bit in ROUNDS[1:]]
+    zl_rows, x_rows = [exchange(two, bit) for bit in ROUNDS[1:3]]
     scales = (1.0 / math.sqrt(HD), float(seq_len))
     side_scratch = [pltpu.VMEM((4 * BLOCK, BLOCK), BF16)] * 2
     near_sum = shape((8 * BLOCK, BLOCK), F32)
@@ -602,6 +602,8 @@
         cost_estimate=cost,
         name="attend_own",
     )(near_own, far_own, near_in)
+    near_1, near_2, two_y = lax.optimization_barrier((near_1, near_2, two))
+    y_rows = exchange(two_y, ROUNDS[3])
     near_1, near_2, far_out = pl.pallas_call(
         functools.partial(attend_far_body, *scales),
         out_shape=(near_sum, near_sum, shape((4, PART, BLOCK), BF16)),

time: 81.8 us -> 84 us (1.027)
  blocking collectives: 16.1 us -> 17.6 us
    ppermute x1, waiting for transfers between devices: 4.69 us -> 6.2 us  [dealt_device(): near_back = lax.ppermute(near_out, 'ctx', ACROSS_Y)]
    all_to_all x1, blocking collectives: 16.1 us -> 17.6 us  [dealt_device(): got = lax.all_to_all(packed, 'ctx', 0, 0, tiled=True)]
    ppermute x14, waiting for transfers between devices: 16 us -> 17.3 us  [exchange(): return lax.ppermute(sent, 'ctx', [(i, i ^ bit) for i in range(16)])]
    ppermute x1, waiting for transfers between devices: 1.59 us -> 0.33 us  [dealt_device(): near_in = lax.ppermute(near_own, 'ctx', ACROSS_Y)]
    ppermute x1, waiting for transfers between devices: 2.53 us -> 1.51 us  [dealt_device(): far_back = lax.ppermute(far_out, ('ctx', 'head'), FAR_BACK)]
  transfers between devices with their start and end apart: 20 -> 20, of which waited for: 13 -> 11; matrix products, arithmetic and copies ran while one was open for 0% -> 0% of each run, Pallas kernels for 5% -> 5%
where the time goes in v7:
time: 84 us; the launch traced here: 83.7 us
  waiting for transfers between devices  26.7 us (32%)
  starting transfers between devices  26.4 us (31%)
  blocking collectives  17.6 us (21%)
  Pallas kernels  7.62 us (9%)
  local copies, waits for them, and re-layouts  3.75 us (4%)
  between operations  1.65 us (2%)
    ppermute x14, starting transfers between devices, exchange(): return lax.ppermute(sent, 'ctx', [(i, i ^ bit) for i in range(16)])  19.1 us
    all_to_all x1, blocking collectives, dealt_device(): got = lax.all_to_all(packed, 'ctx', 0, 0, tiled=True)  17.6 us
    ppermute x14, waiting for transfers between devices, exchange(): return lax.ppermute(sent, 'ctx', [(i, i ^ bit) for i in range(16)])  17.3 us
    ppermute x1, waiting for transfers between devices, dealt_device(): near_back = lax.ppermute(near_out, 'ctx', ACROSS_Y)  6.2 us
    unnamed x22, local copies, waits for them, and re-layouts  3.74 us
    pallas_call x1, Pallas kernels, dealt_device(): pl.pallas_call(finish_body, out_shape=(shape((width // n_ctx, head_cols),...  2.63 us
    pallas_call x1, Pallas kernels, dealt_device(): pl.pallas_call(functools.partial(attend_own_body, scales[0]), out_shape=(...  2.51 us
    ppermute x1, starting transfers between devices, dealt_device(): far_in = lax.ppermute(far_own, ('ctx', 'head'), FAR_OUT)  2.47 us
  transfers between devices with their start and end apart: 20, of which 11 were waited for; matrix products, arithmetic and copies ran while one was open for 0% of the time, Pallas kernels for 5%

profile of v7, /device:TPU:0, one launch (start us, length us, event | category | flops | bytes accessed | tf_op | source)
XLA Modules:
  0.0 83.7 jit_solution(800435010025902613)
XLA Ops:
  1.3 0.0 copy-start.5
  1.3 0.9 %copy-done.5 = bf16[2,128,512]{2,1,0:T(8,128)(2,1)S(1)} copy-done((bf16[2,128,512]{2,1,0:T(8,128)(2,1)S(1)}, bf16[2,128,512]{2,1,0:T(8,128)(2,1)}, u32[]{:S(2)}) %copy-start.5) | copy-done | bytes 262168
  2.2 0.9 %copy-done.6 = bf16[128,1024]{1,0:T(8,128)(2,1)S(1)} copy-done((bf16[128,1024]{1,0:T(8,128)(2,1)S(1)}, bf16[128,1024]{1,0:T(8,128)(2,1)}, u32[]{:S(2)}) %copy-start.6) | copy-done | bytes 262168
  3.2 0.9 %copy-done.7 = bf16[128,512]{1,0:T(8,128)(2,1)S(1)} copy-done((bf16[128,512]{1,0:T(8,128)(2,1)S(1)}, bf16[128,512]{1,0:T(8,128)(2,1)}, u32[]{:S(2)}) %copy-start.7) | copy-done | bytes 131096
  4.1 0.9 %copy-done.8 = bf16[128,512]{1,0:T(8,128)(2,1)S(1)} copy-done((bf16[128,512]{1,0:T(8,128)(2,1)S(1)}, bf16[128,512]{1,0:T(8,128)(2,1)}, u32[]{:S(2)}) %copy-start.8) | copy-done | bytes 131096
  5.0 0.3 deal.1
  5.3 4.1 %collective-permute-start = (bf16[144,512]{1,0:T(8,128)(2,1)S(1)}, bf16[144,512]{1,0:T(8,128)(2,1)S(1)}, u32[]{:S(2)}, u32[]{:S(2)}) collective-permute-start(bf16[144,512]{1,0:T(8,128)(2,1)S(1)} %get-tuple-element.59.rows_1), channel_id=1, source_target_pairs={{0,16},{2,18},{4,20},{6,22},{8,24},{10,26},{12,28},{14,30},{16,0},... | collective-permute-start | bytes 442376 | tf_op jit(solution)/shard_map/ppermute | solution.py:577
  9.4 2.5 %collective-permute-start.1 = (bf16[560,128]{1,0:T(8,128)(2,1)S(1)}, bf16[560,128]{1,0:T(8,128)(2,1)S(1)}, u32[]{:S(2)}, u32[]{:S(2)}) collective-permute-start(bf16[560,128]{1,0:T(8,128)(2,1)S(1)} %get-tuple-element.60), channel_id=1, source_target_pairs={{0,10},{2,8},{4,14},{6,12},{8,2},{10,0},{12,6},{14,4},{16,26},{18,... | collective-permute-start | bytes 430088 | tf_op jit(solution)/shard_map/ppermute | solution.py:577
  11.9 0.4 collective-permute-start.2
  12.4 0.5 collective-permute-start.3
  12.9 6.1 %collective-permute-done.1.by_both = bf16[560,128]{1,0:T(8,128)(2,1)S(1)} collective-permute-done((bf16[560,128]{1,0:T(8,128)(2,1)S(1)}, bf16[560,128]{1,0:T(8,128)(2,1)S(1)}, u32[]{:S(2)}, u32[]{:S(2)}) %collective-permute-start.1) | collective-permute-done | bytes 143392 | tf_op jit(solution)/shard_map/ppermute | solution.py:577
  19.0 1.6 %collective-permute-done.2.by_zl = bf16[560,128]{1,0:T(8,128)(2,1)S(1)} collective-permute-done((bf16[560,128]{1,0:T(8,128)(2,1)S(1)}, bf16[560,128]{1,0:T(8,128)(2,1)S(1)}, u32[]{:S(2)}, u32[]{:S(2)}) %collective-permute-start.2) | collective-permute-done | bytes 143392 | tf_op jit(solution)/shard_map/ppermute | solution.py:577
  20.6 0.0 collective-permute-done.3.by_x
  20.6 0.0 collective-permute-done.rows_2
  20.6 0.1 gather.1
  20.7 1.6 %collective-permute-start.4 = (bf16[4,272,128]{2,1,0:T(8,128)(2,1)S(1)}, bf16[4,272,128]{2,1,0:T(8,128)(2,1)S(1)}, u32[]{:S(2)}, u32[]{:S(2)}) collective-permute-start(bf16[4,272,128]{2,1,0:T(8,128)(2,1)S(1)} %get-tuple-element.67.near_own), channel_id=1, source_target_pairs={{0,4},{2,6},{4,0},{6,2},{8,12},{10,14},{12,8},{14,10},{16,20},{18,... | collective-permute-start | bytes 835592 | tf_op jit(solution)/shard_map/ppermute | solution.py:589
  22.3 2.5 %collective-permute-start.5 = (bf16[4,288,128]{2,1,0:T(8,128)(2,1)S(1)}, bf16[4,288,128]{2,1,0:T(8,128)(2,1)S(1)}, u32[]{:S(2)}, u32[]{:S(2)}) collective-permute-start(bf16[4,288,128]{2,1,0:T(8,128)(2,1)S(1)} %get-tuple-element.68.far_own), channel_id=1, source_target_pairs={{0,16},{2,18},{4,20},{6,22},{8,24},{10,26},{12,28},{14,30},{17,1},... | collective-permute-start | bytes 884744 | tf_op jit(solution)/shard_map/ppermute | solution.py:588
  24.8 2.5 %collective-permute-start.6 = (bf16[256,512]{1,0:T(8,128)(2,1)S(1)}, bf16[256,512]{1,0:T(8,128)(2,1)S(1)}, u32[]{:S(2)}, u32[]{:S(2)}) collective-permute-start(bf16[256,512]{1,0:T(8,128)(2,1)S(1)} %get-tuple-element.77.refs_0_), channel_id=1, source_target_pairs={{0,8},{2,10},{4,12},{6,14},{8,0},{10,2},{12,4},{14,6},{16,24},{18,... | collective-permute-start | bytes 786440 | tf_op jit(solution)/shard_map/ppermute | solution.py:577
  27.4 0.5 collective-permute-start.7
  27.9 0.3 collective-permute-done.4.near_in
  28.2 2.5 %attend_own.1 = (f32[1024,128]{1,0:T(8,128)S(1)}, f32[1024,128]{1,0:T(8,128)S(1)}, f32[2,512,128]{2,1,0:T(8,128)S(1)}) custom-call(bf16[4,272,128]{2,1,0:T(8,128)(2,1)S(1)} %get-tuple-element.67.near_own, bf16[4,288,128]{2,1,0:T(8,128)(2,1)S(1)} %get-tuple-element.68.far_own, bf16[4,272,128]{2,1,0:T(8,128)(2,1)S(1)} %collective-permute-done.4.near_in), custom_call_target="tpu_custom_call" | custom-call | flops 1000000000 | bytes 1048576 | tf_op jit(solution)/shard_map/attend_own/pallas_call | solution.py:595
  30.8 1.6 %collective-permute-start.8 = (bf16[256,512]{1,0:T(8,128)(2,1)S(1)}, bf16[256,512]{1,0:T(8,128)(2,1)S(1)}, u32[]{:S(2)}, u32[]{:S(2)}) collective-permute-start(bf16[256,512]{1,0:T(8,128)(2,1)S(1)} %get-tuple-element.77.refs_0_), channel_id=1, source_target_pairs={{0,4},{2,6},{4,0},{6,2},{8,12},{10,14},{12,8},{14,10},{16,20},{18,... | collective-permute-start | bytes 786440 | tf_op jit(solution)/shard_map/ppermute | solution.py:577
  32.4 0.0 collective-permute-done.5.far_in
  32.4 0.0 copy-start
  32.5 1.5 %collective-permute-done.6.refs_1_ = bf16[256,512]{1,0:T(8,128)(2,1)S(1)} collective-permute-done((bf16[256,512]{1,0:T(8,128)(2,1)S(1)}, bf16[256,512]{1,0:T(8,128)(2,1)S(1)}, u32[]{:S(2)}, u32[]{:S(2)}) %collective-permute-start.6) | collective-permute-done | bytes 262176 | tf_op jit(solution)/shard_map/ppermute | solution.py:577
  33.9 0.0 collective-permute-done.7.refs_2_
  33.9 3.4 %collective-permute-done.8.refs_4_ = bf16[256,512]{1,0:T(8,128)(2,1)S(1)} collective-permute-done((bf16[256,512]{1,0:T(8,128)(2,1)S(1)}, bf16[256,512]{1,0:T(8,128)(2,1)S(1)}, u32[]{:S(2)}, u32[]{:S(2)}) %collective-permute-start.8) | collective-permute-done | bytes 262176 | tf_op jit(solution)/shard_map/ppermute | solution.py:577
  37.3 1.5 %collective-permute-start.9 = (bf16[4,272,128]{2,1,0:T(8,128)(2,1)S(1)}, bf16[4,272,128]{2,1,0:T(8,128)(2,1)S(1)}, u32[]{:S(2)}, u32[]{:S(2)}) collective-permute-start(bf16[4,272,128]{2,1,0:T(8,128)(2,1)S(1)} %get-tuple-element.78), channel_id=1, source_target_pairs={{16,0},{18,2},{20,4},{22,6},{24,8},{26,10},{28,12},{30,14},{1,17},... | collective-permute-start | bytes 835592 | tf_op jit(solution)/shard_map/ppermute | solution.py:626
  38.8 1.6 %collective-permute-start.10 = (bf16[4,2,128,128]{3,2,1,0:T(8,128)(2,1)S(1)}, bf16[4,2,128,128]{3,2,1,0:T(8,128)(2,1)S(1)}, u32[]{:S(2)}, u32[]{:S(2)}) collective-permute-start(bf16[4,2,128,128]{3,2,1,0:T(8,128)(2,1)S(1)} %near.1), channel_id=1, source_target_pairs={{0,4},{2,6},{4,0},{6,2},{8,12},{10,14},{12,8},{14,10},{16,20},{18,... | collective-permute-start | bytes 786440 | tf_op jit(solution)/shard_map/ppermute | solution.py:627
  40.5 0.1 collective-permute-start.11
  40.6 1.3 %collective-permute-start.15 = (bf16[256,512]{1,0:T(8,128)(2,1)S(1)}, bf16[256,512]{1,0:T(8,128)(2,1)S(1)}, u32[]{:S(2)}, u32[]{:S(2)}) collective-permute-start(bf16[256,512]{1,0:T(8,128)(2,1)S(1)} %collective-permute-done.6.refs_1_), channel_id=1, source_target_pairs={{0,4},{2,6},{4,0},{6,2},{8,12},{10,14},{12,8},{14,10},{16,20},{18,... | collective-permute-start | bytes 786440 | tf_op jit(solution)/shard_map/ppermute | solution.py:577
  42.0 6.2 %collective-permute-done.10.near = bf16[4,2,128,128]{3,2,1,0:T(8,128)(2,1)S(1)} collective-permute-done((bf16[4,2,128,128]{3,2,1,0:T(8,128)(2,1)S(1)}, bf16[4,2,128,128]{3,2,1,0:T(8,128)(2,1)S(1)}, u32[]{:S(2)}, u32[]{:S(2)}) %collective-permute-start.10) | collective-permute-done | bytes 262176 | tf_op jit(solution)/shard_map/ppermute | solution.py:627
  48.2 1.5 %collective-permute-done.9.far = bf16[4,272,128]{2,1,0:T(8,128)(2,1)S(1)} collective-permute-done((bf16[4,272,128]{2,1,0:T(8,128)(2,1)S(1)}, bf16[4,272,128]{2,1,0:T(8,128)(2,1)S(1)}, u32[]{:S(2)}, u32[]{:S(2)}) %collective-permute-start.9) | collective-permute-done | bytes 278560 | tf_op jit(solution)/shard_map/ppermute | solution.py:626
  49.7 0.0 copy-start.9
  49.7 0.0 copy-start.10
  49.7 0.0 copy-start.1
  49.7 0.1 merge.1
  49.8 0.0 collective-permute-done.11.refs_3_
  49.8 1.7 %collective-permute-start.16 = (bf16[256,512]{1,0:T(8,128)(2,1)S(1)}, bf16[256,512]{1,0:T(8,128)(2,1)S(1)}, u32[]{:S(2)}, u32[]{:S(2)}) collective-permute-start(bf16[256,512]{1,0:T(8,128)(2,1)S(1)} %collective-permute-done.11.refs_3_), channel_id=1, source_target_pairs={{0,4},{2,6},{4,0},{6,2},{8,12},{10,14},{12,8},{14,10},{16,20},{18,... | collective-permute-start | bytes 786440 | tf_op jit(solution)/shard_map/ppermute | solution.py:577
  51.5 0.0 collective-permute-start.12
  51.5 1.6 %collective-permute-start.13 = (bf16[3,128,128]{2,1,0:T(8,128)(2,1)S(1)}, bf16[3,128,128]{2,1,0:T(8,128)(2,1)S(1)}, u32[]{:S(2)}, u32[]{:S(2)}) collective-permute-start(bf16[3,128,128]{2,1,0:T(8,128)(2,1)S(1)} %get-tuple-element.92), channel_id=1, source_target_pairs={{0,8},{2,10},{4,12},{6,14},{8,0},{10,2},{12,4},{14,6},{16,24},{18,... | collective-permute-start | bytes 294920 | tf_op jit(solution)/shard_map/ppermute | solution.py:577
  53.1 1.9 %collective-permute-start.14 = (bf16[3,128,128]{2,1,0:T(8,128)(2,1)S(1)}, bf16[3,128,128]{2,1,0:T(8,128)(2,1)S(1)}, u32[]{:S(2)}, u32[]{:S(2)}) collective-permute-start(bf16[3,128,128]{2,1,0:T(8,128)(2,1)S(1)} %get-tuple-element.93), channel_id=1, source_target_pairs={{0,2},{2,0},{4,6},{6,4},{8,10},{10,8},{12,14},{14,12},{16,18},{18,... | collective-permute-start | bytes 294920 | tf_op jit(solution)/shard_map/ppermute | solution.py:577
  55.0 0.0 collective-permute-done.15.refs_5_
  55.0 0.2 collective-permute-start.18
  55.2 1.9 %collective-permute-done.12.by_both = bf16[3,128,128]{2,1,0:T(8,128)(2,1)S(1)} collective-permute-done((bf16[3,128,128]{2,1,0:T(8,128)(2,1)S(1)}, bf16[3,128,128]{2,1,0:T(8,128)(2,1)S(1)}, u32[]{:S(2)}, u32[]{:S(2)}) %collective-permute-start.12) | collective-permute-done | bytes 98336 | tf_op jit(solution)/shard_map/ppermute | solution.py:577
  57.1 0.0 collective-permute-done.13.by_zl
  57.1 1.0 %collective-permute-done.14.by_x = bf16[3,128,128]{2,1,0:T(8,128)(2,1)S(1)} collective-permute-done((bf16[3,128,128]{2,1,0:T(8,128)(2,1)S(1)}, bf16[3,128,128]{2,1,0:T(8,128)(2,1)S(1)}, u32[]{:S(2)}, u32[]{:S(2)}) %collective-permute-start.14) | collective-permute-done | bytes 98336 | tf_op jit(solution)/shard_map/ppermute | solution.py:577
  58.1 0.0 collective-permute-done.16.refs_7_
  58.1 0.0 copy-done
  58.1 0.0 copy-start.3
  58.1 0.0 copy-start.4
  58.1 1.2 %project.1 = (f32[128,1024]{1,0:T(8,128)S(1)}, bf16[128,1024]{1,0:T(8,128)(2,1)S(1)}) custom-call(bf16[3,128,128]{2,1,0:T(8,128)(2,1)S(1)} %collective-permute-done.12.by_both, bf16[3,128,128]{2,1,0:T(8,128)(2,1)S(1)} %collective-permute-done.13.by_zl, bf16[3,128,128]{2,1,0:T(8,128)(2,1)S(1)} %collective-permute-done.14.by_x, ...), custom_call_target="tpu_custom_call" | custom-call | tf_op jit(solution)/shard_map/project/pallas_call | solution.py:637
  59.3 0.1 collective-permute-start.17
  59.4 0.0 copy-done.9
  59.4 0.0 copy-done.10
  59.4 0.2 place.1
  59.6 1.8 %collective-permute-done.18.refs_6_ = bf16[256,512]{1,0:T(8,128)(2,1)S(1)} collective-permute-done((bf16[256,512]{1,0:T(8,128)(2,1)S(1)}, bf16[256,512]{1,0:T(8,128)(2,1)S(1)}, u32[]{:S(2)}, u32[]{:S(2)}) %collective-permute-start.18) | collective-permute-done | bytes 262176 | tf_op jit(solution)/shard_map/ppermute | solution.py:577
  61.4 0.0 collective-permute-done.17.other
  61.4 0.0 copy-done.1
  61.4 0.5 pack.1
  61.9 17.6 %all_to_all.5.got = bf16[16,112,128]{2,1,0:T(8,128)(2,1)S(1)} all-to-all(bf16[16,112,128]{2,1,0:T(8,128)(2,1)S(1)} %pack.1), channel_id=1, replica_groups=mesh['ctx'=16,'head'=2] {'ctx'}, dimensions={0} | all-to-all | bytes 917504 | tf_op jit(solution)/shard_map/all_to_all | solution.py:666
  79.5 0.1 collective-permute-start.19
  79.6 1.3 %collective-permute-done.19.other = bf16[16,32,128]{2,1,0:T(8,128)(2,1)S(1)} collective-permute-done((bf16[16,32,128]{2,1,0:T(8,128)(2,1)S(1)}, bf16[16,32,128]{2,1,0:T(8,128)(2,1)S(1)}, u32[]{:S(2)}, u32[]{:S(2)}) %collective-permute-start.19) | collective-permute-done | bytes 131104 | tf_op jit(solution)/shard_map/ppermute | solution.py:667
  80.9 2.6 %finish.1 = (f32[64,512]{1,0:T(8,128)}, f32[256,512]{1,0:T(8,128)}, f32[256,512]{1,0:T(8,128)}, f32[256,512]{1,0:T(8,128)}) custom-call(bf16[16,112,128]{2,1,0:T(8,128)(2,1)S(1)} %all_to_all.5.got, bf16[16,32,128]{2,1,0:T(8,128)(2,1)S(1)} %collective-permute-done.19.other, bf16[256,512]{1,0:T(8,128)(2,1)S(1)} %get-tuple-element.77.refs_0_, ...), custom_call_target="tpu_custom_call" | custom-call | tf_op jit(solution)/shard_map/finish/pallas_call | solution.py:670
  (11 shorter events, 0.1 us)
Async XLA Ops:
  1.3 1.0 %copy-start.5 = (bf16[2,128,512]{2,1,0:T(8,128)(2,1)S(1)}, bf16[2,128,512]{2,1,0:T(8,128)(2,1)}, u32[]{:S(2)}) copy-start(bf16[2,128,512]{2,1,0:T(8,128)(2,1)} %keys_values.1) | copy-start | bytes 786436
  2.2 0.9 %copy-start.6 = (bf16[128,1024]{1,0:T(8,128)(2,1)S(1)}, bf16[128,1024]{1,0:T(8,128)(2,1)}, u32[]{:S(2)}) copy-start(bf16[128,1024]{1,0:T(8,128)(2,1)} %rows.1) | copy-start | bytes 786436
  3.2 0.9 %copy-start.7 = (bf16[128,512]{1,0:T(8,128)(2,1)S(1)}, bf16[128,512]{1,0:T(8,128)(2,1)}, u32[]{:S(2)}) copy-start(bf16[128,512]{1,0:T(8,128)(2,1)} %queries.1) | copy-start | bytes 393220
  4.1 0.9 %copy-start.8 = (bf16[128,512]{1,0:T(8,128)(2,1)S(1)}, bf16[128,512]{1,0:T(8,128)(2,1)}, u32[]{:S(2)}) copy-start(bf16[128,512]{1,0:T(8,128)(2,1)} %cot.1) | copy-start | bytes 393220
  5.3 15.3 %collective-permute-start = (bf16[144,512]{1,0:T(8,128)(2,1)S(1)}, bf16[144,512]{1,0:T(8,128)(2,1)S(1)}, u32[]{:S(2)}, u32[]{:S(2)}) collective-permute-start(bf16[144,512]{1,0:T(8,128)(2,1)S(1)} %get-tuple-element.59.rows_1), channel_id=1, source_target_pairs={{0,16},{2,18},{4,20},{6,22},{8,24},{10,26},{12,28},{14,30},{16,0},... | collective-permute-start | bytes 442376 | tf_op jit(solution)/shard_map/ppermute | solution.py:577
  9.4 9.6 %collective-permute-start.1 = (bf16[560,128]{1,0:T(8,128)(2,1)S(1)}, bf16[560,128]{1,0:T(8,128)(2,1)S(1)}, u32[]{:S(2)}, u32[]{:S(2)}) collective-permute-start(bf16[560,128]{1,0:T(8,128)(2,1)S(1)} %get-tuple-element.60), channel_id=1, source_target_pairs={{0,10},{2,8},{4,14},{6,12},{8,2},{10,0},{12,6},{14,4},{16,26},{18,... | collective-permute-start | bytes 430088 | tf_op jit(solution)/shard_map/ppermute | solution.py:577
  11.9 8.7 %collective-permute-start.2 = (bf16[560,128]{1,0:T(8,128)(2,1)S(1)}, bf16[560,128]{1,0:T(8,128)(2,1)S(1)}, u32[]{:S(2)}, u32[]{:S(2)}) collective-permute-start(bf16[560,128]{1,0:T(8,128)(2,1)S(1)} %get-tuple-element.61), channel_id=1, source_target_pairs={{0,8},{2,10},{4,12},{6,14},{8,0},{10,2},{12,4},{14,6},{16,24},{18,... | collective-permute-start | bytes 430088 | tf_op jit(solution)/shard_map/ppermute | solution.py:577
  12.4 8.3 %collective-permute-start.3 = (bf16[560,128]{1,0:T(8,128)(2,1)S(1)}, bf16[560,128]{1,0:T(8,128)(2,1)S(1)}, u32[]{:S(2)}, u32[]{:S(2)}) collective-permute-start(bf16[560,128]{1,0:T(8,128)(2,1)S(1)} %get-tuple-element.62), channel_id=1, source_target_pairs={{0,2},{2,0},{4,6},{6,4},{8,10},{10,8},{12,14},{14,12},{16,18},{18,... | collective-permute-start | bytes 430088 | tf_op jit(solution)/shard_map/ppermute | solution.py:577
  20.7 7.5 %collective-permute-start.4 = (bf16[4,272,128]{2,1,0:T(8,128)(2,1)S(1)}, bf16[4,272,128]{2,1,0:T(8,128)(2,1)S(1)}, u32[]{:S(2)}, u32[]{:S(2)}) collective-permute-start(bf16[4,272,128]{2,1,0:T(8,128)(2,1)S(1)} %get-tuple-element.67.near_own), channel_id=1, source_target_pairs={{0,4},{2,6},{4,0},{6,2},{8,12},{10,14},{12,8},{14,10},{16,20},{18,... | collective-permute-start | bytes 835592 | tf_op jit(solution)/shard_map/ppermute | solution.py:589
  22.3 10.1 %collective-permute-start.5 = (bf16[4,288,128]{2,1,0:T(8,128)(2,1)S(1)}, bf16[4,288,128]{2,1,0:T(8,128)(2,1)S(1)}, u32[]{:S(2)}, u32[]{:S(2)}) collective-permute-start(bf16[4,288,128]{2,1,0:T(8,128)(2,1)S(1)} %get-tuple-element.68.far_own), channel_id=1, source_target_pairs={{0,16},{2,18},{4,20},{6,22},{8,24},{10,26},{12,28},{14,30},{17,1},... | collective-permute-start | bytes 884744 | tf_op jit(solution)/shard_map/ppermute | solution.py:588
  24.8 9.1 %collective-permute-start.6 = (bf16[256,512]{1,0:T(8,128)(2,1)S(1)}, bf16[256,512]{1,0:T(8,128)(2,1)S(1)}, u32[]{:S(2)}, u32[]{:S(2)}) collective-permute-start(bf16[256,512]{1,0:T(8,128)(2,1)S(1)} %get-tuple-element.77.refs_0_), channel_id=1, source_target_pairs={{0,8},{2,10},{4,12},{6,14},{8,0},{10,2},{12,4},{14,6},{16,24},{18,... | collective-permute-start | bytes 786440 | tf_op jit(solution)/shard_map/ppermute | solution.py:577
  27.4 6.6 %collective-permute-start.7 = (bf16[256,512]{1,0:T(8,128)(2,1)S(1)}, bf16[256,512]{1,0:T(8,128)(2,1)S(1)}, u32[]{:S(2)}, u32[]{:S(2)}) collective-permute-start(bf16[256,512]{1,0:T(8,128)(2,1)S(1)} %get-tuple-element.77.refs_0_), channel_id=1, source_target_pairs={{0,2},{2,0},{4,6},{6,4},{8,10},{10,8},{12,14},{14,12},{16,18},{18,... | collective-permute-start | bytes 786440 | tf_op jit(solution)/shard_map/ppermute | solution.py:577
  30.8 6.6 %collective-permute-start.8 = (bf16[256,512]{1,0:T(8,128)(2,1)S(1)}, bf16[256,512]{1,0:T(8,128)(2,1)S(1)}, u32[]{:S(2)}, u32[]{:S(2)}) collective-permute-start(bf16[256,512]{1,0:T(8,128)(2,1)S(1)} %get-tuple-element.77.refs_0_), channel_id=1, source_target_pairs={{0,4},{2,6},{4,0},{6,2},{8,12},{10,14},{12,8},{14,10},{16,20},{18,... | collective-permute-start | bytes 786440 | tf_op jit(solution)/shard_map/ppermute | solution.py:577
  32.4 25.6 %copy-start = (bf16[3,1024,512]{2,1,0:T(8,128)(2,1)S(1)}, bf16[3,1024,512]{2,1,0:T(8,128)(2,1)}, u32[]{:S(2)}) copy-start(bf16[3,1024,512]{2,1,0:T(8,128)(2,1)} %weight.1) | copy-start | bytes 9437188
  37.3 12.3 %collective-permute-start.9 = (bf16[4,272,128]{2,1,0:T(8,128)(2,1)S(1)}, bf16[4,272,128]{2,1,0:T(8,128)(2,1)S(1)}, u32[]{:S(2)}, u32[]{:S(2)}) collective-permute-start(bf16[4,272,128]{2,1,0:T(8,128)(2,1)S(1)} %get-tuple-element.78), channel_id=1, source_target_pairs={{16,0},{18,2},{20,4},{22,6},{24,8},{26,10},{28,12},{30,14},{1,17},... | collective-permute-start | bytes 835592 | tf_op jit(solution)/shard_map/ppermute | solution.py:626
  38.8 9.3 %collective-permute-start.10 = (bf16[4,2,128,128]{3,2,1,0:T(8,128)(2,1)S(1)}, bf16[4,2,128,128]{3,2,1,0:T(8,128)(2,1)S(1)}, u32[]{:S(2)}, u32[]{:S(2)}) collective-permute-start(bf16[4,2,128,128]{3,2,1,0:T(8,128)(2,1)S(1)} %near.1), channel_id=1, source_target_pairs={{0,4},{2,6},{4,0},{6,2},{8,12},{10,14},{12,8},{14,10},{16,20},{18,... | collective-permute-start | bytes 786440 | tf_op jit(solution)/shard_map/ppermute | solution.py:627
  40.5 9.4 %collective-permute-start.11 = (bf16[256,512]{1,0:T(8,128)(2,1)S(1)}, bf16[256,512]{1,0:T(8,128)(2,1)S(1)}, u32[]{:S(2)}, u32[]{:S(2)}) collective-permute-start(bf16[256,512]{1,0:T(8,128)(2,1)S(1)} %collective-permute-done.6.refs_1_), channel_id=1, source_target_pairs={{0,2},{2,0},{4,6},{6,4},{8,10},{10,8},{12,14},{14,12},{16,18},{18,... | collective-permute-start | bytes 786440 | tf_op jit(solution)/shard_map/ppermute | solution.py:577
  40.6 14.4 %collective-permute-start.15 = (bf16[256,512]{1,0:T(8,128)(2,1)S(1)}, bf16[256,512]{1,0:T(8,128)(2,1)S(1)}, u32[]{:S(2)}, u32[]{:S(2)}) collective-permute-start(bf16[256,512]{1,0:T(8,128)(2,1)S(1)} %collective-permute-done.6.refs_1_), channel_id=1, source_target_pairs={{0,4},{2,6},{4,0},{6,2},{8,12},{10,14},{12,8},{14,10},{16,20},{18,... | collective-permute-start | bytes 786440 | tf_op jit(solution)/shard_map/ppermute | solution.py:577
  49.7 9.7 %copy-start.9 = (s32[128,1]{0,1:T(1,128)S(1)}, s32[128,1]{0,1:T(1,128)}, u32[]{:S(2)}) copy-start(s32[128,1]{0,1:T(1,128)} %param.19) | copy-start | bytes 1540
  49.7 9.7 %copy-start.10 = (s32[128]{0:T(128)S(1)}, s32[128]{0:T(128)}, u32[]{:S(2)}) copy-start(s32[128]{0:T(128)} %param.20) | copy-start | bytes 1540
  49.7 11.7 %copy-start.1 = (bf16[1024,512]{1,0:T(8,128)(2,1)S(1)}, bf16[1024,512]{1,0:T(8,128)(2,1)}, u32[]{:S(2)}) copy-start(bf16[1024,512]{1,0:T(8,128)(2,1)} %adapter.1) | copy-start | bytes 3145732
  49.8 8.2 %collective-permute-start.16 = (bf16[256,512]{1,0:T(8,128)(2,1)S(1)}, bf16[256,512]{1,0:T(8,128)(2,1)S(1)}, u32[]{:S(2)}, u32[]{:S(2)}) collective-permute-start(bf16[256,512]{1,0:T(8,128)(2,1)S(1)} %collective-permute-done.11.refs_3_), channel_id=1, source_target_pairs={{0,4},{2,6},{4,0},{6,2},{8,12},{10,14},{12,8},{14,10},{16,20},{18,... | collective-permute-start | bytes 786440 | tf_op jit(solution)/shard_map/ppermute | solution.py:577
  51.5 5.5 %collective-permute-start.12 = (bf16[3,128,128]{2,1,0:T(8,128)(2,1)S(1)}, bf16[3,128,128]{2,1,0:T(8,128)(2,1)S(1)}, u32[]{:S(2)}, u32[]{:S(2)}) collective-permute-start(bf16[3,128,128]{2,1,0:T(8,128)(2,1)S(1)} %merge_both.1), channel_id=1, source_target_pairs={{0,10},{2,8},{4,14},{6,12},{8,2},{10,0},{12,6},{14,4},{16,26},{18,... | collective-permute-start | bytes 294920 | tf_op jit(solution)/shard_map/ppermute | solution.py:577
  51.5 5.5 %collective-permute-start.13 = (bf16[3,128,128]{2,1,0:T(8,128)(2,1)S(1)}, bf16[3,128,128]{2,1,0:T(8,128)(2,1)S(1)}, u32[]{:S(2)}, u32[]{:S(2)}) collective-permute-start(bf16[3,128,128]{2,1,0:T(8,128)(2,1)S(1)} %get-tuple-element.92), channel_id=1, source_target_pairs={{0,8},{2,10},{4,12},{6,14},{8,0},{10,2},{12,4},{14,6},{16,24},{18,... | collective-permute-start | bytes 294920 | tf_op jit(solution)/shard_map/ppermute | solution.py:577
  53.1 5.0 %collective-permute-start.14 = (bf16[3,128,128]{2,1,0:T(8,128)(2,1)S(1)}, bf16[3,128,128]{2,1,0:T(8,128)(2,1)S(1)}, u32[]{:S(2)}, u32[]{:S(2)}) collective-permute-start(bf16[3,128,128]{2,1,0:T(8,128)(2,1)S(1)} %get-tuple-element.93), channel_id=1, source_target_pairs={{0,2},{2,0},{4,6},{6,4},{8,10},{10,8},{12,14},{14,12},{16,18},{18,... | collective-permute-start | bytes 294920 | tf_op jit(solution)/shard_map/ppermute | solution.py:577
  55.0 6.4 %collective-permute-start.18 = (bf16[256,512]{1,0:T(8,128)(2,1)S(1)}, bf16[256,512]{1,0:T(8,128)(2,1)S(1)}, u32[]{:S(2)}, u32[]{:S(2)}) collective-permute-start(bf16[256,512]{1,0:T(8,128)(2,1)S(1)} %collective-permute-done.8.refs_4_), channel_id=1, source_target_pairs={{0,2},{2,0},{4,6},{6,4},{8,10},{10,8},{12,14},{14,12},{16,18},{18,... | collective-permute-start | bytes 786440 | tf_op jit(solution)/shard_map/ppermute | solution.py:577
  58.1 22.8 %copy-start.2 = (f32[256,512]{1,0:T(8,128)S(1)}, f32[256,512]{1,0:T(8,128)}, u32[]{:S(2)}) copy-start(f32[256,512]{1,0:T(8,128)} %refs_8_.1) | copy-start | bytes 1572868
  58.1 22.8 %copy-start.3 = (f32[256,512]{1,0:T(8,128)S(1)}, f32[256,512]{1,0:T(8,128)}, u32[]{:S(2)}) copy-start(f32[256,512]{1,0:T(8,128)} %refs_9_.1) | copy-start | bytes 1572868
  58.1 22.8 %copy-start.4 = (f32[256,512]{1,0:T(8,128)S(1)}, f32[256,512]{1,0:T(8,128)}, u32[]{:S(2)}) copy-start(f32[256,512]{1,0:T(8,128)} %refs_10_.1) | copy-start | bytes 1572868
  59.3 2.1 %collective-permute-start.17 = (bf16[128,1024]{1,0:T(8,128)(2,1)S(1)}, bf16[128,1024]{1,0:T(8,128)(2,1)S(1)}, u32[]{:S(2)}, u32[]{:S(2)}) collective-permute-start(bf16[128,1024]{1,0:T(8,128)(2,1)S(1)} %get-tuple-element.101), channel_id=1, source_target_pairs={{0,1},{1,0},{2,3},{3,2},{4,5},{5,4},{6,7},{7,6},{8,9},{9,8},{10,11... | collective-permute-start | bytes 786440 | tf_op jit(solution)/shard_map/ppermute | solution.py:653
  79.5 1.4 %collective-permute-start.19 = (bf16[16,32,128]{2,1,0:T(8,128)(2,1)S(1)}, bf16[16,32,128]{2,1,0:T(8,128)(2,1)S(1)}, u32[]{:S(2)}, u32[]{:S(2)}) collective-permute-start(bf16[16,32,128]{2,1,0:T(8,128)(2,1)S(1)} %slice.4), channel_id=1, source_target_pairs={{0,1},{1,0},{2,3},{3,2},{4,5},{5,4},{6,7},{7,6},{8,9},{9,8},{10,11... | collective-permute-start | bytes 393224 | tf_op jit(solution)/shard_map/ppermute | solution.py:667
